TPU v7x, 256 devices: a whole 4x4x8 slice. The times are simulated.
256 devices in a mesh: tok: 8 (over x, core), vocab: 32 (over z, y).
Axes of the slice: x: 4, y: 4, z: 8, core: 2. Of those that a mesh axis runs over, the one named last changes fastest.
Arguments:
- policy_hidden: bfloat16 [512, 5120], P(('tok', 'vocab')), may hold values from -15 to 15
- reference_hidden: bfloat16 [512, 5120], P(('tok', 'vocab')), may hold values from -15 to 15
- head_weight: bfloat16 [5120, 131072], P(None, ('tok', 'vocab')), may hold values from -1.118034 to 1.118034
- pair_map: int32 [512], replicated, may hold values from 0 to 511, each once
- response_mask: int32 [512], P(('tok', 'vocab')), may hold values 0 or 1
Outputs:
- token_divergence: float32 [512], P(('tok', 'vocab'))
- hidden_grad: bfloat16 [512, 5120], P(('tok', 'vocab'))
Inputs may be any that keep to these rules, and one draw needn't show every extreme that they name: pair_map is a permutation of the 512 rows.
All inputs are finite; a program needn't handle non-finite values. No bound on the sum of `response_mask` on one device may be relied on, other than what follows from the above.
Results may differ from a plain program's by a relative error of at most 0.015.
Values may be sent and summed in bfloat16 or wider, within the bound.
No kernel may reach another device: no remote copies, remote signals or barrier semaphores. Data moves between devices by JAX's collectives and lax.ppermute only.
A program may use at most 128 MiB of HBM per device.

v0:
```python
import functools

import jax
import jax.numpy as jnp
from jax import lax
from jax.experimental import pallas as pl
from jax.experimental.pallas import tpu as pltpu
from jax.sharding import Mesh, PartitionSpec as P

X, CORES, Z, Y = 4, 2, 8, 4
AXES = ("x", "core", "z", "y")
F32, BF16 = jnp.float32, jnp.bfloat16


def flat(x, c, z, y):
    return ((x * CORES + c) * Z + z) * Y + y


def exchange(value, partner):
    pairs = [
        (flat(x, c, z, y), flat(*partner(x, c, z, y)))
        for x in range(X)
        for c in range(CORES)
        for z in range(Z)
        for y in range(Y)
    ]
    return lax.ppermute(value, AXES, pairs)


def along_x(first, second):
    return lambda x, c, z, y: (x ^ (second if c else first), c, z, y)


def along_y(first, second):
    return lambda x, c, z, y: (x, c, z, y ^ (second if c else first))


def along_z(step):
    return lambda x, c, z, y: (x, c, z ^ step, y)


def across_cores(x, c, z, y):
    return (x, 1 - c, z, y)


Z_STEPS = (1, 2, 6)


def gray(j):
    return j ^ (j >> 1)


def z_slot(j):
    return j ^ ((j >> 2) << 1)


def gather_z(rows):
    for step in Z_STEPS:
        rows = jnp.concatenate([rows, exchange(rows, along_z(step))], 0)
    return rows


def ring_near(rows, along):
    return exchange(rows, along(1, 3))


def ring_far(rows, near, along):
    return exchange(jnp.concatenate([rows, near], 0), along(3, 1))


def scatter_step(total, partner):
    half = total.shape[0] // 2
    return total[:half] + exchange(total[half:].astype(BF16), partner).astype(F32)


CONTRACT_LAST = (((1,), (1,)), ((), ()))
VMEM_LIMIT = 40 * 1024 * 1024


def whole(array):
    zeros = (0,) * array.ndim
    return pl.BlockSpec(array.shape, lambda *_: zeros)


def run(kernel, name, flags, operands, outputs, grid=(1,), scratch=(), in_specs=None, out_specs=None, flops=0):
    bytes_accessed = sum(v.size * v.dtype.itemsize for v in (*operands, *outputs))
    return pl.pallas_call(
        kernel,
        out_shape=outputs,
        grid_spec=pltpu.PrefetchScalarGridSpec(
            num_scalar_prefetch=1,
            grid=grid,
            in_specs=in_specs or [whole(v) for v in operands],
            out_specs=out_specs or [whole(v) for v in outputs],
            scratch_shapes=list(scratch),
        ),
        compiler_params=pltpu.CompilerParams(vmem_limit_bytes=VMEM_LIMIT),
        cost_estimate=pl.CostEstimate(flops=flops, bytes_accessed=bytes_accessed, transcendentals=0),
        name=name,
    )(flags, *operands)


def ring_places(core):
    return (0, 1 + core, 2 - core, 3)


def rows_at(block, count):
    return pl.ds(pl.multiple_of(block * count, count), count)


def order_kernel(line, flags, low, low_near, low_far, high, high_near, high_far, ra, rb, pa, pb):
    places = ring_places(flags[0])
    for rows, near, far, base, policy in ((low, low_near, low_far, ra, pa), (high, high_near, high_far, rb, pb)):
        count = 2 * line
        pieces = ((rows, 0), (near, 0), (far, 0), (far, count))
        for (piece, start), place in zip(pieces, places):
            policy[rows_at(place, line), :] = piece[start : start + line, :]
            base[rows_at(place, line), :] = piece[start + line : start + count, :]


def two_products(x, part, head_keep, head_got):
    def product(head):
        return jnp.dot(x[0], head[:part, :], preferred_element_type=F32) + jnp.dot(
            x[1], head[part:, :], preferred_element_type=F32
        )

    return product(head_keep), product(head_got)


def store_halves(own, other, keep, send):
    columns = own.shape[1]
    step = pl.program_id(0)

    @pl.when(step == 0)
    def _():
        keep[:, :columns] = own
        keep[:, columns:] = other

    @pl.when(step == 1)
    def _():
        send[:, :columns] = other
        send[:, columns:] = own


def base_kernel(
    flags, low_place, high_place, a, a_near, a_far, b, b_near, b_far, head_keep, head_got, keep, send
):
    def pick(place, rows, near, far):
        count, ring = place.shape[0], rows.shape[0]
        lanes = lax.broadcasted_iota(jnp.int32, (count, 4 * ring), 1)
        one_hot = jnp.where(place[...] == lanes, 1.0, 0.0).astype(BF16)
        total = jnp.dot(one_hot[:, :ring], rows[...], preferred_element_type=F32)
        total += jnp.dot(one_hot[:, ring : 2 * ring], near[...], preferred_element_type=F32)
        total += jnp.dot(one_hot[:, 2 * ring :], far[...], preferred_element_type=F32)
        return total.astype(BF16)

    x = (pick(low_place, a, a_near, a_far), pick(high_place, b, b_near, b_far))
    own, other = two_products(x, a.shape[1], head_keep, head_got)
    store_halves(own, other, keep, send)


def policy_kernel(line, flags, a, a_near, a_far, b, b_near, b_far, head_keep, head_got, keep, send, rows):
    step = pl.program_id(0)
    ring, part = a.shape
    mine = keep.shape[0]

    @pl.when(step == 0)
    def _():
        places = ring_places(flags[0])
        flip = 2 * flags[1]
        low = (a[...], a_near[...], a_far[:ring, :], a_far[ring:, :])
        for piece, place in zip(low, places):
            rows[rows_at(place ^ flip, ring), :part] = piece
        high = ((b, 0), (b_near, 0), (b_far, 0), (b_far, ring))
        for (piece, start), place in zip(high, places):
            for y in range(Y):
                rows[rows_at((y ^ flip) * X + place, line), part:] = piece[start + y * line : start + (y + 1) * line, :]

    x = rows[rows_at(step, mine), :]
    own, other = two_products((x[:, :part], x[:, part:]), part, head_keep, head_got)
    store_halves(own, other, keep, send)


def local_kernel(flags, common, policy_keep, policy_got, base_keep, base_got, message, parts, parts_sent):
    step = pl.program_id(0)
    policy = policy_keep[...] + policy_got[...]
    base = base_keep[...] + base_got[...]
    difference = policy - base
    columns = policy.shape[1] // 2
    policy_peak = jnp.max(policy, axis=1, keepdims=True)
    base_peak = jnp.max(base, axis=1, keepdims=True)
    policy_exp = jnp.exp(policy - policy_peak)
    policy_total = jnp.sum(policy_exp, axis=1, keepdims=True)
    base_total = jnp.sum(jnp.exp(base - base_peak), axis=1, keepdims=True)
    center = jnp.sum(policy_exp * difference, axis=1, keepdims=True) / policy_total
    first = (policy_exp * (difference - center)).astype(BF16)
    second = policy_exp.astype(BF16)
    for i, v in enumerate((first, second)):
        parts[i] = v
        parts_sent[i, :, :columns] = v[:, columns:]
        parts_sent[i, :, columns:] = v[:, :columns]
    mine = message.shape[1]
    lanes = lax.broadcasted_iota(jnp.int32, (policy.shape[0], mine), 1) + flags[0] * mine
    match = common[...] == lanes
    values = (
        policy_peak + jnp.log(policy_total),
        base_peak + jnp.log(base_total),
        center,
        policy_peak,
    )
    lines = [jnp.sum(jnp.where(match, v, 0.0), axis=0, keepdims=True) for v in values]
    block = jnp.concatenate(lines + [jnp.zeros((4, mine), F32)], axis=0)

    @pl.when(step == 0)
    def _():
        message[...] = block

    @pl.when(step > 0)
    def _():
        message[...] += block


def merged(messages):
    policy, base, mean = messages[:, 0], messages[:, 1], messages[:, 2]
    policy_peak = jnp.max(policy, axis=0, keepdims=True)
    base_peak = jnp.max(base, axis=0, keepdims=True)
    weights = jnp.exp(policy - policy_peak)
    total = jnp.sum(weights, axis=0, keepdims=True)
    base_total = jnp.sum(jnp.exp(base - base_peak), axis=0, keepdims=True)
    return (
        policy_peak + jnp.log(total),
        base_peak + jnp.log(base_total),
        jnp.sum(weights * mean, axis=0, keepdims=True) / total,
    )


def merge_kernel(flags, messages, out):
    lines = merged(messages[...])
    out[...] = jnp.concatenate([*lines, jnp.zeros((5, out.shape[1]), F32)], axis=0)


def result_kernel(flags, messages, local, out):
    policy, base, mean = merged(messages[...])
    scale = jnp.exp(local[3:4, :] - policy)
    out[...] = jnp.concatenate(
        [scale, local[2:3, :] - mean, mean - policy + base, jnp.zeros((5, out.shape[1]), F32)], axis=0
    )


def sent_kernel(
    line, flags, common, result, result_got, parts, parts_got, head_keep, head_got, low, high, low_rows, high_rows, by_y, by_x
):
    mine = result.shape[1]
    core, flip = flags[0], 2 * flags[1]

    def raw(place):
        return jnp.where((place == 1) | (place == 2), jnp.where(core == 1, 3 - place, place), place)

    for h, (values, source) in enumerate(((result, parts), (result_got, parts_got))):
        first = (core if h == 0 else 1 - core) * mine
        lanes = lax.broadcasted_iota(jnp.int32, (mine, mine), 1) + first
        match = common[h * mine : (h + 1) * mine, :] == lanes
        scale = jnp.sum(jnp.where(match, values[0:1, :], 0.0), axis=1, keepdims=True)
        shift = jnp.sum(jnp.where(match, values[1:2, :], 0.0), axis=1, keepdims=True)
        grad = (scale * (source[0].astype(F32) + shift * source[1].astype(F32))).astype(BF16)
        for block in range(2 * X):
            y, x = raw((2 * h + block // X) ^ flip), raw(block % X + 0 * core)
            piece = grad[block * line : (block + 1) * line]
            by_y[rows_at(y * X + x, line), :] = piece
            by_x[rows_at(x * Y + y, line), :] = piece
    low[...] = gradient(by_y[mine:, :], head_keep, head_got, 0).astype(BF16)
    high[...] = gradient(by_x[mine:, :], head_keep, head_got, 1).astype(BF16)
    low_rows[...] = by_y[:mine, :]
    high_rows[...] = by_x[:mine, :]


def gradient(rows, head_keep, head_got, which):
    columns = head_keep.shape[1]
    part = head_keep.shape[0] // 2
    span = slice(which * part, (which + 1) * part)
    return lax.dot_general(
        rows[:, :columns], head_keep[span, :], CONTRACT_LAST, preferred_element_type=F32
    ) + lax.dot_general(rows[:, columns:], head_got[span, :], CONTRACT_LAST, preferred_element_type=F32)


def kept_kernel(flags, low_rows, high_rows, head_keep, head_got, low, high):
    low[...] = gradient(low_rows[...], head_keep, head_got, 0)
    high[...] = gradient(high_rows[...], head_keep, head_got, 1)


def on_device(policy_hidden, reference_hidden, head_weight, pair_map, response_mask):
    x0, c0, z0, y0 = (lax.axis_index(name) for name in ("x", "core", "z", "y"))
    second = c0 == 1
    swapped = (c0 ^ (y0 >> 1)) == 1
    own_rows, width = policy_hidden.shape
    half = width // 2
    part = half // 2
    columns = head_weight.shape[1]
    chip_rows = CORES * own_rows
    line = Z * chip_rows
    ring = X * line
    tokens = Y * ring
    mine = tokens // 2

    own = jnp.concatenate([policy_hidden, reference_hidden], 0)
    keep = lax.dynamic_slice_in_dim(own, c0 * half, half, 1)
    got = exchange(lax.dynamic_slice_in_dim(own, (1 - c0) * half, half, 1), across_cores)
    first_rows = jnp.where(second, got, keep)
    second_rows = jnp.where(second, keep, got)
    rows = jnp.concatenate(
        [first_rows[:own_rows], second_rows[:own_rows], first_rows[own_rows:], second_rows[own_rows:]], 0
    )
    rows, head_weight = lax.optimization_barrier((rows, head_weight))
    head_got = exchange(lax.dynamic_slice_in_dim(head_weight, (1 - c0) * half, half, 0), across_cores)
    flags = jnp.stack([c0, c0 ^ (y0 >> 1)]).astype(jnp.int32)
    head = (head_weight, head_got)
    head_specs = [pl.BlockSpec((half, columns), lambda i, f: (f[0], 0)), whole(head_got)]

    rows = gather_z(rows)

    slot = jnp.arange(tokens, dtype=jnp.int32)

    def raw(j):
        return jnp.where(second, jnp.where(j == 0, 0, jnp.where(j == 3, 1, j + 1)), gray(j))

    sr, sc = slot % own_rows, (slot // own_rows) % CORES
    sz = z_slot((slot // chip_rows) % Z) ^ z0
    sx = gray((slot // line) % X) ^ x0
    sy = gray((slot // ring) ^ jnp.where(swapped, 2, 0)) ^ y0
    partner = jnp.take(pair_map, flat(sx, sc, sz, sy) * own_rows + sr, axis=0)
    pr, pdev = partner % own_rows, partner // own_rows
    py, pz, pc, px = pdev % Y, (pdev // Y) % Z, (pdev // (Y * Z)) % CORES, pdev // (Y * Z * CORES)
    tail = (z_slot(pz ^ z0) * CORES + pc) * own_rows + pr
    low_place = ((raw(py ^ y0) * X + gray(px ^ x0)) * line + tail)[:, None]
    high_place = ((raw(px ^ x0) * Y + gray(py ^ y0)) * line + tail)[:, None]
    common = (((sy * X + sx) * Z + sz) * chip_rows + sc * own_rows + sr)[:, None]

    rows = rows.reshape(Z, 2, chip_rows, half).swapaxes(0, 1).reshape(2 * line, half)
    low, high = rows[:, :part], rows[:, part:]
    low_near, high_near = ring_near(low, along_x), ring_near(high, along_y)
    low_far, high_far = ring_far(low, low_near, along_x), ring_far(high, high_near, along_y)
    block = jax.ShapeDtypeStruct((ring, part), BF16)
    ra, rb, pa, pb = run(
        functools.partial(order_kernel, line),
        "order",
        flags,
        (low, low_near, low_far, high, high_near, high_far),
        [block] * 4,
    )

    ra_near, rb_near = ring_near(ra, along_y), ring_near(rb, along_x)
    pa_near, pb_near = ring_near(pa, along_y), ring_near(pb, along_x)
    ra_far, rb_far = ring_far(ra, ra_near, along_y), ring_far(rb, rb_near, along_x)
    pa_far, pb_far = ring_far(pa, pa_near, along_y), ring_far(pb, pb_near, along_x)

    logits = [jax.ShapeDtypeStruct((mine, 2 * columns), F32)] * 2
    flops = 4 * tokens * half * columns
    base = (ra, ra_near, ra_far, rb, rb_near, rb_far)
    base_keep, base_send = run(
        base_kernel,
        "base_logits",
        flags,
        (low_place, high_place, *base, *head),
        logits,
        grid=(2,),
        in_specs=[pl.BlockSpec((mine, 1), lambda i, f: (i, 0))] * 2 + [whole(v) for v in base] + head_specs,
        flops=2 * flops,
    )
    base_got = exchange(base_send, across_cores)
    policy = (pa, pa_near, pa_far, pb, pb_near, pb_far)
    policy_keep, policy_send = run(
        functools.partial(policy_kernel, line),
        "policy_logits",
        flags,
        (*policy, *head),
        logits,
        grid=(2,),
        in_specs=[whole(v) for v in policy] + head_specs,
        scratch=[pltpu.VMEM((tokens, half), BF16)],
        flops=flops,
    )
    policy_got = exchange(policy_send, across_cores)

    steps = 4
    row_spec = pl.BlockSpec((mine // steps, 2 * columns), lambda i, f: (i, 0))
    part_spec = pl.BlockSpec((2, mine // steps, 2 * columns), lambda i, f: (0, i, 0))
    message_shape = jax.ShapeDtypeStruct((8, mine), F32)
    parts_shape = jax.ShapeDtypeStruct((2, mine, 2 * columns), BF16)
    message, parts, parts_sent = run(
        local_kernel,
        "local_sums",
        flags,
        (common[:mine], policy_keep, policy_got, base_keep, base_got),
        [message_shape, parts_shape, parts_shape],
        grid=(steps,),
        in_specs=[pl.BlockSpec((mine // steps, 1), lambda i, f: (i, 0))] + [row_spec] * 4,
        out_specs=[whole(message_shape), part_spec, part_spec],
    )
    parts_got = exchange(parts_sent, across_cores)

    gathered = message
    for step in Z_STEPS:
        gathered = jnp.concatenate([gathered, exchange(gathered, along_z(step))], 0)
    (line_message,) = run(merge_kernel, "merge", flags, (gathered.reshape(Z, 8, mine),), [message_shape])
    everyone = lax.all_to_all(jnp.broadcast_to(line_message[None], (X * Y, 8, mine)), ("x", "y"), 0, 0)
    (result,) = run(result_kernel, "result", flags, (everyone, message), [message_shape])
    result_got = exchange(result, across_cores)

    rows_shape = jax.ShapeDtypeStruct((mine, 2 * columns), BF16)
    sent_shape = jax.ShapeDtypeStruct((mine, part), BF16)
    kept_shape = jax.ShapeDtypeStruct((mine, part), F32)
    operands = (common, result, result_got, parts, parts_got)
    low_sent, high_sent, low_rows, high_rows = run(
        functools.partial(sent_kernel, line),
        "gradient_sent",
        flags,
        (*operands, *head),
        [sent_shape, sent_shape, rows_shape, rows_shape],
        in_specs=[whole(v) for v in operands] + head_specs,
        scratch=[pltpu.VMEM((tokens, 2 * columns), BF16)] * 2,
        flops=flops // 2,
    )
    low_got, high_got = exchange(low_sent, along_y(3, 1)), exchange(high_sent, along_x(3, 1))
    low_kept, high_kept = run(
        kept_kernel,
        "gradient_kept",
        flags,
        (low_rows, high_rows, *head),
        [kept_shape, kept_shape],
        in_specs=[whole(low_rows), whole(high_rows)] + head_specs,
        flops=flops // 2,
    )
    low_total = low_kept + low_got.astype(F32)
    high_total = high_kept + high_got.astype(F32)
    low_total = scatter_step(low_total, along_y(1, 3))
    high_total = scatter_step(high_total, along_x(1, 3))
    low_total = scatter_step(scatter_step(low_total, along_x(3, 1)), along_x(1, 3))
    high_total = scatter_step(scatter_step(high_total, along_y(3, 1)), along_y(1, 3))
    total = jnp.concatenate([low_total, high_total], 1)
    for step in Z_STEPS[::-1]:
        total = scatter_step(total, along_z(step))

    keep = lax.dynamic_slice_in_dim(total, c0 * own_rows, own_rows, 0)
    got = exchange(lax.dynamic_slice_in_dim(total, (1 - c0) * own_rows, own_rows, 0), across_cores)
    grad = jnp.concatenate([jnp.where(second, got, keep), jnp.where(second, keep, got)], 1)
    position = ((y0 * X + x0) * Z + z0) * chip_rows + c0 * own_rows
    divergence = jnp.where(second, jnp.stack([result_got[2], result[2]]), jnp.stack([result[2], result_got[2]]))
    own_divergence = lax.dynamic_slice_in_dim(divergence.reshape(-1), position, own_rows, 0)
    weight = response_mask.astype(F32)
    return (weight * own_divergence, (weight[:, None] * grad).astype(BF16))


def solution(mesh):
    chips = Mesh(mesh.devices.reshape(X, CORES, Z, Y), AXES)
    return jax.shard_map(
        on_device,
        mesh=chips,
        in_specs=(P(AXES, None), P(AXES, None), P(None, AXES), P(), P(AXES)),
        out_specs=(P(AXES), P(AXES, None)),
        check_vma=False,
    )
```

profile of v0, /device:TPU:1, one launch (start us, length us, event | category | flops | bytes accessed | tf_op | source)
XLA Modules:
  0.0 181.0 jit_solution(17561809232141109866)
XLA Ops:
  1.5 3.3 %collective-permute-start = (bf16[4,2560]{1,0:T(4,128)(2,1)S(1)}, bf16[4,2560]{1,0:T(4,128)(2,1)S(1)}, u32[]{:S(2)}, u32[]{:S(2)}) collective-permute-start(bf16[4,2560]{1,0:T(4,128)(2,1)S(1)} %fusion.40), channel_id=1, source_target_pairs={{0,32},{1,33},{2,34},{3,35},{4,36},{5,37},{6,38},{7,39},{8,40},{9,... | collective-permute-start | bytes 61448 | tf_op jit(solution)/shard_map/ppermute | solution.py:27
  6.7 2.8 %collective-permute-done.1 = bf16[8,2560]{1,0:T(8,128)(2,1)S(1)} collective-permute-done((bf16[8,2560]{1,0:T(8,128)(2,1)S(1)}, bf16[8,2560]{1,0:T(8,128)(2,1)S(1)}, u32[]{:S(2)}, u32[]{:S(2)}) %collective-permute-start.1) | collective-permute-done | bytes 40992 | tf_op jit(solution)/shard_map/ppermute | solution.py:27
  11.0 3.6 %collective-permute-done.2 = bf16[16,2560]{1,0:T(8,128)(2,1)S(1)} collective-permute-done((bf16[16,2560]{1,0:T(8,128)(2,1)S(1)}, bf16[16,2560]{1,0:T(8,128)(2,1)S(1)}, u32[]{:S(2)}, u32[]{:S(2)}) %collective-permute-start.2) | collective-permute-done | bytes 81952 | tf_op jit(solution)/shard_map/ppermute | solution.py:27
  14.7 3.6 %collective-permute-start.3 = (bf16[32,2560]{1,0:T(8,128)(2,1)S(1)}, bf16[32,2560]{1,0:T(8,128)(2,1)S(1)}, u32[]{:S(2)}, u32[]{:S(2)}) collective-permute-start(bf16[32,2560]{1,0:T(8,128)(2,1)S(1)} %pad_maximum_fusion.8), channel_id=1, source_target_pairs={{0,24},{1,25},{2,26},{3,27},{4,28},{5,29},{6,30},{7,31},{8,16},{9,... | collective-permute-start | bytes 491528 | tf_op jit(solution)/shard_map/ppermute | solution.py:27
  18.3 4.2 %collective-permute-done.3 = bf16[32,2560]{1,0:T(8,128)(2,1)S(1)} collective-permute-done((bf16[32,2560]{1,0:T(8,128)(2,1)S(1)}, bf16[32,2560]{1,0:T(8,128)(2,1)S(1)}, u32[]{:S(2)}, u32[]{:S(2)}) %collective-permute-start.3) | collective-permute-done | bytes 163872 | tf_op jit(solution)/shard_map/ppermute | solution.py:27
  22.8 2.8 %collective-permute-start.6 = (bf16[64,1280]{1,0:T(8,128)(2,1)S(1)}, bf16[64,1280]{1,0:T(8,128)(2,1)S(1)}, u32[]{:S(2)}, u32[]{:S(2)}) collective-permute-start(bf16[64,1280]{1,0:T(8,128)(2,1)S(1)} %get-tuple-element.42.high), channel_id=1, source_target_pairs={{0,1},{1,0},{2,3},{3,2},{4,5},{5,4},{6,7},{7,6},{8,9},{9,8},{10,11... | collective-permute-start | bytes 491528 | tf_op jit(solution)/shard_map/ppermute | solution.py:27
  25.6 3.4 %constant_dynamic-slice_fusion.1 = bf16[2560,512]{1,0:T(8,128)(2,1)} fusion(bf16[5120,512]{1,0:T(8,128)(2,1)} %head_keep.3, s32[]{:T(128)S(6)} %select_n.509), kind=kLoop, calls=%fused_computation.194 | loop fusion | bytes 5242884 | tf_op jit(solution)/shard_map/dynamic_slice | solution.py:314
  38.5 3.5 %gather_fusion = s32[512]{0:T(512)S(1)} fusion(s32[512]{0:T(512)S(1)} %copy-done, s32[1024]{0:T(1024)S(1)} %pad_clamp_fusion), kind=kCustom, calls=%fused_computation | custom fusion | bytes 6144 | tf_op jit(solution)/shard_map/jit(_take)/gather | solution.py:330
  55.6 3.8 %collective-permute-done.10.b_near = bf16[128,1280]{1,0:T(8,128)(2,1)S(1)} collective-permute-done((bf16[128,1280]{1,0:T(8,128)(2,1)S(1)}, bf16[128,1280]{1,0:T(8,128)(2,1)S(1)}, u32[]{:S(2)}, u32[]{:S(2)}) %collective-permute-start.10) | collective-permute-done | bytes 327712 | tf_op jit(solution)/shard_map/ppermute | solution.py:27
  61.0 5.0 %collective-permute-done.15.a_far = bf16[256,1280]{1,0:T(8,128)(2,1)S(1)} collective-permute-done((bf16[256,1280]{1,0:T(8,128)(2,1)S(1)}, bf16[256,1280]{1,0:T(8,128)(2,1)S(1)}, u32[]{:S(2)}, u32[]{:S(2)}) %collective-permute-start.15) | collective-permute-done | bytes 655392 | tf_op jit(solution)/shard_map/ppermute | solution.py:27
  68.5 6.9 %base_logits.1 = (f32[256,1024]{1,0:T(8,128)S(1)}, f32[256,1024]{1,0:T(8,128)}) custom-call(s32[2]{0:T(128)S(1)} %pad_add_fusion.flags, s32[512,1]{1,0:T(8,128)S(1)} %multiply_add_fusion.1.low_place, s32[512,1]{1,0:T(8,128)S(1)} %get-tuple-element.40.high_place, bf16[128,1280]{1,0:T(8,128)(2,1)S(1)} %get-tuple-element.27.a, ...), custom_call_target="tpu_custom_call" | custom-call | flops 5368709120 | bytes 12587008 | tf_op jit(solution)/shard_map/base_logits/pallas_call | solution.py:87
  76.5 3.7 %collective-permute-start.18 = (f32[256,1024]{1,0:T(8,128)}, f32[256,1024]{1,0:T(8,128)}, u32[]{:S(2)}, u32[]{:S(2)}) collective-permute-start(f32[256,1024]{1,0:T(8,128)} %get-tuple-element.30), channel_id=1, source_target_pairs={{0,32},{1,33},{2,34},{3,35},{4,36},{5,37},{6,38},{7,39},{8,40},{9,... | collective-permute-start | bytes 3145736 | tf_op jit(solution)/shard_map/ppermute | solution.py:27
  80.1 4.9 %policy_logits.1 = (f32[256,1024]{1,0:T(8,128)S(1)}, f32[256,1024]{1,0:T(8,128)}) custom-call(s32[2]{0:T(128)S(1)} %pad_add_fusion.flags, bf16[128,1280]{1,0:T(8,128)(2,1)S(1)} %get-tuple-element.22.a, bf16[128,1280]{1,0:T(8,128)(2,1)S(1)} %collective-permute-done.8.a_near, bf16[256,1280]{1,0:T(8,128)(2,1)S(1)} %collective-permute-done.9.a_far, ...), custom_call_target="tpu_custom_call" | custom-call | flops 2684354560 | bytes 12582912 | tf_op jit(solution)/shard_map/policy_logits/pallas_call | solution.py:87
  86.2 2.8 %collective-permute-done.13.policy_got = f32[256,1024]{1,0:T(8,128)} collective-permute-done((f32[256,1024]{1,0:T(8,128)}, f32[256,1024]{1,0:T(8,128)}, u32[]{:S(2)}, u32[]{:S(2)}) %collective-permute-start.13) | collective-permute-done | bytes 1048608 | tf_op jit(solution)/shard_map/ppermute | solution.py:27
  91.5 3.7 %local_sums.1 = (f32[8,256]{1,0:T(8,128)S(1)}, bf16[2,256,1024]{2,1,0:T(8,128)(2,1)S(1)}, bf16[2,256,1024]{2,1,0:T(8,128)(2,1)S(1)}) custom-call(s32[2]{0:T(128)S(1)} %pad_add_fusion.flags, s32[256,1]{1,0:T(8,128)S(1)} %copy.10.common, f32[256,1024]{1,0:T(8,128)S(1)} %copy-done.6, f32[256,1024]{1,0:T(8,128)} %collective-permute-done.13.policy_got, ...), custom_call_target="tpu_custom_call" | custom-call | bytes 6300672 | tf_op jit(solution)/shard_map/local_sums/pallas_call | solution.py:87
  101.9 3.8 %collective-permute-start.21 = (f32[32,256]{1,0:T(8,128)S(1)}, f32[32,256]{1,0:T(8,128)S(1)}, u32[]{:S(2)}, u32[]{:S(2)}) collective-permute-start(f32[32,256]{1,0:T(8,128)S(1)} %pad_maximum_fusion.11), channel_id=1, source_target_pairs={{0,24},{1,25},{2,26},{3,27},{4,28},{5,29},{6,30},{7,31},{8,16},{9,... | collective-permute-start | bytes 98312 | tf_op jit(solution)/shard_map/ppermute | solution.py:27
  107.7 11.1 %all_to_all.5.messages = f32[16,8,256]{2,1,0:T(8,128)S(1)} all-to-all(f32[16,8,256]{2,1,0:T(8,128)S(1)} %broadcast_in_dim.22), channel_id=1, replica_groups=mesh['x'=4,'core'=2,'z'=8,'y'=4] {'x','y'}, dimensions={0} | all-to-all | bytes 262144 | tf_op jit(solution)/shard_map/all_to_all | solution.py:405
  119.4 5.0 %collective-permute-start.22 = (f32[8,256]{1,0:T(8,128)S(1)}, f32[8,256]{1,0:T(8,128)S(1)}, u32[]{:S(2)}, u32[]{:S(2)}) collective-permute-start(f32[8,256]{1,0:T(8,128)S(1)} %result.1), channel_id=1, source_target_pairs={{0,32},{1,33},{2,34},{3,35},{4,36},{5,37},{6,38},{7,39},{8,40},{9,... | collective-permute-start | bytes 24584 | tf_op jit(solution)/shard_map/ppermute | solution.py:27
  127.8 2.7 %gradient_sent.1 = (bf16[256,1280]{1,0:T(8,128)(2,1)S(1)}, bf16[256,1280]{1,0:T(8,128)(2,1)S(1)}, bf16[256,1024]{1,0:T(8,128)(2,1)S(1)}, bf16[256,1024]{1,0:T(8,128)(2,1)S(1)}) custom-call(s32[2]{0:T(128)S(1)} %pad_add_fusion.flags, s32[512,1]{1,0:T(8,128)S(1)} %fusion.2.common, f32[8,256]{1,0:T(8,128)S(1)} %result.1, ...), custom_call_target="tpu_custom_call" | custom-call | flops 1342177280 | bytes 12339200 | tf_op jit(solution)/shard_map/gradient_sent/pallas_call | solution.py:87
  133.3 7.2 %collective-permute-done.28 = bf16[256,1280]{1,0:T(8,128)(2,1)S(1)} collective-permute-done((bf16[256,1280]{1,0:T(8,128)(2,1)S(1)}, bf16[256,1280]{1,0:T(8,128)(2,1)S(1)}, u32[]{:S(2)}, u32[]{:S(2)}) %collective-permute-start.28) | collective-permute-done | bytes 655392 | tf_op jit(solution)/shard_map/ppermute | solution.py:27
  142.7 5.2 %collective-permute-done.29 = bf16[128,1280]{1,0:T(8,128)(2,1)S(1)} collective-permute-done((bf16[128,1280]{1,0:T(8,128)(2,1)S(1)}, bf16[128,1280]{1,0:T(8,128)(2,1)S(1)}, u32[]{:S(2)}, u32[]{:S(2)}) %collective-permute-start.29) | collective-permute-done | bytes 327712 | tf_op jit(solution)/shard_map/ppermute | solution.py:27
  149.6 2.9 %collective-permute-done.30 = bf16[64,1280]{1,0:T(8,128)(2,1)S(1)} collective-permute-done((bf16[64,1280]{1,0:T(8,128)(2,1)S(1)}, bf16[64,1280]{1,0:T(8,128)(2,1)S(1)}, u32[]{:S(2)}, u32[]{:S(2)}) %collective-permute-start.30) | collective-permute-done | bytes 163872 | tf_op jit(solution)/shard_map/ppermute | solution.py:27
  158.6 3.9 %collective-permute-start.32 = (bf16[16,2560]{1,0:T(8,128)(2,1)S(1)}, bf16[16,2560]{1,0:T(8,128)(2,1)S(1)}, u32[]{:S(2)}, u32[]{:S(2)}) collective-permute-start(bf16[16,2560]{1,0:T(8,128)(2,1)S(1)} %fusion.36), channel_id=1, source_target_pairs={{0,24},{1,25},{2,26},{3,27},{4,28},{5,29},{6,30},{7,31},{8,16},{9,... | collective-permute-start | bytes 245768 | tf_op jit(solution)/shard_map/ppermute | solution.py:27
  171.9 7.5 %collective-permute-start.35 = (f32[2,2560]{1,0:T(2,128)S(1)}, f32[2,2560]{1,0:T(2,128)S(1)}, u32[]{:S(2)}, u32[]{:S(2)}) collective-permute-start(f32[2,2560]{1,0:T(2,128)S(1)} %constant_dynamic-slice_fusion), channel_id=1, source_target_pairs={{0,32},{1,33},{2,34},{3,35},{4,36},{5,37},{6,38},{7,39},{8,40},{9,... | collective-permute-start | bytes 61448 | tf_op jit(solution)/shard_map/ppermute | solution.py:27
  (140 shorter events, 72.4 us)
Async XLA Ops:
  14.7 7.8 %collective-permute-start.3 = (bf16[32,2560]{1,0:T(8,128)(2,1)S(1)}, bf16[32,2560]{1,0:T(8,128)(2,1)S(1)}, u32[]{:S(2)}, u32[]{:S(2)}) collective-permute-start(bf16[32,2560]{1,0:T(8,128)(2,1)S(1)} %pad_maximum_fusion.8), channel_id=1, source_target_pairs={{0,24},{1,25},{2,26},{3,27},{4,28},{5,29},{6,30},{7,31},{8,16},{9,... | collective-permute-start | bytes 491528 | tf_op jit(solution)/shard_map/ppermute | solution.py:27
  22.8 11.3 %collective-permute-start.6 = (bf16[64,1280]{1,0:T(8,128)(2,1)S(1)}, bf16[64,1280]{1,0:T(8,128)(2,1)S(1)}, u32[]{:S(2)}, u32[]{:S(2)}) collective-permute-start(bf16[64,1280]{1,0:T(8,128)(2,1)S(1)} %get-tuple-element.42.high), channel_id=1, source_target_pairs={{0,1},{1,0},{2,3},{3,2},{4,5},{5,4},{6,7},{7,6},{8,9},{9,8},{10,11... | collective-permute-start | bytes 491528 | tf_op jit(solution)/shard_map/ppermute | solution.py:27
  29.0 37.0 %collective-permute-start.12 = (bf16[2560,512]{1,0:T(8,128)(2,1)}, bf16[2560,512]{1,0:T(8,128)(2,1)S(1)}, u32[]{:S(2)}, u32[]{:S(2)}) collective-permute-start(bf16[2560,512]{1,0:T(8,128)(2,1)} %constant_dynamic-slice_fusion.1), channel_id=1, source_target_pairs={{0,32},{1,33},{2,34},{3,35},{4,36},{5,37},{6,38},{7,39},{8,40},{9,... | collective-permute-start | bytes 7864328 | tf_op jit(solution)/shard_map/ppermute | solution.py:27
  31.6 5.4 %collective-permute-start.4 = (bf16[64,1280]{1,0:T(8,128)(2,1)S(1)}, bf16[64,1280]{1,0:T(8,128)(2,1)S(1)}, u32[]{:S(2)}, u32[]{:S(2)}) collective-permute-start(bf16[64,1280]{1,0:T(8,128)(2,1)S(1)} %get-tuple-element.43.low), channel_id=1, source_target_pairs={{0,64},{1,65},{2,66},{3,67},{4,68},{5,69},{6,70},{7,71},{8,72},{9,... | collective-permute-start | bytes 491528 | tf_op jit(solution)/shard_map/ppermute | solution.py:27
  34.9 7.3 %collective-permute-start.7 = (bf16[128,1280]{1,0:T(8,128)(2,1)}, bf16[128,1280]{1,0:T(8,128)(2,1)}, u32[]{:S(2)}, u32[]{:S(2)}) collective-permute-start(bf16[128,1280]{1,0:T(8,128)(2,1)} %pad_maximum_fusion.6), channel_id=1, source_target_pairs={{0,3},{1,2},{2,1},{3,0},{4,7},{5,6},{6,5},{7,4},{8,11},{9,10},{10,... | collective-permute-start | bytes 983048 | tf_op jit(solution)/shard_map/ppermute | solution.py:27
  37.8 6.5 %collective-permute-start.5 = (bf16[128,1280]{1,0:T(8,128)(2,1)}, bf16[128,1280]{1,0:T(8,128)(2,1)}, u32[]{:S(2)}, u32[]{:S(2)}) collective-permute-start(bf16[128,1280]{1,0:T(8,128)(2,1)} %pad_maximum_fusion.5), channel_id=1, source_target_pairs={{0,192},{1,193},{2,194},{3,195},{4,196},{5,197},{6,198},{7,199},{8... | collective-permute-start | bytes 983048 | tf_op jit(solution)/shard_map/ppermute | solution.py:27
  46.3 7.2 %collective-permute-start.14 = (bf16[128,1280]{1,0:T(8,128)(2,1)S(1)}, bf16[128,1280]{1,0:T(8,128)(2,1)S(1)}, u32[]{:S(2)}, u32[]{:S(2)}) collective-permute-start(bf16[128,1280]{1,0:T(8,128)(2,1)S(1)} %get-tuple-element.27.a), channel_id=1, source_target_pairs={{0,1},{1,0},{2,3},{3,2},{4,5},{5,4},{6,7},{7,6},{8,9},{9,8},{10,11... | collective-permute-start | bytes 983048 | tf_op jit(solution)/shard_map/ppermute | solution.py:27
  48.3 7.1 %collective-permute-start.16 = (bf16[128,1280]{1,0:T(8,128)(2,1)S(1)}, bf16[128,1280]{1,0:T(8,128)(2,1)S(1)}, u32[]{:S(2)}, u32[]{:S(2)}) collective-permute-start(bf16[128,1280]{1,0:T(8,128)(2,1)S(1)} %get-tuple-element.28.b), channel_id=1, source_target_pairs={{0,64},{1,65},{2,66},{3,67},{4,68},{5,69},{6,70},{7,71},{8,72},{9,... | collective-permute-start | bytes 983048 | tf_op jit(solution)/shard_map/ppermute | solution.py:27
  52.1 7.2 %collective-permute-start.10 = (bf16[128,1280]{1,0:T(8,128)(2,1)S(1)}, bf16[128,1280]{1,0:T(8,128)(2,1)S(1)}, u32[]{:S(2)}, u32[]{:S(2)}) collective-permute-start(bf16[128,1280]{1,0:T(8,128)(2,1)S(1)} %get-tuple-element.23.b), channel_id=1, source_target_pairs={{0,64},{1,65},{2,66},{3,67},{4,68},{5,69},{6,70},{7,71},{8,72},{9,... | collective-permute-start | bytes 983048 | tf_op jit(solution)/shard_map/ppermute | solution.py:27
  52.4 7.3 %collective-permute-start.8 = (bf16[128,1280]{1,0:T(8,128)(2,1)S(1)}, bf16[128,1280]{1,0:T(8,128)(2,1)S(1)}, u32[]{:S(2)}, u32[]{:S(2)}) collective-permute-start(bf16[128,1280]{1,0:T(8,128)(2,1)S(1)} %get-tuple-element.22.a), channel_id=1, source_target_pairs={{0,1},{1,0},{2,3},{3,2},{4,5},{5,4},{6,7},{7,6},{8,9},{9,8},{10,11... | collective-permute-start | bytes 983048 | tf_op jit(solution)/shard_map/ppermute | solution.py:27
  53.5 12.4 %collective-permute-start.15 = (bf16[256,1280]{1,0:T(8,128)(2,1)S(1)}, bf16[256,1280]{1,0:T(8,128)(2,1)S(1)}, u32[]{:S(2)}, u32[]{:S(2)}) collective-permute-start(bf16[256,1280]{1,0:T(8,128)(2,1)S(1)} %pad_maximum_fusion.2), channel_id=1, source_target_pairs={{0,3},{1,2},{2,1},{3,0},{4,7},{5,6},{6,5},{7,4},{8,11},{9,10},{10,... | collective-permute-start | bytes 1966088 | tf_op jit(solution)/shard_map/ppermute | solution.py:27
  55.5 10.6 %collective-permute-start.17 = (bf16[256,1280]{1,0:T(8,128)(2,1)S(1)}, bf16[256,1280]{1,0:T(8,128)(2,1)S(1)}, u32[]{:S(2)}, u32[]{:S(2)}) collective-permute-start(bf16[256,1280]{1,0:T(8,128)(2,1)S(1)} %pad_maximum_fusion.3), channel_id=1, source_target_pairs={{0,192},{1,193},{2,194},{3,195},{4,196},{5,197},{6,198},{7,199},{8... | collective-permute-start | bytes 1966088 | tf_op jit(solution)/shard_map/ppermute | solution.py:27
  59.4 20.8 %collective-permute-start.11 = (bf16[256,1280]{1,0:T(8,128)(2,1)S(1)}, bf16[256,1280]{1,0:T(8,128)(2,1)S(1)}, u32[]{:S(2)}, u32[]{:S(2)}) collective-permute-start(bf16[256,1280]{1,0:T(8,128)(2,1)S(1)} %pad_maximum_fusion.1), channel_id=1, source_target_pairs={{0,192},{1,193},{2,194},{3,195},{4,196},{5,197},{6,198},{7,199},{8... | collective-permute-start | bytes 1966088 | tf_op jit(solution)/shard_map/ppermute | solution.py:27
  59.7 20.4 %collective-permute-start.9 = (bf16[256,1280]{1,0:T(8,128)(2,1)S(1)}, bf16[256,1280]{1,0:T(8,128)(2,1)S(1)}, u32[]{:S(2)}, u32[]{:S(2)}) collective-permute-start(bf16[256,1280]{1,0:T(8,128)(2,1)S(1)} %pad_maximum_fusion), channel_id=1, source_target_pairs={{0,3},{1,2},{2,1},{3,0},{4,7},{5,6},{6,5},{7,4},{8,11},{9,10},{10,... | collective-permute-start | bytes 1966088 | tf_op jit(solution)/shard_map/ppermute | solution.py:27
  76.5 9.8 %collective-permute-start.18 = (f32[256,1024]{1,0:T(8,128)}, f32[256,1024]{1,0:T(8,128)}, u32[]{:S(2)}, u32[]{:S(2)}) collective-permute-start(f32[256,1024]{1,0:T(8,128)} %get-tuple-element.30), channel_id=1, source_target_pairs={{0,32},{1,33},{2,34},{3,35},{4,36},{5,37},{6,38},{7,39},{8,40},{9,... | collective-permute-start | bytes 3145736 | tf_op jit(solution)/shard_map/ppermute | solution.py:27
  95.2 30.0 %collective-permute-start.23 = (bf16[2,256,1024]{2,1,0:T(8,128)(2,1)S(1)}, bf16[2,256,1024]{2,1,0:T(8,128)(2,1)S(1)}, u32[]{:S(2)}, u32[]{:S(2)}) collective-permute-start(bf16[2,256,1024]{2,1,0:T(8,128)(2,1)S(1)} %get-tuple-element.33), channel_id=1, source_target_pairs={{0,32},{1,33},{2,34},{3,35},{4,36},{5,37},{6,38},{7,39},{8,40},{9,... | collective-permute-start | bytes 3145736 | tf_op jit(solution)/shard_map/ppermute | solution.py:27
  101.9 5.2 %collective-permute-start.21 = (f32[32,256]{1,0:T(8,128)S(1)}, f32[32,256]{1,0:T(8,128)S(1)}, u32[]{:S(2)}, u32[]{:S(2)}) collective-permute-start(f32[32,256]{1,0:T(8,128)S(1)} %pad_maximum_fusion.11), channel_id=1, source_target_pairs={{0,24},{1,25},{2,26},{3,27},{4,28},{5,29},{6,30},{7,31},{8,16},{9,... | collective-permute-start | bytes 98312 | tf_op jit(solution)/shard_map/ppermute | solution.py:27
  119.4 5.9 %collective-permute-start.22 = (f32[8,256]{1,0:T(8,128)S(1)}, f32[8,256]{1,0:T(8,128)S(1)}, u32[]{:S(2)}, u32[]{:S(2)}) collective-permute-start(f32[8,256]{1,0:T(8,128)S(1)} %result.1), channel_id=1, source_target_pairs={{0,32},{1,33},{2,34},{3,35},{4,36},{5,37},{6,38},{7,39},{8,40},{9,... | collective-permute-start | bytes 24584 | tf_op jit(solution)/shard_map/ppermute | solution.py:27
  130.5 10.0 %collective-permute-start.28 = (bf16[256,1280]{1,0:T(8,128)(2,1)S(1)}, bf16[256,1280]{1,0:T(8,128)(2,1)S(1)}, u32[]{:S(2)}, u32[]{:S(2)}) collective-permute-start(bf16[256,1280]{1,0:T(8,128)(2,1)S(1)} %get-tuple-element.39), channel_id=1, source_target_pairs={{0,192},{1,193},{2,194},{3,195},{4,196},{5,197},{6,198},{7,199},{8... | collective-permute-start | bytes 1966088 | tf_op jit(solution)/shard_map/ppermute | solution.py:27
  131.0 10.7 %collective-permute-start.24 = (bf16[256,1280]{1,0:T(8,128)(2,1)S(1)}, bf16[256,1280]{1,0:T(8,128)(2,1)S(1)}, u32[]{:S(2)}, u32[]{:S(2)}) collective-permute-start(bf16[256,1280]{1,0:T(8,128)(2,1)S(1)} %get-tuple-element.37), channel_id=1, source_target_pairs={{0,3},{1,2},{2,1},{3,0},{4,7},{5,6},{6,5},{7,4},{8,11},{9,10},{10,... | collective-permute-start | bytes 1966088 | tf_op jit(solution)/shard_map/ppermute | solution.py:27
  140.7 7.2 %collective-permute-start.29 = (bf16[128,1280]{1,0:T(8,128)(2,1)S(1)}, bf16[128,1280]{1,0:T(8,128)(2,1)S(1)}, u32[]{:S(2)}, u32[]{:S(2)}) collective-permute-start(bf16[128,1280]{1,0:T(8,128)(2,1)S(1)} %slice.175), channel_id=1, source_target_pairs={{0,64},{1,65},{2,66},{3,67},{4,68},{5,69},{6,70},{7,71},{8,72},{9,... | collective-permute-start | bytes 983048 | tf_op jit(solution)/shard_map/ppermute | solution.py:27
  141.8 7.2 %collective-permute-start.25 = (bf16[128,1280]{1,0:T(8,128)(2,1)S(1)}, bf16[128,1280]{1,0:T(8,128)(2,1)S(1)}, u32[]{:S(2)}, u32[]{:S(2)}) collective-permute-start(bf16[128,1280]{1,0:T(8,128)(2,1)S(1)} %slice.176), channel_id=1, source_target_pairs={{0,1},{1,0},{2,3},{3,2},{4,5},{5,4},{6,7},{7,6},{8,9},{9,8},{10,11... | collective-permute-start | bytes 983048 | tf_op jit(solution)/shard_map/ppermute | solution.py:27
  158.6 5.8 %collective-permute-start.32 = (bf16[16,2560]{1,0:T(8,128)(2,1)S(1)}, bf16[16,2560]{1,0:T(8,128)(2,1)S(1)}, u32[]{:S(2)}, u32[]{:S(2)}) collective-permute-start(bf16[16,2560]{1,0:T(8,128)(2,1)S(1)} %fusion.36), channel_id=1, source_target_pairs={{0,24},{1,25},{2,26},{3,27},{4,28},{5,29},{6,30},{7,31},{8,16},{9,... | collective-permute-start | bytes 245768 | tf_op jit(solution)/shard_map/ppermute | solution.py:27
  171.9 8.4 %collective-permute-start.35 = (f32[2,2560]{1,0:T(2,128)S(1)}, f32[2,2560]{1,0:T(2,128)S(1)}, u32[]{:S(2)}, u32[]{:S(2)}) collective-permute-start(f32[2,2560]{1,0:T(2,128)S(1)} %constant_dynamic-slice_fusion), channel_id=1, source_target_pairs={{0,32},{1,33},{2,34},{3,35},{4,36},{5,37},{6,38},{7,39},{8,40},{9,... | collective-permute-start | bytes 61448 | tf_op jit(solution)/shard_map/ppermute | solution.py:27
  (22 other events, 156.8 us)
where the time goes:
time: 181 us
  starting transfers between devices  62.6 us (35%)
  waiting for transfers between devices  57.4 us (32%)
  Pallas kernels  23.5 us (13%)
  local copies, waits for them, and re-layouts  17.1 us (9%)
  blocking collectives  11.1 us (6%)
  other arithmetic  8.19 us (5%)
    ppermute x36, starting transfers between devices, exchange(): return lax.ppermute(value, AXES, pairs)  62.6 us
    ppermute x36, waiting for transfers between devices, exchange(): return lax.ppermute(value, AXES, pairs)  57.4 us
    pallas_call x8, Pallas kernels, run(): pl.pallas_call(kernel, out_shape=outputs, grid_spec=pltpu.PrefetchScalarG...  23.5 us
    all_to_all x1, blocking collectives, on_device(): lax.all_to_all(jnp.broadcast_to(line_message[None], (X * Y, 8, mine)), ('...  11.1 us
    unnamed x21, local copies, waits for them, and re-layouts  9.43 us
    gather x2, local copies, waits for them, and re-layouts, on_device(): partner = jnp.take(pair_map, flat(sx, sc, sz, sy) * own_rows + sr, axis=0)  3.64 us
  transfers between devices with their start and end apart: 36, of which 25 were waited for; matrix products, arithmetic and copies ran while one was open for 7% of the time, Pallas kernels for 9%

commit v1 on v0

--- a/solution.py
+++ b/solution.py
@@ -74,15 +74,13 @@
 
 
 CONTRACT_LAST = (((1,), (1,)), ((), ()))
-VMEM_LIMIT = 40 * 1024 * 1024
-
-
-def whole(array):
-    zeros = (0,) * array.ndim
-    return pl.BlockSpec(array.shape, lambda *_: zeros)
-
-
-def run(kernel, name, flags, operands, outputs, grid=(1,), scratch=(), in_specs=None, out_specs=None, flops=0):
+VMEM_LIMIT = 24 * 1024 * 1024
+
+
+WHOLE = pl.BlockSpec(memory_space=pltpu.VMEM)
+
+
+def run(kernel, name, flags, operands, outputs, grid=(1,), scratch=(), in_specs=None, flops=0):
     bytes_accessed = sum(v.size * v.dtype.itemsize for v in (*operands, *outputs))
     return pl.pallas_call(
         kernel,
@@ -90,8 +88,8 @@
         grid_spec=pltpu.PrefetchScalarGridSpec(
             num_scalar_prefetch=1,
             grid=grid,
-            in_specs=in_specs or [whole(v) for v in operands],
-            out_specs=out_specs or [whole(v) for v in outputs],
+            in_specs=in_specs or [WHOLE] * len(operands),
+            out_specs=[WHOLE] * len(outputs),
             scratch_shapes=list(scratch),
         ),
         compiler_params=pltpu.CompilerParams(vmem_limit_bytes=VMEM_LIMIT),
@@ -118,13 +116,18 @@
             base[rows_at(place, line), :] = piece[start + line : start + count, :]
 
 
-def two_products(x, part, head_keep, head_got):
-    def product(head):
-        return jnp.dot(x[0], head[:part, :], preferred_element_type=F32) + jnp.dot(
-            x[1], head[part:, :], preferred_element_type=F32
+def take_head(flags, head, head_keep):
+    head_keep[...] = head[...]
+
+
+def two_products(core, x, part, head_keep, head_got):
+    def product(head, first):
+        return jnp.dot(x[0], head[first(0), :], preferred_element_type=F32) + jnp.dot(
+            x[1], head[first(1), :], preferred_element_type=F32
         )
 
-    return product(head_keep), product(head_got)
+    own = product(head_keep, lambda i: pl.ds(i * part, part))
+    return own, product(head_got, lambda i: pl.ds(pl.multiple_of(core * 2 * part + i * part, part), part))
 
 
 def store_halves(own, other, keep, send):
@@ -145,17 +148,20 @@
 def base_kernel(
     flags, low_place, high_place, a, a_near, a_far, b, b_near, b_far, head_keep, head_got, keep, send
 ):
+    count = keep.shape[0]
+    here = rows_at(pl.program_id(0), count)
+
     def pick(place, rows, near, far):
-        count, ring = place.shape[0], rows.shape[0]
+        ring = rows.shape[0]
         lanes = lax.broadcasted_iota(jnp.int32, (count, 4 * ring), 1)
-        one_hot = jnp.where(place[...] == lanes, 1.0, 0.0).astype(BF16)
+        one_hot = jnp.where(place[here, :] == lanes, 1.0, 0.0).astype(BF16)
         total = jnp.dot(one_hot[:, :ring], rows[...], preferred_element_type=F32)
         total += jnp.dot(one_hot[:, ring : 2 * ring], near[...], preferred_element_type=F32)
         total += jnp.dot(one_hot[:, 2 * ring :], far[...], preferred_element_type=F32)
         return total.astype(BF16)
 
     x = (pick(low_place, a, a_near, a_far), pick(high_place, b, b_near, b_far))
-    own, other = two_products(x, a.shape[1], head_keep, head_got)
+    own, other = two_products(flags[0], x, a.shape[1], head_keep, head_got)
     store_halves(own, other, keep, send)
 
 
@@ -177,14 +183,15 @@
                 rows[rows_at((y ^ flip) * X + place, line), part:] = piece[start + y * line : start + (y + 1) * line, :]
 
     x = rows[rows_at(step, mine), :]
-    own, other = two_products((x[:, :part], x[:, part:]), part, head_keep, head_got)
+    own, other = two_products(flags[0], (x[:, :part], x[:, part:]), part, head_keep, head_got)
     store_halves(own, other, keep, send)
 
 
-def local_kernel(flags, common, policy_keep, policy_got, base_keep, base_got, message, parts, parts_sent):
+def local_kernel(steps, flags, common, policy_keep, policy_got, base_keep, base_got, message, parts, parts_sent):
     step = pl.program_id(0)
-    policy = policy_keep[...] + policy_got[...]
-    base = base_keep[...] + base_got[...]
+    here = rows_at(step, policy_keep.shape[0] // steps)
+    policy = policy_keep[here, :] + policy_got[here, :]
+    base = base_keep[here, :] + base_got[here, :]
     difference = policy - base
     columns = policy.shape[1] // 2
     policy_peak = jnp.max(policy, axis=1, keepdims=True)
@@ -196,12 +203,12 @@
     first = (policy_exp * (difference - center)).astype(BF16)
     second = policy_exp.astype(BF16)
     for i, v in enumerate((first, second)):
-        parts[i] = v
-        parts_sent[i, :, :columns] = v[:, columns:]
-        parts_sent[i, :, columns:] = v[:, :columns]
+        parts[i, here, :] = v
+        parts_sent[i, here, :columns] = v[:, columns:]
+        parts_sent[i, here, columns:] = v[:, :columns]
     mine = message.shape[1]
     lanes = lax.broadcasted_iota(jnp.int32, (policy.shape[0], mine), 1) + flags[0] * mine
-    match = common[...] == lanes
+    match = common[here, :] == lanes
     values = (
         policy_peak + jnp.log(policy_total),
         base_peak + jnp.log(base_total),
@@ -268,24 +275,24 @@
             piece = grad[block * line : (block + 1) * line]
             by_y[rows_at(y * X + x, line), :] = piece
             by_x[rows_at(x * Y + y, line), :] = piece
-    low[...] = gradient(by_y[mine:, :], head_keep, head_got, 0).astype(BF16)
-    high[...] = gradient(by_x[mine:, :], head_keep, head_got, 1).astype(BF16)
+    low[...] = gradient(core, by_y[mine:, :], head_keep, head_got, 0).astype(BF16)
+    high[...] = gradient(core, by_x[mine:, :], head_keep, head_got, 1).astype(BF16)
     low_rows[...] = by_y[:mine, :]
     high_rows[...] = by_x[:mine, :]
 
 
-def gradient(rows, head_keep, head_got, which):
-    columns = head_keep.shape[1]
-    part = head_keep.shape[0] // 2
-    span = slice(which * part, (which + 1) * part)
+def gradient(core, rows, head_keep, head_got, which):
+    half, columns = head_keep.shape
+    part = half // 2
+    got = head_got[pl.ds(pl.multiple_of(core * half + which * part, part), part), :]
     return lax.dot_general(
-        rows[:, :columns], head_keep[span, :], CONTRACT_LAST, preferred_element_type=F32
-    ) + lax.dot_general(rows[:, columns:], head_got[span, :], CONTRACT_LAST, preferred_element_type=F32)
+        rows[:, :columns], head_keep[which * part : (which + 1) * part, :], CONTRACT_LAST, preferred_element_type=F32
+    ) + lax.dot_general(rows[:, columns:], got, CONTRACT_LAST, preferred_element_type=F32)
 
 
 def kept_kernel(flags, low_rows, high_rows, head_keep, head_got, low, high):
-    low[...] = gradient(low_rows[...], head_keep, head_got, 0)
-    high[...] = gradient(high_rows[...], head_keep, head_got, 1)
+    low[...] = gradient(flags[0], low_rows[...], head_keep, head_got, 0)
+    high[...] = gradient(flags[0], high_rows[...], head_keep, head_got, 1)
 
 
 def on_device(policy_hidden, reference_hidden, head_weight, pair_map, response_mask):
@@ -311,10 +318,16 @@
         [first_rows[:own_rows], second_rows[:own_rows], first_rows[own_rows:], second_rows[own_rows:]], 0
     )
     rows, head_weight = lax.optimization_barrier((rows, head_weight))
-    head_got = exchange(lax.dynamic_slice_in_dim(head_weight, (1 - c0) * half, half, 0), across_cores)
+    head_got = exchange(head_weight, across_cores)
     flags = jnp.stack([c0, c0 ^ (y0 >> 1)]).astype(jnp.int32)
-    head = (head_weight, head_got)
-    head_specs = [pl.BlockSpec((half, columns), lambda i, f: (f[0], 0)), whole(head_got)]
+    (head_keep,) = run(
+        take_head,
+        "take_head",
+        flags,
+        (head_weight,),
+        [jax.ShapeDtypeStruct((half, columns), BF16)],
+        in_specs=[pl.BlockSpec((half, columns), lambda i, f: (f[0], 0))],
+    )
 
     rows = gather_z(rows)
 
@@ -328,6 +341,8 @@
     sx = gray((slot // line) % X) ^ x0
     sy = gray((slot // ring) ^ jnp.where(swapped, 2, 0)) ^ y0
     partner = jnp.take(pair_map, flat(sx, sc, sz, sy) * own_rows + sr, axis=0)
+    rows, partner, head_keep = lax.optimization_barrier((rows, partner, head_keep))
+    head = (head_keep, head_got)
     pr, pdev = partner % own_rows, partner // own_rows
     py, pz, pc, px = pdev % Y, (pdev // Y) % Z, (pdev // (Y * Z)) % CORES, pdev // (Y * Z * CORES)
     tail = (z_slot(pz ^ z0) * CORES + pc) * own_rows + pr
@@ -363,7 +378,6 @@
         (low_place, high_place, *base, *head),
         logits,
         grid=(2,),
-        in_specs=[pl.BlockSpec((mine, 1), lambda i, f: (i, 0))] * 2 + [whole(v) for v in base] + head_specs,
         flops=2 * flops,
     )
     base_got = exchange(base_send, across_cores)
@@ -375,26 +389,21 @@
         (*policy, *head),
         logits,
         grid=(2,),
-        in_specs=[whole(v) for v in policy] + head_specs,
         scratch=[pltpu.VMEM((tokens, half), BF16)],
         flops=flops,
     )
     policy_got = exchange(policy_send, across_cores)
 
     steps = 4
-    row_spec = pl.BlockSpec((mine // steps, 2 * columns), lambda i, f: (i, 0))
-    part_spec = pl.BlockSpec((2, mine // steps, 2 * columns), lambda i, f: (0, i, 0))
     message_shape = jax.ShapeDtypeStruct((8, mine), F32)
     parts_shape = jax.ShapeDtypeStruct((2, mine, 2 * columns), BF16)
     message, parts, parts_sent = run(
-        local_kernel,
+        functools.partial(local_kernel, steps),
         "local_sums",
         flags,
         (common[:mine], policy_keep, policy_got, base_keep, base_got),
         [message_shape, parts_shape, parts_shape],
         grid=(steps,),
-        in_specs=[pl.BlockSpec((mine // steps, 1), lambda i, f: (i, 0))] + [row_spec] * 4,
-        out_specs=[whole(message_shape), part_spec, part_spec],
     )
     parts_got = exchange(parts_sent, across_cores)
 
@@ -416,7 +425,6 @@
         flags,
         (*operands, *head),
         [sent_shape, sent_shape, rows_shape, rows_shape],
-        in_specs=[whole(v) for v in operands] + head_specs,
         scratch=[pltpu.VMEM((tokens, 2 * columns), BF16)] * 2,
         flops=flops // 2,
     )
@@ -427,7 +435,6 @@
         flags,
         (low_rows, high_rows, *head),
         [kept_shape, kept_shape],
-        in_specs=[whole(low_rows), whole(high_rows)] + head_specs,
         flops=flops // 2,
     )
     low_total = low_kept + low_got.astype(F32)

time: 181 us -> 190 us (1.050)
  Pallas kernels: 23.5 us -> 33.4 us
  waiting for transfers between devices: 57.4 us -> 54.1 us
    pallas_call x8 -> x9, Pallas kernels: 23.5 us -> 33.4 us  [run(): pl.pallas_call(kernel, out_shape=outputs, grid_spec=pltpu.PrefetchScalarG...]
    dynamic_slice x1 -> x0, local copies, waits for them, and re-layouts: 3.39 us -> none  [on_device(): lax.dynamic_slice_in_dim(head_weight, (1 - c0) * half, half, 0)]
    ppermute x36, waiting for transfers between devices: 57.4 us -> 54.1 us  [exchange(): return lax.ppermute(value, AXES, pairs)]
    unnamed x21 -> x41, local copies, waits for them, and re-layouts: 9.43 us -> 11.8 us
    concatenate x6, other arithmetic: 1.69 us -> 3.93 us  [ring_far(): return exchange(jnp.concatenate([rows, near], 0), along(3, 1))]
  transfers between devices with their start and end apart: 36 -> 36, of which waited for: 25 -> 27; matrix products, arithmetic and copies ran while one was open for 7% -> 7% of each run, Pallas kernels for 9% -> 13%
where the time goes in v1:
time: 190 us; the launch traced here: 189 us
  starting transfers between devices  62.1 us (33%)
  waiting for transfers between devices  54.1 us (28%)
  Pallas kernels  33.4 us (18%)
  local copies, waits for them, and re-layouts  18.7 us (10%)
  blocking collectives  11.7 us (6%)
  other arithmetic  8.34 us (4%)
    ppermute x36, starting transfers between devices, exchange(): return lax.ppermute(value, AXES, pairs)  62.1 us
    ppermute x36, waiting for transfers between devices, exchange(): return lax.ppermute(value, AXES, pairs)  54.1 us
    pallas_call x9, Pallas kernels, run(): pl.pallas_call(kernel, out_shape=outputs, grid_spec=pltpu.PrefetchScalarG...  33.4 us
    unnamed x41, local copies, waits for them, and re-layouts  11.8 us
    all_to_all x1, blocking collectives, on_device(): lax.all_to_all(jnp.broadcast_to(line_message[None], (X * Y, 8, mine)), ('...  11.7 us
    concatenate x6, other arithmetic, ring_far(): return exchange(jnp.concatenate([rows, near], 0), along(3, 1))  3.93 us
  transfers between devices with their start and end apart: 36, of which 27 were waited for; matrix products, arithmetic and copies ran while one was open for 7% of the time, Pallas kernels for 13%

profile of v1, /device:TPU:1, one launch (start us, length us, event | category | flops | bytes accessed | tf_op | source)
XLA Modules:
  0.0 189.3 jit_solution(3577582133411353508)
XLA Ops:
  1.5 3.3 %collective-permute-start = (bf16[4,2560]{1,0:T(4,128)(2,1)S(1)}, bf16[4,2560]{1,0:T(4,128)(2,1)S(1)}, u32[]{:S(2)}, u32[]{:S(2)}) collective-permute-start(bf16[4,2560]{1,0:T(4,128)(2,1)S(1)} %fusion.25), channel_id=1, source_target_pairs={{0,32},{1,33},{2,34},{3,35},{4,36},{5,37},{6,38},{7,39},{8,40},{9,... | collective-permute-start | bytes 61448 | tf_op jit(solution)/shard_map/ppermute | solution.py:27
  11.4 3.5 %gather_fusion = s32[512]{0:T(512)S(1)} fusion(s32[512]{0:T(512)S(1)} %copy-done, s32[1024]{0:T(1024)S(1)} %pad_clamp_fusion), kind=kCustom, calls=%fused_computation | custom fusion | bytes 6144 | tf_op jit(solution)/shard_map/jit(_take)/gather | solution.py:343
  15.0 4.0 %collective-permute-start.3 = (bf16[32,2560]{1,0:T(8,128)(2,1)S(1)}, bf16[32,2560]{1,0:T(8,128)(2,1)S(1)}, u32[]{:S(2)}, u32[]{:S(2)}) collective-permute-start(bf16[32,2560]{1,0:T(8,128)(2,1)S(1)} %pad_maximum_fusion.8), channel_id=1, source_target_pairs={{0,24},{1,25},{2,26},{3,27},{4,28},{5,29},{6,30},{7,31},{8,16},{9,... | collective-permute-start | bytes 491528 | tf_op jit(solution)/shard_map/ppermute | solution.py:27
  22.3 3.1 %collective-permute-done.3 = bf16[32,2560]{1,0:T(8,128)(2,1)S(1)} collective-permute-done((bf16[32,2560]{1,0:T(8,128)(2,1)S(1)}, bf16[32,2560]{1,0:T(8,128)(2,1)S(1)}, u32[]{:S(2)}, u32[]{:S(2)}) %collective-permute-start.3) | collective-permute-done | bytes 163872 | tf_op jit(solution)/shard_map/ppermute | solution.py:27
  27.5 2.8 %collective-permute-start.6 = (bf16[64,1280]{1,0:T(8,128)(2,1)S(1)}, bf16[64,1280]{1,0:T(8,128)(2,1)S(1)}, u32[]{:S(2)}, u32[]{:S(2)}) collective-permute-start(bf16[64,1280]{1,0:T(8,128)(2,1)S(1)} %get-tuple-element.48.high), channel_id=1, source_target_pairs={{0,1},{1,0},{2,3},{3,2},{4,5},{5,4},{6,7},{7,6},{8,9},{9,8},{10,11... | collective-permute-start | bytes 491528 | tf_op jit(solution)/shard_map/ppermute | solution.py:27
  33.2 2.5 %collective-permute-done.4.low_near = bf16[64,1280]{1,0:T(8,128)(2,1)S(1)} collective-permute-done((bf16[64,1280]{1,0:T(8,128)(2,1)S(1)}, bf16[64,1280]{1,0:T(8,128)(2,1)S(1)}, u32[]{:S(2)}, u32[]{:S(2)}) %collective-permute-start.4) | collective-permute-done | bytes 163872 | tf_op jit(solution)/shard_map/ppermute | solution.py:27
  36.1 3.3 %collective-permute-done.7.high_far = bf16[128,1280]{1,0:T(8,128)(2,1)S(1)} collective-permute-done((bf16[128,1280]{1,0:T(8,128)(2,1)S(1)}, bf16[128,1280]{1,0:T(8,128)(2,1)S(1)}, u32[]{:S(2)}, u32[]{:S(2)}) %collective-permute-start.7) | collective-permute-done | bytes 327712 | tf_op jit(solution)/shard_map/ppermute | solution.py:27
  39.4 2.7 %collective-permute-done.5.low_far = bf16[128,1280]{1,0:T(8,128)(2,1)S(1)} collective-permute-done((bf16[128,1280]{1,0:T(8,128)(2,1)S(1)}, bf16[128,1280]{1,0:T(8,128)(2,1)S(1)}, u32[]{:S(2)}, u32[]{:S(2)}) %collective-permute-start.5) | collective-permute-done | bytes 327712 | tf_op jit(solution)/shard_map/ppermute | solution.py:27
  57.9 6.1 %collective-permute-done.15.a_far = bf16[256,1280]{1,0:T(8,128)(2,1)} collective-permute-done((bf16[256,1280]{1,0:T(8,128)(2,1)}, bf16[256,1280]{1,0:T(8,128)(2,1)}, u32[]{:S(2)}, u32[]{:S(2)}) %collective-permute-start.15) | collective-permute-done | bytes 655392 | tf_op jit(solution)/shard_map/ppermute | solution.py:27
  69.0 9.8 %base_logits.1 = (f32[256,1024]{1,0:T(8,128)S(1)}, f32[256,1024]{1,0:T(8,128)}) custom-call(s32[2]{0:T(128)S(1)} %pad_add_fusion.flags, s32[512,1]{1,0:T(8,128)S(1)} %copy.15.low_place, s32[512,1]{1,0:T(8,128)S(1)} %copy-done.18, bf16[128,1280]{1,0:T(8,128)(2,1)S(1)} %copy-done.11, bf16[128,1280]{1,0:T(8,128)(2,1)S(1)} %copy-done.15, ...), custom_call_target="tpu_custom_call" | custom-call | flops 5368709120 | bytes 12587008 | tf_op jit(solution)/shard_map/base_logits/pallas_call | solution.py:85
  79.8 4.4 %collective-permute-start.18 = (f32[256,1024]{1,0:T(8,128)}, f32[256,1024]{1,0:T(8,128)}, u32[]{:S(2)}, u32[]{:S(2)}) collective-permute-start(f32[256,1024]{1,0:T(8,128)} %get-tuple-element.36), channel_id=1, source_target_pairs={{0,32},{1,33},{2,34},{3,35},{4,36},{5,37},{6,38},{7,39},{8,40},{9,... | collective-permute-start | bytes 3145736 | tf_op jit(solution)/shard_map/ppermute | solution.py:27
  84.3 7.8 %policy_logits.1 = (f32[256,1024]{1,0:T(8,128)S(1)}, f32[256,1024]{1,0:T(8,128)}) custom-call(s32[2]{0:T(128)S(1)} %pad_add_fusion.flags, bf16[128,1280]{1,0:T(8,128)(2,1)S(1)} %get-tuple-element.27.a, bf16[128,1280]{1,0:T(8,128)(2,1)S(1)} %copy-done.5, bf16[256,1280]{1,0:T(8,128)(2,1)} %collective-permute-done.9.a_far, ...), custom_call_target="tpu_custom_call" | custom-call | flops 2684354560 | bytes 12582912 | tf_op jit(solution)/shard_map/policy_logits/pallas_call | solution.py:85
  93.2 2.8 %collective-permute-done.13.policy_got = f32[256,1024]{1,0:T(8,128)} collective-permute-done((f32[256,1024]{1,0:T(8,128)}, f32[256,1024]{1,0:T(8,128)}, u32[]{:S(2)}, u32[]{:S(2)}) %collective-permute-start.13) | collective-permute-done | bytes 1048608 | tf_op jit(solution)/shard_map/ppermute | solution.py:27
  98.5 3.4 %local_sums.1 = (f32[8,256]{1,0:T(8,128)S(1)}, bf16[2,256,1024]{2,1,0:T(8,128)(2,1)S(1)}, bf16[2,256,1024]{2,1,0:T(8,128)(2,1)S(1)}) custom-call(s32[2]{0:T(128)S(1)} %pad_add_fusion.flags, s32[256,1]{1,0:T(8,128)S(1)} %copy.17.common, f32[256,1024]{1,0:T(8,128)S(1)} %copy-done.9, f32[256,1024]{1,0:T(8,128)} %collective-permute-done.13.policy_got, ...), custom_call_target="tpu_custom_call" | custom-call | bytes 6300672 | tf_op jit(solution)/shard_map/local_sums/pallas_call | solution.py:85
  108.5 4.9 %collective-permute-start.21 = (f32[32,256]{1,0:T(8,128)S(1)}, f32[32,256]{1,0:T(8,128)S(1)}, u32[]{:S(2)}, u32[]{:S(2)}) collective-permute-start(f32[32,256]{1,0:T(8,128)S(1)} %pad_maximum_fusion.11), channel_id=1, source_target_pairs={{0,24},{1,25},{2,26},{3,27},{4,28},{5,29},{6,30},{7,31},{8,16},{9,... | collective-permute-start | bytes 98312 | tf_op jit(solution)/shard_map/ppermute | solution.py:27
  115.5 11.7 %all_to_all.5.messages = f32[16,8,256]{2,1,0:T(8,128)S(1)} all-to-all(f32[16,8,256]{2,1,0:T(8,128)S(1)} %broadcast_in_dim.28), channel_id=1, replica_groups=mesh['x'=4,'core'=2,'z'=8,'y'=4] {'x','y'}, dimensions={0} | all-to-all | bytes 262144 | tf_op jit(solution)/shard_map/all_to_all | solution.py:414
  127.8 4.7 %collective-permute-start.22 = (f32[8,256]{1,0:T(8,128)S(1)}, f32[8,256]{1,0:T(8,128)S(1)}, u32[]{:S(2)}, u32[]{:S(2)}) collective-permute-start(f32[8,256]{1,0:T(8,128)S(1)} %result.1), channel_id=1, source_target_pairs={{0,32},{1,33},{2,34},{3,35},{4,36},{5,37},{6,38},{7,39},{8,40},{9,... | collective-permute-start | bytes 24584 | tf_op jit(solution)/shard_map/ppermute | solution.py:27
  133.3 5.2 %gradient_sent.1 = (bf16[256,1280]{1,0:T(8,128)(2,1)S(1)}, bf16[256,1280]{1,0:T(8,128)(2,1)S(1)}, bf16[256,1024]{1,0:T(8,128)(2,1)S(1)}, bf16[256,1024]{1,0:T(8,128)(2,1)S(1)}) custom-call(s32[2]{0:T(128)S(1)} %pad_add_fusion.flags, s32[512,1]{1,0:T(8,128)S(1)} %fusion.2.common, f32[8,256]{1,0:T(8,128)S(1)} %result.1, ...), custom_call_target="tpu_custom_call" | custom-call | flops 1342177280 | bytes 12339200 | tf_op jit(solution)/shard_map/gradient_sent/pallas_call | solution.py:85
  139.1 4.6 %gradient_kept.1 = (f32[256,1280]{1,0:T(8,128)S(1)}, f32[256,1280]{1,0:T(8,128)S(1)}) custom-call(s32[2]{0:T(128)S(1)} %pad_add_fusion.flags, bf16[256,1024]{1,0:T(8,128)(2,1)S(1)} %get-tuple-element.40.low_rows, bf16[256,1024]{1,0:T(8,128)(2,1)S(1)} %get-tuple-element.41.high_rows, bf16[2560,512]{1,0:T(8,128)(2,1)S(1)} %take_head.1.head_keep, ...), custom_call_target="tpu_custom_call" | custom-call | flops 1342177280 | bytes 11534336 | tf_op jit(solution)/shard_map/gradient_kept/pallas_call | solution.py:85
  143.7 4.6 %collective-permute-done.28 = bf16[256,1280]{1,0:T(8,128)(2,1)S(1)} collective-permute-done((bf16[256,1280]{1,0:T(8,128)(2,1)S(1)}, bf16[256,1280]{1,0:T(8,128)(2,1)S(1)}, u32[]{:S(2)}, u32[]{:S(2)}) %collective-permute-start.28) | collective-permute-done | bytes 655392 | tf_op jit(solution)/shard_map/ppermute | solution.py:27
  150.5 5.2 %collective-permute-done.29 = bf16[128,1280]{1,0:T(8,128)(2,1)S(1)} collective-permute-done((bf16[128,1280]{1,0:T(8,128)(2,1)S(1)}, bf16[128,1280]{1,0:T(8,128)(2,1)S(1)}, u32[]{:S(2)}, u32[]{:S(2)}) %collective-permute-start.29) | collective-permute-done | bytes 327712 | tf_op jit(solution)/shard_map/ppermute | solution.py:27
  157.4 2.9 %collective-permute-done.30 = bf16[64,1280]{1,0:T(8,128)(2,1)S(1)} collective-permute-done((bf16[64,1280]{1,0:T(8,128)(2,1)S(1)}, bf16[64,1280]{1,0:T(8,128)(2,1)S(1)}, u32[]{:S(2)}, u32[]{:S(2)}) %collective-permute-start.30) | collective-permute-done | bytes 163872 | tf_op jit(solution)/shard_map/ppermute | solution.py:27
  166.5 4.2 %collective-permute-start.32 = (bf16[16,2560]{1,0:T(8,128)(2,1)S(1)}, bf16[16,2560]{1,0:T(8,128)(2,1)S(1)}, u32[]{:S(2)}, u32[]{:S(2)}) collective-permute-start(bf16[16,2560]{1,0:T(8,128)(2,1)S(1)} %fusion.22), channel_id=1, source_target_pairs={{0,24},{1,25},{2,26},{3,27},{4,28},{5,29},{6,30},{7,31},{8,16},{9,... | collective-permute-start | bytes 245768 | tf_op jit(solution)/shard_map/ppermute | solution.py:27
  179.9 7.8 %collective-permute-start.35 = (f32[2,2560]{1,0:T(2,128)S(1)}, f32[2,2560]{1,0:T(2,128)S(1)}, u32[]{:S(2)}, u32[]{:S(2)}) collective-permute-start(f32[2,2560]{1,0:T(2,128)S(1)} %constant_dynamic-slice_fusion), channel_id=1, source_target_pairs={{0,32},{1,33},{2,34},{3,35},{4,36},{5,37},{6,38},{7,39},{8,40},{9,... | collective-permute-start | bytes 61448 | tf_op jit(solution)/shard_map/ppermute | solution.py:27
  (161 shorter events, 72.8 us)
Async XLA Ops:
  6.6 57.5 %collective-permute-start.12 = (bf16[5120,512]{1,0:T(8,128)(2,1)}, bf16[5120,512]{1,0:T(8,128)(2,1)}, u32[]{:S(2)}, u32[]{:S(2)}) collective-permute-start(bf16[5120,512]{1,0:T(8,128)(2,1)} %head), channel_id=1, source_target_pairs={{0,32},{1,33},{2,34},{3,35},{4,36},{5,37},{6,38},{7,39},{8,40},{9,... | collective-permute-start | bytes 15728648 | tf_op jit(solution)/shard_map/ppermute | solution.py:27
  15.0 10.4 %collective-permute-start.3 = (bf16[32,2560]{1,0:T(8,128)(2,1)S(1)}, bf16[32,2560]{1,0:T(8,128)(2,1)S(1)}, u32[]{:S(2)}, u32[]{:S(2)}) collective-permute-start(bf16[32,2560]{1,0:T(8,128)(2,1)S(1)} %pad_maximum_fusion.8), channel_id=1, source_target_pairs={{0,24},{1,25},{2,26},{3,27},{4,28},{5,29},{6,30},{7,31},{8,16},{9,... | collective-permute-start | bytes 491528 | tf_op jit(solution)/shard_map/ppermute | solution.py:27
  27.5 5.5 %collective-permute-start.6 = (bf16[64,1280]{1,0:T(8,128)(2,1)S(1)}, bf16[64,1280]{1,0:T(8,128)(2,1)S(1)}, u32[]{:S(2)}, u32[]{:S(2)}) collective-permute-start(bf16[64,1280]{1,0:T(8,128)(2,1)S(1)} %get-tuple-element.48.high), channel_id=1, source_target_pairs={{0,1},{1,0},{2,3},{3,2},{4,5},{5,4},{6,7},{7,6},{8,9},{9,8},{10,11... | collective-permute-start | bytes 491528 | tf_op jit(solution)/shard_map/ppermute | solution.py:27
  30.3 5.4 %collective-permute-start.4 = (bf16[64,1280]{1,0:T(8,128)(2,1)S(1)}, bf16[64,1280]{1,0:T(8,128)(2,1)S(1)}, u32[]{:S(2)}, u32[]{:S(2)}) collective-permute-start(bf16[64,1280]{1,0:T(8,128)(2,1)S(1)} %get-tuple-element.49.low), channel_id=1, source_target_pairs={{0,64},{1,65},{2,66},{3,67},{4,68},{5,69},{6,70},{7,71},{8,72},{9,... | collective-permute-start | bytes 491528 | tf_op jit(solution)/shard_map/ppermute | solution.py:27
  33.0 6.3 %collective-permute-start.7 = (bf16[128,1280]{1,0:T(8,128)(2,1)S(1)}, bf16[128,1280]{1,0:T(8,128)(2,1)S(1)}, u32[]{:S(2)}, u32[]{:S(2)}) collective-permute-start(bf16[128,1280]{1,0:T(8,128)(2,1)S(1)} %pad_maximum_fusion.6), channel_id=1, source_target_pairs={{0,3},{1,2},{2,1},{3,0},{4,7},{5,6},{6,5},{7,4},{8,11},{9,10},{10,... | collective-permute-start | bytes 983048 | tf_op jit(solution)/shard_map/ppermute | solution.py:27
  35.7 6.3 %collective-permute-start.5 = (bf16[128,1280]{1,0:T(8,128)(2,1)S(1)}, bf16[128,1280]{1,0:T(8,128)(2,1)S(1)}, u32[]{:S(2)}, u32[]{:S(2)}) collective-permute-start(bf16[128,1280]{1,0:T(8,128)(2,1)S(1)} %pad_maximum_fusion.5), channel_id=1, source_target_pairs={{0,192},{1,193},{2,194},{3,195},{4,196},{5,197},{6,198},{7,199},{8... | collective-permute-start | bytes 983048 | tf_op jit(solution)/shard_map/ppermute | solution.py:27
  42.7 7.2 %collective-permute-start.14 = (bf16[128,1280]{1,0:T(8,128)(2,1)S(1)}, bf16[128,1280]{1,0:T(8,128)(2,1)S(1)}, u32[]{:S(2)}, u32[]{:S(2)}) collective-permute-start(bf16[128,1280]{1,0:T(8,128)(2,1)S(1)} %get-tuple-element.33.a), channel_id=1, source_target_pairs={{0,1},{1,0},{2,3},{3,2},{4,5},{5,4},{6,7},{7,6},{8,9},{9,8},{10,11... | collective-permute-start | bytes 983048 | tf_op jit(solution)/shard_map/ppermute | solution.py:27
  42.9 7.9 %collective-permute-start.16 = (bf16[128,1280]{1,0:T(8,128)(2,1)S(1)}, bf16[128,1280]{1,0:T(8,128)(2,1)S(1)}, u32[]{:S(2)}, u32[]{:S(2)}) collective-permute-start(bf16[128,1280]{1,0:T(8,128)(2,1)S(1)} %get-tuple-element.34.b), channel_id=1, source_target_pairs={{0,64},{1,65},{2,66},{3,67},{4,68},{5,69},{6,70},{7,71},{8,72},{9,... | collective-permute-start | bytes 983048 | tf_op jit(solution)/shard_map/ppermute | solution.py:27
  45.4 8.1 %collective-permute-start.10 = (bf16[128,1280]{1,0:T(8,128)(2,1)S(1)}, bf16[128,1280]{1,0:T(8,128)(2,1)S(1)}, u32[]{:S(2)}, u32[]{:S(2)}) collective-permute-start(bf16[128,1280]{1,0:T(8,128)(2,1)S(1)} %get-tuple-element.28.b), channel_id=1, source_target_pairs={{0,64},{1,65},{2,66},{3,67},{4,68},{5,69},{6,70},{7,71},{8,72},{9,... | collective-permute-start | bytes 983048 | tf_op jit(solution)/shard_map/ppermute | solution.py:27
  45.7 9.2 %collective-permute-start.8 = (bf16[128,1280]{1,0:T(8,128)(2,1)S(1)}, bf16[128,1280]{1,0:T(8,128)(2,1)S(1)}, u32[]{:S(2)}, u32[]{:S(2)}) collective-permute-start(bf16[128,1280]{1,0:T(8,128)(2,1)S(1)} %get-tuple-element.27.a), channel_id=1, source_target_pairs={{0,1},{1,0},{2,3},{3,2},{4,5},{5,4},{6,7},{7,6},{8,9},{9,8},{10,11... | collective-permute-start | bytes 983048 | tf_op jit(solution)/shard_map/ppermute | solution.py:27
  50.8 13.1 %collective-permute-start.15 = (bf16[256,1280]{1,0:T(8,128)(2,1)}, bf16[256,1280]{1,0:T(8,128)(2,1)}, u32[]{:S(2)}, u32[]{:S(2)}) collective-permute-start(bf16[256,1280]{1,0:T(8,128)(2,1)} %pad_maximum_fusion.2), channel_id=1, source_target_pairs={{0,3},{1,2},{2,1},{3,0},{4,7},{5,6},{6,5},{7,4},{8,11},{9,10},{10,... | collective-permute-start | bytes 1966088 | tf_op jit(solution)/shard_map/ppermute | solution.py:27
  51.9 12.3 %collective-permute-start.17 = (bf16[256,1280]{1,0:T(8,128)(2,1)}, bf16[256,1280]{1,0:T(8,128)(2,1)}, u32[]{:S(2)}, u32[]{:S(2)}) collective-permute-start(bf16[256,1280]{1,0:T(8,128)(2,1)} %pad_maximum_fusion.3), channel_id=1, source_target_pairs={{0,192},{1,193},{2,194},{3,195},{4,196},{5,197},{6,198},{7,199},{8... | collective-permute-start | bytes 1966088 | tf_op jit(solution)/shard_map/ppermute | solution.py:27
  54.6 29.7 %collective-permute-start.11 = (bf16[256,1280]{1,0:T(8,128)(2,1)}, bf16[256,1280]{1,0:T(8,128)(2,1)}, u32[]{:S(2)}, u32[]{:S(2)}) collective-permute-start(bf16[256,1280]{1,0:T(8,128)(2,1)} %pad_maximum_fusion.1), channel_id=1, source_target_pairs={{0,192},{1,193},{2,194},{3,195},{4,196},{5,197},{6,198},{7,199},{8... | collective-permute-start | bytes 1966088 | tf_op jit(solution)/shard_map/ppermute | solution.py:27
  55.8 28.4 %collective-permute-start.9 = (bf16[256,1280]{1,0:T(8,128)(2,1)}, bf16[256,1280]{1,0:T(8,128)(2,1)}, u32[]{:S(2)}, u32[]{:S(2)}) collective-permute-start(bf16[256,1280]{1,0:T(8,128)(2,1)} %pad_maximum_fusion), channel_id=1, source_target_pairs={{0,3},{1,2},{2,1},{3,0},{4,7},{5,6},{6,5},{7,4},{8,11},{9,10},{10,... | collective-permute-start | bytes 1966088 | tf_op jit(solution)/shard_map/ppermute | solution.py:27
  79.8 13.4 %collective-permute-start.18 = (f32[256,1024]{1,0:T(8,128)}, f32[256,1024]{1,0:T(8,128)}, u32[]{:S(2)}, u32[]{:S(2)}) collective-permute-start(f32[256,1024]{1,0:T(8,128)} %get-tuple-element.36), channel_id=1, source_target_pairs={{0,32},{1,33},{2,34},{3,35},{4,36},{5,37},{6,38},{7,39},{8,40},{9,... | collective-permute-start | bytes 3145736 | tf_op jit(solution)/shard_map/ppermute | solution.py:27
  101.9 31.4 %collective-permute-start.23 = (bf16[2,256,1024]{2,1,0:T(8,128)(2,1)S(1)}, bf16[2,256,1024]{2,1,0:T(8,128)(2,1)S(1)}, u32[]{:S(2)}, u32[]{:S(2)}) collective-permute-start(bf16[2,256,1024]{2,1,0:T(8,128)(2,1)S(1)} %get-tuple-element.39), channel_id=1, source_target_pairs={{0,32},{1,33},{2,34},{3,35},{4,36},{5,37},{6,38},{7,39},{8,40},{9,... | collective-permute-start | bytes 3145736 | tf_op jit(solution)/shard_map/ppermute | solution.py:27
  108.5 6.3 %collective-permute-start.21 = (f32[32,256]{1,0:T(8,128)S(1)}, f32[32,256]{1,0:T(8,128)S(1)}, u32[]{:S(2)}, u32[]{:S(2)}) collective-permute-start(f32[32,256]{1,0:T(8,128)S(1)} %pad_maximum_fusion.11), channel_id=1, source_target_pairs={{0,24},{1,25},{2,26},{3,27},{4,28},{5,29},{6,30},{7,31},{8,16},{9,... | collective-permute-start | bytes 98312 | tf_op jit(solution)/shard_map/ppermute | solution.py:27
  127.8 5.5 %collective-permute-start.22 = (f32[8,256]{1,0:T(8,128)S(1)}, f32[8,256]{1,0:T(8,128)S(1)}, u32[]{:S(2)}, u32[]{:S(2)}) collective-permute-start(f32[8,256]{1,0:T(8,128)S(1)} %result.1), channel_id=1, source_target_pairs={{0,32},{1,33},{2,34},{3,35},{4,36},{5,37},{6,38},{7,39},{8,40},{9,... | collective-permute-start | bytes 24584 | tf_op jit(solution)/shard_map/ppermute | solution.py:27
  138.5 9.8 %collective-permute-start.28 = (bf16[256,1280]{1,0:T(8,128)(2,1)S(1)}, bf16[256,1280]{1,0:T(8,128)(2,1)S(1)}, u32[]{:S(2)}, u32[]{:S(2)}) collective-permute-start(bf16[256,1280]{1,0:T(8,128)(2,1)S(1)} %get-tuple-element.45), channel_id=1, source_target_pairs={{0,192},{1,193},{2,194},{3,195},{4,196},{5,197},{6,198},{7,199},{8... | collective-permute-start | bytes 1966088 | tf_op jit(solution)/shard_map/ppermute | solution.py:27
  138.8 10.7 %collective-permute-start.24 = (bf16[256,1280]{1,0:T(8,128)(2,1)S(1)}, bf16[256,1280]{1,0:T(8,128)(2,1)S(1)}, u32[]{:S(2)}, u32[]{:S(2)}) collective-permute-start(bf16[256,1280]{1,0:T(8,128)(2,1)S(1)} %get-tuple-element.43), channel_id=1, source_target_pairs={{0,3},{1,2},{2,1},{3,0},{4,7},{5,6},{6,5},{7,4},{8,11},{9,10},{10,... | collective-permute-start | bytes 1966088 | tf_op jit(solution)/shard_map/ppermute | solution.py:27
  148.5 7.2 %collective-permute-start.29 = (bf16[128,1280]{1,0:T(8,128)(2,1)S(1)}, bf16[128,1280]{1,0:T(8,128)(2,1)S(1)}, u32[]{:S(2)}, u32[]{:S(2)}) collective-permute-start(bf16[128,1280]{1,0:T(8,128)(2,1)S(1)} %slice.175), channel_id=1, source_target_pairs={{0,64},{1,65},{2,66},{3,67},{4,68},{5,69},{6,70},{7,71},{8,72},{9,... | collective-permute-start | bytes 983048 | tf_op jit(solution)/shard_map/ppermute | solution.py:27
  149.6 7.2 %collective-permute-start.25 = (bf16[128,1280]{1,0:T(8,128)(2,1)S(1)}, bf16[128,1280]{1,0:T(8,128)(2,1)S(1)}, u32[]{:S(2)}, u32[]{:S(2)}) collective-permute-start(bf16[128,1280]{1,0:T(8,128)(2,1)S(1)} %slice.176), channel_id=1, source_target_pairs={{0,1},{1,0},{2,3},{3,2},{4,5},{5,4},{6,7},{7,6},{8,9},{9,8},{10,11... | collective-permute-start | bytes 983048 | tf_op jit(solution)/shard_map/ppermute | solution.py:27
  166.5 6.5 %collective-permute-start.32 = (bf16[16,2560]{1,0:T(8,128)(2,1)S(1)}, bf16[16,2560]{1,0:T(8,128)(2,1)S(1)}, u32[]{:S(2)}, u32[]{:S(2)}) collective-permute-start(bf16[16,2560]{1,0:T(8,128)(2,1)S(1)} %fusion.22), channel_id=1, source_target_pairs={{0,24},{1,25},{2,26},{3,27},{4,28},{5,29},{6,30},{7,31},{8,16},{9,... | collective-permute-start | bytes 245768 | tf_op jit(solution)/shard_map/ppermute | solution.py:27
  179.9 8.7 %collective-permute-start.35 = (f32[2,2560]{1,0:T(2,128)S(1)}, f32[2,2560]{1,0:T(2,128)S(1)}, u32[]{:S(2)}, u32[]{:S(2)}) collective-permute-start(f32[2,2560]{1,0:T(2,128)S(1)} %constant_dynamic-slice_fusion), channel_id=1, source_target_pairs={{0,32},{1,33},{2,34},{3,35},{4,36},{5,37},{6,38},{7,39},{8,40},{9,... | collective-permute-start | bytes 61448 | tf_op jit(solution)/shard_map/ppermute | solution.py:27
  (32 other events, 165.5 us)

commit v2 on v1

--- a/solution.py
+++ b/solution.py
@@ -54,8 +54,8 @@
     return j ^ ((j >> 2) << 1)
 
 
-def gather_z(rows):
-    for step in Z_STEPS:
+def gather_z(rows, steps):
+    for step in steps:
         rows = jnp.concatenate([rows, exchange(rows, along_z(step))], 0)
     return rows
 
@@ -74,7 +74,7 @@
 
 
 CONTRACT_LAST = (((1,), (1,)), ((), ()))
-VMEM_LIMIT = 24 * 1024 * 1024
+VMEM_LIMIT = 20 * 1024 * 1024
 
 
 WHOLE = pl.BlockSpec(memory_space=pltpu.VMEM)
@@ -106,28 +106,41 @@
     return pl.ds(pl.multiple_of(block * count, count), count)
 
 
-def order_kernel(line, flags, low, low_near, low_far, high, high_near, high_far, ra, rb, pa, pb):
+def as_column(row, start, count):
+    here = lax.broadcasted_iota(jnp.int32, (count, row.shape[1]), 0) + start
+    lanes = lax.broadcasted_iota(jnp.int32, (count, row.shape[1]), 1)
+    return jnp.sum(jnp.where(here == lanes, row, 0.0), axis=1, keepdims=True).astype(jnp.int32)
+
+
+def order_kernel(flags, low, low_near, low_far, high, high_near, high_far, ra, rb, pa, pb):
+    line, width = low.shape
+    part = width // 2
     places = ring_places(flags[0])
     for rows, near, far, base, policy in ((low, low_near, low_far, ra, pa), (high, high_near, high_far, rb, pb)):
-        count = 2 * line
-        pieces = ((rows, 0), (near, 0), (far, 0), (far, count))
-        for (piece, start), place in zip(pieces, places):
-            policy[rows_at(place, line), :] = piece[start : start + line, :]
-            base[rows_at(place, line), :] = piece[start + line : start + count, :]
-
-
-def take_head(flags, head, head_keep):
-    head_keep[...] = head[...]
-
-
-def two_products(core, x, part, head_keep, head_got):
-    def product(head, first):
-        return jnp.dot(x[0], head[first(0), :], preferred_element_type=F32) + jnp.dot(
-            x[1], head[first(1), :], preferred_element_type=F32
+        for (piece, start), place in zip(((rows, 0), (near, 0), (far, 0), (far, line)), places):
+            policy[rows_at(place, line), :] = piece[start : start + line, :part]
+            base[rows_at(place, line), :] = piece[start : start + line, part:]
+
+
+def take_head(flags, head, keep, send, keep_done, send_done):
+    half = keep.shape[0]
+    copies = [
+        pltpu.make_async_copy(head.at[rows_at(index, half), :], half_ref, done)
+        for index, half_ref, done in ((flags[0], keep, keep_done), (1 - flags[0], send, send_done))
+    ]
+    for copy in copies:
+        copy.start()
+    for copy in copies:
+        copy.wait()
+
+
+def two_products(x, part, head_keep, head_got):
+    def product(head):
+        return jnp.dot(x[0], head[:part, :], preferred_element_type=F32) + jnp.dot(
+            x[1], head[part:, :], preferred_element_type=F32
         )
 
-    own = product(head_keep, lambda i: pl.ds(i * part, part))
-    return own, product(head_got, lambda i: pl.ds(pl.multiple_of(core * 2 * part + i * part, part), part))
+    return product(head_keep), product(head_got)
 
 
 def store_halves(own, other, keep, send):
@@ -149,19 +162,19 @@
     flags, low_place, high_place, a, a_near, a_far, b, b_near, b_far, head_keep, head_got, keep, send
 ):
     count = keep.shape[0]
-    here = rows_at(pl.program_id(0), count)
+    first = pl.program_id(0) * count
 
     def pick(place, rows, near, far):
         ring = rows.shape[0]
         lanes = lax.broadcasted_iota(jnp.int32, (count, 4 * ring), 1)
-        one_hot = jnp.where(place[here, :] == lanes, 1.0, 0.0).astype(BF16)
+        one_hot = jnp.where(as_column(place[...], first, count) == lanes, 1.0, 0.0).astype(BF16)
         total = jnp.dot(one_hot[:, :ring], rows[...], preferred_element_type=F32)
         total += jnp.dot(one_hot[:, ring : 2 * ring], near[...], preferred_element_type=F32)
         total += jnp.dot(one_hot[:, 2 * ring :], far[...], preferred_element_type=F32)
         return total.astype(BF16)
 
     x = (pick(low_place, a, a_near, a_far), pick(high_place, b, b_near, b_far))
-    own, other = two_products(flags[0], x, a.shape[1], head_keep, head_got)
+    own, other = two_products(x, a.shape[1], head_keep, head_got)
     store_halves(own, other, keep, send)
 
 
@@ -183,7 +196,7 @@
                 rows[rows_at((y ^ flip) * X + place, line), part:] = piece[start + y * line : start + (y + 1) * line, :]
 
     x = rows[rows_at(step, mine), :]
-    own, other = two_products(flags[0], (x[:, :part], x[:, part:]), part, head_keep, head_got)
+    own, other = two_products((x[:, :part], x[:, part:]), part, head_keep, head_got)
     store_halves(own, other, keep, send)
 
 
@@ -208,7 +221,7 @@
         parts_sent[i, here, columns:] = v[:, :columns]
     mine = message.shape[1]
     lanes = lax.broadcasted_iota(jnp.int32, (policy.shape[0], mine), 1) + flags[0] * mine
-    match = common[here, :] == lanes
+    match = as_column(common[...], step * (mine // steps), mine // steps) == lanes
     values = (
         policy_peak + jnp.log(policy_total),
         base_peak + jnp.log(base_total),
@@ -266,7 +279,7 @@
     for h, (values, source) in enumerate(((result, parts), (result_got, parts_got))):
         first = (core if h == 0 else 1 - core) * mine
         lanes = lax.broadcasted_iota(jnp.int32, (mine, mine), 1) + first
-        match = common[h * mine : (h + 1) * mine, :] == lanes
+        match = as_column(common[:, h * mine : (h + 1) * mine], 0, mine) == lanes
         scale = jnp.sum(jnp.where(match, values[0:1, :], 0.0), axis=1, keepdims=True)
         shift = jnp.sum(jnp.where(match, values[1:2, :], 0.0), axis=1, keepdims=True)
         grad = (scale * (source[0].astype(F32) + shift * source[1].astype(F32))).astype(BF16)
@@ -275,24 +288,24 @@
             piece = grad[block * line : (block + 1) * line]
             by_y[rows_at(y * X + x, line), :] = piece
             by_x[rows_at(x * Y + y, line), :] = piece
-    low[...] = gradient(core, by_y[mine:, :], head_keep, head_got, 0).astype(BF16)
-    high[...] = gradient(core, by_x[mine:, :], head_keep, head_got, 1).astype(BF16)
+    low[...] = gradient(by_y[mine:, :], head_keep, head_got, 0).astype(BF16)
+    high[...] = gradient(by_x[mine:, :], head_keep, head_got, 1).astype(BF16)
     low_rows[...] = by_y[:mine, :]
     high_rows[...] = by_x[:mine, :]
 
 
-def gradient(core, rows, head_keep, head_got, which):
-    half, columns = head_keep.shape
-    part = half // 2
-    got = head_got[pl.ds(pl.multiple_of(core * half + which * part, part), part), :]
+def gradient(rows, head_keep, head_got, which):
+    columns = head_keep.shape[1]
+    part = head_keep.shape[0] // 2
+    span = slice(which * part, (which + 1) * part)
     return lax.dot_general(
-        rows[:, :columns], head_keep[which * part : (which + 1) * part, :], CONTRACT_LAST, preferred_element_type=F32
-    ) + lax.dot_general(rows[:, columns:], got, CONTRACT_LAST, preferred_element_type=F32)
+        rows[:, :columns], head_keep[span, :], CONTRACT_LAST, preferred_element_type=F32
+    ) + lax.dot_general(rows[:, columns:], head_got[span, :], CONTRACT_LAST, preferred_element_type=F32)
 
 
 def kept_kernel(flags, low_rows, high_rows, head_keep, head_got, low, high):
-    low[...] = gradient(flags[0], low_rows[...], head_keep, head_got, 0)
-    high[...] = gradient(flags[0], high_rows[...], head_keep, head_got, 1)
+    low[...] = gradient(low_rows[...], head_keep, head_got, 0)
+    high[...] = gradient(high_rows[...], head_keep, head_got, 1)
 
 
 def on_device(policy_hidden, reference_hidden, head_weight, pair_map, response_mask):
@@ -309,29 +322,27 @@
     tokens = Y * ring
     mine = tokens // 2
 
-    own = jnp.concatenate([policy_hidden, reference_hidden], 0)
-    keep = lax.dynamic_slice_in_dim(own, c0 * half, half, 1)
-    got = exchange(lax.dynamic_slice_in_dim(own, (1 - c0) * half, half, 1), across_cores)
-    first_rows = jnp.where(second, got, keep)
-    second_rows = jnp.where(second, keep, got)
-    rows = jnp.concatenate(
-        [first_rows[:own_rows], second_rows[:own_rows], first_rows[own_rows:], second_rows[own_rows:]], 0
-    )
+    def side_by_side(first):
+        p = lax.dynamic_slice_in_dim(policy_hidden, first, half, 1)
+        r = lax.dynamic_slice_in_dim(reference_hidden, first, half, 1)
+        return jnp.concatenate([p[:, :part], r[:, :part], p[:, part:], r[:, part:]], 1)
+
+    keep = side_by_side(c0 * half)
+    got = exchange(side_by_side((1 - c0) * half), across_cores)
+    rows = jnp.concatenate([jnp.where(second, got, keep), jnp.where(second, keep, got)], 0)
     rows, head_weight = lax.optimization_barrier((rows, head_weight))
-    head_got = exchange(head_weight, across_cores)
     flags = jnp.stack([c0, c0 ^ (y0 >> 1)]).astype(jnp.int32)
-    (head_keep,) = run(
+    head_shape = jax.ShapeDtypeStruct((half, columns), BF16)
+    head_keep, head_send = run(
         take_head,
         "take_head",
         flags,
         (head_weight,),
-        [jax.ShapeDtypeStruct((half, columns), BF16)],
-        in_specs=[pl.BlockSpec((half, columns), lambda i, f: (f[0], 0))],
-    )
-
-    rows = gather_z(rows)
-
-    slot = jnp.arange(tokens, dtype=jnp.int32)
+        [head_shape, head_shape],
+        in_specs=[pl.BlockSpec(memory_space=pltpu.HBM)],
+        scratch=[pltpu.SemaphoreType.DMA] * 2,
+    )
+    slot = jnp.arange(tokens, dtype=jnp.int32)[None]
 
     def raw(j):
         return jnp.where(second, jnp.where(j == 0, 0, jnp.where(j == 3, 1, j + 1)), gray(j))
@@ -341,22 +352,25 @@
     sx = gray((slot // line) % X) ^ x0
     sy = gray((slot // ring) ^ jnp.where(swapped, 2, 0)) ^ y0
     partner = jnp.take(pair_map, flat(sx, sc, sz, sy) * own_rows + sr, axis=0)
-    rows, partner, head_keep = lax.optimization_barrier((rows, partner, head_keep))
-    head = (head_keep, head_got)
+    rows = gather_z(rows, Z_STEPS[:1])
+    rows, partner = lax.optimization_barrier((rows, partner))
+    rows = gather_z(rows, Z_STEPS[1:2])
+    rows, head_keep, head_send = lax.optimization_barrier((rows, head_keep, head_send))
+    head = (head_keep, exchange(head_send, across_cores))
+    rows = gather_z(rows, Z_STEPS[2:])
     pr, pdev = partner % own_rows, partner // own_rows
     py, pz, pc, px = pdev % Y, (pdev // Y) % Z, (pdev // (Y * Z)) % CORES, pdev // (Y * Z * CORES)
     tail = (z_slot(pz ^ z0) * CORES + pc) * own_rows + pr
-    low_place = ((raw(py ^ y0) * X + gray(px ^ x0)) * line + tail)[:, None]
-    high_place = ((raw(px ^ x0) * Y + gray(py ^ y0)) * line + tail)[:, None]
-    common = (((sy * X + sx) * Z + sz) * chip_rows + sc * own_rows + sr)[:, None]
-
-    rows = rows.reshape(Z, 2, chip_rows, half).swapaxes(0, 1).reshape(2 * line, half)
-    low, high = rows[:, :part], rows[:, part:]
+    low_place = ((raw(py ^ y0) * X + gray(px ^ x0)) * line + tail).astype(F32)
+    high_place = ((raw(px ^ x0) * Y + gray(py ^ y0)) * line + tail).astype(F32)
+    common = (((sy * X + sx) * Z + sz) * chip_rows + sc * own_rows + sr).astype(F32)
+
+    low, high = rows[:, :half], rows[:, half:]
     low_near, high_near = ring_near(low, along_x), ring_near(high, along_y)
     low_far, high_far = ring_far(low, low_near, along_x), ring_far(high, high_near, along_y)
     block = jax.ShapeDtypeStruct((ring, part), BF16)
     ra, rb, pa, pb = run(
-        functools.partial(order_kernel, line),
+        order_kernel,
         "order",
         flags,
         (low, low_near, low_far, high, high_near, high_far),
@@ -401,7 +415,7 @@
         functools.partial(local_kernel, steps),
         "local_sums",
         flags,
-        (common[:mine], policy_keep, policy_got, base_keep, base_got),
+        (common[:, :mine], policy_keep, policy_got, base_keep, base_got),
         [message_shape, parts_shape, parts_shape],
         grid=(steps,),
     )

time: 190 us -> 167 us (0.88)
  Pallas kernels: 33.4 us -> 19.3 us
  waiting for transfers between devices: 54.1 us -> 67.3 us
  local copies, waits for them, and re-layouts: 18.7 us -> 7.08 us
  other arithmetic: 8.34 us -> 2.51 us
  blocking collectives: 11.7 us -> 9.25 us
    pallas_call x9, Pallas kernels: 33.4 us -> 19.3 us  [run(): pl.pallas_call(kernel, out_shape=outputs, grid_spec=pltpu.PrefetchScalarG...]
    ppermute x36, waiting for transfers between devices: 54.1 us -> 67.3 us  [exchange(): return lax.ppermute(value, AXES, pairs)]
    unnamed x41 -> x8, local copies, waits for them, and re-layouts: 11.8 us -> 2.52 us
    concatenate x6, other arithmetic: 3.93 us -> 0.22 us  [ring_far(): return exchange(jnp.concatenate([rows, near], 0), along(3, 1))]
    all_to_all x1, blocking collectives: 11.7 us -> 9.25 us  [on_device(): lax.all_to_all(jnp.broadcast_to(line_message[None], (X * Y, 8, mine)), ('...]
    reshape x3 -> x0, local copies, waits for them, and re-layouts: 1.97 us -> none  [on_device(): rows.reshape(Z, 2, chip_rows, half).swapaxes(0, 1).reshape(2 * line, half)]
  transfers between devices with their start and end apart: 36 -> 36, of which waited for: 27 -> 27; matrix products, arithmetic and copies ran while one was open for 7% -> 3% of each run, Pallas kernels for 13% -> 9%
where the time goes in v2:
time: 167 us
  waiting for transfers between devices  67.3 us (40%)
  starting transfers between devices  60.5 us (36%)
  Pallas kernels  19.3 us (12%)
  blocking collectives  9.25 us (6%)
  local copies, waits for them, and re-layouts  7.08 us (4%)
  other arithmetic  2.51 us (2%)
    ppermute x36, waiting for transfers between devices, exchange(): return lax.ppermute(value, AXES, pairs)  67.3 us
    ppermute x36, starting transfers between devices, exchange(): return lax.ppermute(value, AXES, pairs)  60.5 us
    pallas_call x9, Pallas kernels, run(): pl.pallas_call(kernel, out_shape=outputs, grid_spec=pltpu.PrefetchScalarG...  19.3 us
    all_to_all x1, blocking collectives, on_device(): lax.all_to_all(jnp.broadcast_to(line_message[None], (X * Y, 8, mine)), ('...  9.25 us
    gather x1, local copies, waits for them, and re-layouts, on_device(): partner = jnp.take(pair_map, flat(sx, sc, sz, sy) * own_rows + sr, axis=0)  3.49 us
  transfers between devices with their start and end apart: 36, of which 27 were waited for; matrix products, arithmetic and copies ran while one was open for 3% of the time, Pallas kernels for 9%

profile of v2, /device:TPU:1, one launch (start us, length us, event | category | flops | bytes accessed | tf_op | source)
XLA Modules:
  0.0 167.0 jit_solution(6830043622443003174)
XLA Ops:
  1.5 3.3 %collective-permute-start = (bf16[2,5120]{1,0:T(2,128)(2,1)S(1)}, bf16[2,5120]{1,0:T(2,128)(2,1)S(1)}, u32[]{:S(2)}, u32[]{:S(2)}) collective-permute-start(bf16[2,5120]{1,0:T(2,128)(2,1)S(1)} %pad_maximum_fusion.11), channel_id=1, source_target_pairs={{0,32},{1,33},{2,34},{3,35},{4,36},{5,37},{6,38},{7,39},{8,40},{9,... | collective-permute-start | bytes 61448 | tf_op jit(solution)/shard_map/ppermute | solution.py:27
  4.9 3.5 %gather_fusion = s32[512]{0:T(512)S(1)} fusion(s32[512]{0:T(512)S(1)} %copy-done, s32[1024]{0:T(1024)S(1)} %pad_clamp_fusion), kind=kCustom, calls=%fused_computation | custom fusion | bytes 6144 | tf_op jit(solution)/shard_map/jit(_take)/gather | solution.py:354
  8.7 2.8 %collective-permute-done.1 = bf16[4,5120]{1,0:T(4,128)(2,1)S(1)} collective-permute-done((bf16[4,5120]{1,0:T(4,128)(2,1)S(1)}, bf16[4,5120]{1,0:T(4,128)(2,1)S(1)}, u32[]{:S(2)}, u32[]{:S(2)}) %collective-permute-start.1) | collective-permute-done | bytes 40992 | tf_op jit(solution)/shard_map/ppermute | solution.py:27
  18.0 2.7 %collective-permute-start.3 = (bf16[16,5120]{1,0:T(8,128)(2,1)S(1)}, bf16[16,5120]{1,0:T(8,128)(2,1)S(1)}, u32[]{:S(2)}, u32[]{:S(2)}) collective-permute-start(bf16[16,5120]{1,0:T(8,128)(2,1)S(1)} %pad_maximum_fusion.7), channel_id=1, source_target_pairs={{0,24},{1,25},{2,26},{3,27},{4,28},{5,29},{6,30},{7,31},{8,16},{9,... | collective-permute-start | bytes 491528 | tf_op jit(solution)/shard_map/ppermute | solution.py:27
  20.7 4.3 %collective-permute-done.3 = bf16[16,5120]{1,0:T(8,128)(2,1)S(1)} collective-permute-done((bf16[16,5120]{1,0:T(8,128)(2,1)S(1)}, bf16[16,5120]{1,0:T(8,128)(2,1)S(1)}, u32[]{:S(2)}, u32[]{:S(2)}) %collective-permute-start.3) | collective-permute-done | bytes 163872 | tf_op jit(solution)/shard_map/ppermute | solution.py:27
  25.0 2.8 %collective-permute-start.6 = (bf16[32,2560]{1,0:T(8,128)(2,1)S(1)}, bf16[32,2560]{1,0:T(8,128)(2,1)S(1)}, u32[]{:S(2)}, u32[]{:S(2)}) collective-permute-start(bf16[32,2560]{1,0:T(8,128)(2,1)S(1)} %get-tuple-element.60.high), channel_id=1, source_target_pairs={{0,1},{1,0},{2,3},{3,2},{4,5},{5,4},{6,7},{7,6},{8,9},{9,8},{10,11... | collective-permute-start | bytes 491528 | tf_op jit(solution)/shard_map/ppermute | solution.py:27
  33.1 2.6 %collective-permute-done.4.low_near = bf16[32,2560]{1,0:T(8,128)(2,1)S(1)} collective-permute-done((bf16[32,2560]{1,0:T(8,128)(2,1)S(1)}, bf16[32,2560]{1,0:T(8,128)(2,1)S(1)}, u32[]{:S(2)}, u32[]{:S(2)}) %collective-permute-start.4) | collective-permute-done | bytes 163872 | tf_op jit(solution)/shard_map/ppermute | solution.py:27
  36.1 3.0 %collective-permute-done.7.high_far = bf16[64,2560]{1,0:T(8,128)(2,1)S(1)} collective-permute-done((bf16[64,2560]{1,0:T(8,128)(2,1)S(1)}, bf16[64,2560]{1,0:T(8,128)(2,1)S(1)}, u32[]{:S(2)}, u32[]{:S(2)}) %collective-permute-start.7) | collective-permute-done | bytes 327712 | tf_op jit(solution)/shard_map/ppermute | solution.py:27
  39.2 2.9 %collective-permute-done.5.low_far = bf16[64,2560]{1,0:T(8,128)(2,1)S(1)} collective-permute-done((bf16[64,2560]{1,0:T(8,128)(2,1)S(1)}, bf16[64,2560]{1,0:T(8,128)(2,1)S(1)}, u32[]{:S(2)}, u32[]{:S(2)}) %collective-permute-start.5) | collective-permute-done | bytes 327712 | tf_op jit(solution)/shard_map/ppermute | solution.py:27
  56.2 7.3 %collective-permute-done.17.b_far = bf16[256,1280]{1,0:T(8,128)(2,1)S(1)} collective-permute-done((bf16[256,1280]{1,0:T(8,128)(2,1)S(1)}, bf16[256,1280]{1,0:T(8,128)(2,1)S(1)}, u32[]{:S(2)}, u32[]{:S(2)}) %collective-permute-start.17) | collective-permute-done | bytes 655392 | tf_op jit(solution)/shard_map/ppermute | solution.py:27
  63.9 6.0 %base_logits.1 = (f32[256,1024]{1,0:T(8,128)S(1)}, f32[256,1024]{1,0:T(8,128)S(1)}) custom-call(s32[2]{0:T(128)S(1)} %pad_add_fusion.flags, f32[1,512]{1,0:T(1,128)S(1)} %add_convert_fusion.1.low_place, f32[1,512]{1,0:T(1,128)S(1)} %get-tuple-element.54.high_place, bf16[128,1280]{1,0:T(8,128)(2,1)S(1)} %get-tuple-element.41.a, ...), custom_call_target="tpu_custom_call" | custom-call | flops 5368709120 | bytes 9965568 | tf_op jit(solution)/shard_map/base_logits/pallas_call | solution.py:85
  69.9 5.2 %collective-permute-start.18 = (f32[256,1024]{1,0:T(8,128)S(1)}, f32[256,1024]{1,0:T(8,128)S(1)}, u32[]{:S(2)}, u32[]{:S(2)}) collective-permute-start(f32[256,1024]{1,0:T(8,128)S(1)} %get-tuple-element.44), channel_id=1, source_target_pairs={{0,32},{1,33},{2,34},{3,35},{4,36},{5,37},{6,38},{7,39},{8,40},{9,... | collective-permute-start | bytes 3145736 | tf_op jit(solution)/shard_map/ppermute | solution.py:27
  75.1 3.9 %policy_logits.1 = (f32[256,1024]{1,0:T(8,128)S(1)}, f32[256,1024]{1,0:T(8,128)S(1)}) custom-call(s32[2]{0:T(128)S(1)} %pad_add_fusion.flags, bf16[128,1280]{1,0:T(8,128)(2,1)S(1)} %get-tuple-element.34.a, bf16[128,1280]{1,0:T(8,128)(2,1)S(1)} %collective-permute-done.8.a_near, bf16[256,1280]{1,0:T(8,128)(2,1)S(1)} %collective-permute-done.9.a_far, ...), custom_call_target="tpu_custom_call" | custom-call | flops 2684354560 | bytes 9961472 | tf_op jit(solution)/shard_map/policy_logits/pallas_call | solution.py:85
  87.3 4.6 %collective-permute-start.20 = (f32[16,256]{1,0:T(8,128)S(1)}, f32[16,256]{1,0:T(8,128)S(1)}, u32[]{:S(2)}, u32[]{:S(2)}) collective-permute-start(f32[16,256]{1,0:T(8,128)S(1)} %pad_maximum_fusion.13), channel_id=1, source_target_pairs={{0,8},{1,9},{2,10},{3,11},{4,12},{5,13},{6,14},{7,15},{8,0},{9,1},... | collective-permute-start | bytes 49160 | tf_op jit(solution)/shard_map/ppermute | solution.py:27
  94.5 3.4 %collective-permute-done.21 = f32[32,256]{1,0:T(8,128)S(1)} collective-permute-done((f32[32,256]{1,0:T(8,128)S(1)}, f32[32,256]{1,0:T(8,128)S(1)}, u32[]{:S(2)}, u32[]{:S(2)}) %collective-permute-start.21) | collective-permute-done | bytes 32800 | tf_op jit(solution)/shard_map/ppermute | solution.py:27
  98.6 9.3 %all_to_all.5.messages = f32[16,8,256]{2,1,0:T(8,128)S(1)} all-to-all(f32[16,8,256]{2,1,0:T(8,128)S(1)} %broadcast_in_dim.20), channel_id=1, replica_groups=mesh['x'=4,'core'=2,'z'=8,'y'=4] {'x','y'}, dimensions={0} | all-to-all | bytes 262144 | tf_op jit(solution)/shard_map/all_to_all | solution.py:428
  108.4 4.6 %collective-permute-start.22 = (f32[8,256]{1,0:T(8,128)S(1)}, f32[8,256]{1,0:T(8,128)S(1)}, u32[]{:S(2)}, u32[]{:S(2)}) collective-permute-start(f32[8,256]{1,0:T(8,128)S(1)} %result.1), channel_id=1, source_target_pairs={{0,32},{1,33},{2,34},{3,35},{4,36},{5,37},{6,38},{7,39},{8,40},{9,... | collective-permute-start | bytes 24584 | tf_op jit(solution)/shard_map/ppermute | solution.py:27
  113.9 2.7 %gradient_sent.1 = (bf16[256,1280]{1,0:T(8,128)(2,1)S(1)}, bf16[256,1280]{1,0:T(8,128)(2,1)S(1)}, bf16[256,1024]{1,0:T(8,128)(2,1)S(1)}, bf16[256,1024]{1,0:T(8,128)(2,1)S(1)}) custom-call(s32[2]{0:T(128)S(1)} %pad_add_fusion.flags, f32[1,512]{1,0:T(1,128)S(1)} %add_convert_fusion.2.common, f32[8,256]{1,0:T(8,128)S(1)} %result.1, ...), custom_call_target="tpu_custom_call" | custom-call | flops 1342177280 | bytes 9717760 | tf_op jit(solution)/shard_map/gradient_sent/pallas_call | solution.py:85
  119.3 7.1 %collective-permute-done.28 = bf16[256,1280]{1,0:T(8,128)(2,1)S(1)} collective-permute-done((bf16[256,1280]{1,0:T(8,128)(2,1)S(1)}, bf16[256,1280]{1,0:T(8,128)(2,1)S(1)}, u32[]{:S(2)}, u32[]{:S(2)}) %collective-permute-start.28) | collective-permute-done | bytes 655392 | tf_op jit(solution)/shard_map/ppermute | solution.py:27
  128.6 5.2 %collective-permute-done.29 = bf16[128,1280]{1,0:T(8,128)(2,1)S(1)} collective-permute-done((bf16[128,1280]{1,0:T(8,128)(2,1)S(1)}, bf16[128,1280]{1,0:T(8,128)(2,1)S(1)}, u32[]{:S(2)}, u32[]{:S(2)}) %collective-permute-start.29) | collective-permute-done | bytes 327712 | tf_op jit(solution)/shard_map/ppermute | solution.py:27
  135.5 2.9 %collective-permute-done.30 = bf16[64,1280]{1,0:T(8,128)(2,1)S(1)} collective-permute-done((bf16[64,1280]{1,0:T(8,128)(2,1)S(1)}, bf16[64,1280]{1,0:T(8,128)(2,1)S(1)}, u32[]{:S(2)}, u32[]{:S(2)}) %collective-permute-start.30) | collective-permute-done | bytes 163872 | tf_op jit(solution)/shard_map/ppermute | solution.py:27
  146.3 3.7 %collective-permute-done.32 = bf16[16,2560]{1,0:T(8,128)(2,1)S(1)} collective-permute-done((bf16[16,2560]{1,0:T(8,128)(2,1)S(1)}, bf16[16,2560]{1,0:T(8,128)(2,1)S(1)}, u32[]{:S(2)}, u32[]{:S(2)}) %collective-permute-start.32) | collective-permute-done | bytes 81952 | tf_op jit(solution)/shard_map/ppermute | solution.py:27
  150.1 3.0 %collective-permute-start.33 = (bf16[8,2560]{1,0:T(8,128)(2,1)S(1)}, bf16[8,2560]{1,0:T(8,128)(2,1)S(1)}, u32[]{:S(2)}, u32[]{:S(2)}) collective-permute-start(bf16[8,2560]{1,0:T(8,128)(2,1)S(1)} %slice.190), channel_id=1, source_target_pairs={{0,8},{1,9},{2,10},{3,11},{4,12},{5,13},{6,14},{7,15},{8,0},{9,1},... | collective-permute-start | bytes 122888 | tf_op jit(solution)/shard_map/ppermute | solution.py:27
  157.3 8.1 %collective-permute-start.35 = (f32[2,2560]{1,0:T(2,128)S(1)}, f32[2,2560]{1,0:T(2,128)S(1)}, u32[]{:S(2)}, u32[]{:S(2)}) collective-permute-start(f32[2,2560]{1,0:T(2,128)S(1)} %constant_dynamic-slice_fusion.4), channel_id=1, source_target_pairs={{0,32},{1,33},{2,34},{3,35},{4,36},{5,37},{6,38},{7,39},{8,40},{9,... | collective-permute-start | bytes 61448 | tf_op jit(solution)/shard_map/ppermute | solution.py:27
  (122 shorter events, 60.7 us)
Async XLA Ops:
  1.5 6.9 %collective-permute-start = (bf16[2,5120]{1,0:T(2,128)(2,1)S(1)}, bf16[2,5120]{1,0:T(2,128)(2,1)S(1)}, u32[]{:S(2)}, u32[]{:S(2)}) collective-permute-start(bf16[2,5120]{1,0:T(2,128)(2,1)S(1)} %pad_maximum_fusion.11), channel_id=1, source_target_pairs={{0,32},{1,33},{2,34},{3,35},{4,36},{5,37},{6,38},{7,39},{8,40},{9,... | collective-permute-start | bytes 61448 | tf_op jit(solution)/shard_map/ppermute | solution.py:27
  11.6 6.4 %collective-permute-start.2 = (bf16[8,5120]{1,0:T(8,128)(2,1)S(1)}, bf16[8,5120]{1,0:T(8,128)(2,1)S(1)}, u32[]{:S(2)}, u32[]{:S(2)}) collective-permute-start(bf16[8,5120]{1,0:T(8,128)(2,1)S(1)} %pad_maximum_fusion.8), channel_id=1, source_target_pairs={{0,8},{1,9},{2,10},{3,11},{4,12},{5,13},{6,14},{7,15},{8,0},{9,1},... | collective-permute-start | bytes 245768 | tf_op jit(solution)/shard_map/ppermute | solution.py:27
  18.0 7.0 %collective-permute-start.3 = (bf16[16,5120]{1,0:T(8,128)(2,1)S(1)}, bf16[16,5120]{1,0:T(8,128)(2,1)S(1)}, u32[]{:S(2)}, u32[]{:S(2)}) collective-permute-start(bf16[16,5120]{1,0:T(8,128)(2,1)S(1)} %pad_maximum_fusion.7), channel_id=1, source_target_pairs={{0,24},{1,25},{2,26},{3,27},{4,28},{5,29},{6,30},{7,31},{8,16},{9,... | collective-permute-start | bytes 491528 | tf_op jit(solution)/shard_map/ppermute | solution.py:27
  25.0 7.8 %collective-permute-start.6 = (bf16[32,2560]{1,0:T(8,128)(2,1)S(1)}, bf16[32,2560]{1,0:T(8,128)(2,1)S(1)}, u32[]{:S(2)}, u32[]{:S(2)}) collective-permute-start(bf16[32,2560]{1,0:T(8,128)(2,1)S(1)} %get-tuple-element.60.high), channel_id=1, source_target_pairs={{0,1},{1,0},{2,3},{3,2},{4,5},{5,4},{6,7},{7,6},{8,9},{9,8},{10,11... | collective-permute-start | bytes 491528 | tf_op jit(solution)/shard_map/ppermute | solution.py:27
  27.9 36.0 %collective-permute-start.12 = (bf16[2560,512]{1,0:T(8,128)(2,1)S(1)}, bf16[2560,512]{1,0:T(8,128)(2,1)S(1)}, u32[]{:S(2)}, u32[]{:S(2)}) collective-permute-start(bf16[2560,512]{1,0:T(8,128)(2,1)S(1)} %get-tuple-element.37), channel_id=1, source_target_pairs={{0,32},{1,33},{2,34},{3,35},{4,36},{5,37},{6,38},{7,39},{8,40},{9,... | collective-permute-start | bytes 7864328 | tf_op jit(solution)/shard_map/ppermute | solution.py:27
  32.8 6.3 %collective-permute-start.7 = (bf16[64,2560]{1,0:T(8,128)(2,1)S(1)}, bf16[64,2560]{1,0:T(8,128)(2,1)S(1)}, u32[]{:S(2)}, u32[]{:S(2)}) collective-permute-start(bf16[64,2560]{1,0:T(8,128)(2,1)S(1)} %pad_maximum_fusion.5), channel_id=1, source_target_pairs={{0,3},{1,2},{2,1},{3,0},{4,7},{5,6},{6,5},{7,4},{8,11},{9,10},{10,... | collective-permute-start | bytes 983048 | tf_op jit(solution)/shard_map/ppermute | solution.py:27
  35.7 6.3 %collective-permute-start.5 = (bf16[64,2560]{1,0:T(8,128)(2,1)S(1)}, bf16[64,2560]{1,0:T(8,128)(2,1)S(1)}, u32[]{:S(2)}, u32[]{:S(2)}) collective-permute-start(bf16[64,2560]{1,0:T(8,128)(2,1)S(1)} %pad_maximum_fusion.4), channel_id=1, source_target_pairs={{0,192},{1,193},{2,194},{3,195},{4,196},{5,197},{6,198},{7,199},{8... | collective-permute-start | bytes 983048 | tf_op jit(solution)/shard_map/ppermute | solution.py:27
  42.7 7.2 %collective-permute-start.16 = (bf16[128,1280]{1,0:T(8,128)(2,1)S(1)}, bf16[128,1280]{1,0:T(8,128)(2,1)S(1)}, u32[]{:S(2)}, u32[]{:S(2)}) collective-permute-start(bf16[128,1280]{1,0:T(8,128)(2,1)S(1)} %get-tuple-element.42.b), channel_id=1, source_target_pairs={{0,64},{1,65},{2,66},{3,67},{4,68},{5,69},{6,70},{7,71},{8,72},{9,... | collective-permute-start | bytes 983048 | tf_op jit(solution)/shard_map/ppermute | solution.py:27
  45.2 7.1 %collective-permute-start.14 = (bf16[128,1280]{1,0:T(8,128)(2,1)S(1)}, bf16[128,1280]{1,0:T(8,128)(2,1)S(1)}, u32[]{:S(2)}, u32[]{:S(2)}) collective-permute-start(bf16[128,1280]{1,0:T(8,128)(2,1)S(1)} %get-tuple-element.41.a), channel_id=1, source_target_pairs={{0,1},{1,0},{2,3},{3,2},{4,5},{5,4},{6,7},{7,6},{8,9},{9,8},{10,11... | collective-permute-start | bytes 983048 | tf_op jit(solution)/shard_map/ppermute | solution.py:27
  47.2 7.2 %collective-permute-start.10 = (bf16[128,1280]{1,0:T(8,128)(2,1)S(1)}, bf16[128,1280]{1,0:T(8,128)(2,1)S(1)}, u32[]{:S(2)}, u32[]{:S(2)}) collective-permute-start(bf16[128,1280]{1,0:T(8,128)(2,1)S(1)} %get-tuple-element.35.b), channel_id=1, source_target_pairs={{0,64},{1,65},{2,66},{3,67},{4,68},{5,69},{6,70},{7,71},{8,72},{9,... | collective-permute-start | bytes 983048 | tf_op jit(solution)/shard_map/ppermute | solution.py:27
  47.5 8.4 %collective-permute-start.8 = (bf16[128,1280]{1,0:T(8,128)(2,1)S(1)}, bf16[128,1280]{1,0:T(8,128)(2,1)S(1)}, u32[]{:S(2)}, u32[]{:S(2)}) collective-permute-start(bf16[128,1280]{1,0:T(8,128)(2,1)S(1)} %get-tuple-element.34.a), channel_id=1, source_target_pairs={{0,1},{1,0},{2,3},{3,2},{4,5},{5,4},{6,7},{7,6},{8,9},{9,8},{10,11... | collective-permute-start | bytes 983048 | tf_op jit(solution)/shard_map/ppermute | solution.py:27
  50.0 13.6 %collective-permute-start.17 = (bf16[256,1280]{1,0:T(8,128)(2,1)S(1)}, bf16[256,1280]{1,0:T(8,128)(2,1)S(1)}, u32[]{:S(2)}, u32[]{:S(2)}) collective-permute-start(bf16[256,1280]{1,0:T(8,128)(2,1)S(1)} %pad_maximum_fusion.3), channel_id=1, source_target_pairs={{0,192},{1,193},{2,194},{3,195},{4,196},{5,197},{6,198},{7,199},{8... | collective-permute-start | bytes 1966088 | tf_op jit(solution)/shard_map/ppermute | solution.py:27
  52.4 11.5 %collective-permute-start.15 = (bf16[256,1280]{1,0:T(8,128)(2,1)S(1)}, bf16[256,1280]{1,0:T(8,128)(2,1)S(1)}, u32[]{:S(2)}, u32[]{:S(2)}) collective-permute-start(bf16[256,1280]{1,0:T(8,128)(2,1)S(1)} %pad_maximum_fusion.2), channel_id=1, source_target_pairs={{0,3},{1,2},{2,1},{3,0},{4,7},{5,6},{6,5},{7,4},{8,11},{9,10},{10,... | collective-permute-start | bytes 1966088 | tf_op jit(solution)/shard_map/ppermute | solution.py:27
  54.5 20.6 %collective-permute-start.11 = (bf16[256,1280]{1,0:T(8,128)(2,1)S(1)}, bf16[256,1280]{1,0:T(8,128)(2,1)S(1)}, u32[]{:S(2)}, u32[]{:S(2)}) collective-permute-start(bf16[256,1280]{1,0:T(8,128)(2,1)S(1)} %pad_maximum_fusion.1), channel_id=1, source_target_pairs={{0,192},{1,193},{2,194},{3,195},{4,196},{5,197},{6,198},{7,199},{8... | collective-permute-start | bytes 1966088 | tf_op jit(solution)/shard_map/ppermute | solution.py:27
  55.9 19.2 %collective-permute-start.9 = (bf16[256,1280]{1,0:T(8,128)(2,1)S(1)}, bf16[256,1280]{1,0:T(8,128)(2,1)S(1)}, u32[]{:S(2)}, u32[]{:S(2)}) collective-permute-start(bf16[256,1280]{1,0:T(8,128)(2,1)S(1)} %pad_maximum_fusion), channel_id=1, source_target_pairs={{0,3},{1,2},{2,1},{3,0},{4,7},{5,6},{6,5},{7,4},{8,11},{9,10},{10,... | collective-permute-start | bytes 1966088 | tf_op jit(solution)/shard_map/ppermute | solution.py:27
  69.9 10.4 %collective-permute-start.18 = (f32[256,1024]{1,0:T(8,128)S(1)}, f32[256,1024]{1,0:T(8,128)S(1)}, u32[]{:S(2)}, u32[]{:S(2)}) collective-permute-start(f32[256,1024]{1,0:T(8,128)S(1)} %get-tuple-element.44), channel_id=1, source_target_pairs={{0,32},{1,33},{2,34},{3,35},{4,36},{5,37},{6,38},{7,39},{8,40},{9,... | collective-permute-start | bytes 3145736 | tf_op jit(solution)/shard_map/ppermute | solution.py:27
  84.4 29.6 %collective-permute-start.23 = (bf16[2,256,1024]{2,1,0:T(8,128)(2,1)S(1)}, bf16[2,256,1024]{2,1,0:T(8,128)(2,1)S(1)}, u32[]{:S(2)}, u32[]{:S(2)}) collective-permute-start(bf16[2,256,1024]{2,1,0:T(8,128)(2,1)S(1)} %get-tuple-element.47), channel_id=1, source_target_pairs={{0,32},{1,33},{2,34},{3,35},{4,36},{5,37},{6,38},{7,39},{8,40},{9,... | collective-permute-start | bytes 3145736 | tf_op jit(solution)/shard_map/ppermute | solution.py:27
  87.3 5.8 %collective-permute-start.20 = (f32[16,256]{1,0:T(8,128)S(1)}, f32[16,256]{1,0:T(8,128)S(1)}, u32[]{:S(2)}, u32[]{:S(2)}) collective-permute-start(f32[16,256]{1,0:T(8,128)S(1)} %pad_maximum_fusion.13), channel_id=1, source_target_pairs={{0,8},{1,9},{2,10},{3,11},{4,12},{5,13},{6,14},{7,15},{8,0},{9,1},... | collective-permute-start | bytes 49160 | tf_op jit(solution)/shard_map/ppermute | solution.py:27
  116.6 9.8 %collective-permute-start.28 = (bf16[256,1280]{1,0:T(8,128)(2,1)S(1)}, bf16[256,1280]{1,0:T(8,128)(2,1)S(1)}, u32[]{:S(2)}, u32[]{:S(2)}) collective-permute-start(bf16[256,1280]{1,0:T(8,128)(2,1)S(1)} %get-tuple-element.53), channel_id=1, source_target_pairs={{0,192},{1,193},{2,194},{3,195},{4,196},{5,197},{6,198},{7,199},{8... | collective-permute-start | bytes 1966088 | tf_op jit(solution)/shard_map/ppermute | solution.py:27
  116.9 10.7 %collective-permute-start.24 = (bf16[256,1280]{1,0:T(8,128)(2,1)S(1)}, bf16[256,1280]{1,0:T(8,128)(2,1)S(1)}, u32[]{:S(2)}, u32[]{:S(2)}) collective-permute-start(bf16[256,1280]{1,0:T(8,128)(2,1)S(1)} %get-tuple-element.51), channel_id=1, source_target_pairs={{0,3},{1,2},{2,1},{3,0},{4,7},{5,6},{6,5},{7,4},{8,11},{9,10},{10,... | collective-permute-start | bytes 1966088 | tf_op jit(solution)/shard_map/ppermute | solution.py:27
  126.6 7.2 %collective-permute-start.29 = (bf16[128,1280]{1,0:T(8,128)(2,1)S(1)}, bf16[128,1280]{1,0:T(8,128)(2,1)S(1)}, u32[]{:S(2)}, u32[]{:S(2)}) collective-permute-start(bf16[128,1280]{1,0:T(8,128)(2,1)S(1)} %slice.184), channel_id=1, source_target_pairs={{0,64},{1,65},{2,66},{3,67},{4,68},{5,69},{6,70},{7,71},{8,72},{9,... | collective-permute-start | bytes 983048 | tf_op jit(solution)/shard_map/ppermute | solution.py:27
  127.7 7.2 %collective-permute-start.25 = (bf16[128,1280]{1,0:T(8,128)(2,1)S(1)}, bf16[128,1280]{1,0:T(8,128)(2,1)S(1)}, u32[]{:S(2)}, u32[]{:S(2)}) collective-permute-start(bf16[128,1280]{1,0:T(8,128)(2,1)S(1)} %slice.185), channel_id=1, source_target_pairs={{0,1},{1,0},{2,3},{3,2},{4,5},{5,4},{6,7},{7,6},{8,9},{9,8},{10,11... | collective-permute-start | bytes 983048 | tf_op jit(solution)/shard_map/ppermute | solution.py:27
  144.5 5.5 %collective-permute-start.32 = (bf16[16,2560]{1,0:T(8,128)(2,1)S(1)}, bf16[16,2560]{1,0:T(8,128)(2,1)S(1)}, u32[]{:S(2)}, u32[]{:S(2)}) collective-permute-start(bf16[16,2560]{1,0:T(8,128)(2,1)S(1)} %fusion.2), channel_id=1, source_target_pairs={{0,24},{1,25},{2,26},{3,27},{4,28},{5,29},{6,30},{7,31},{8,16},{9,... | collective-permute-start | bytes 245768 | tf_op jit(solution)/shard_map/ppermute | solution.py:27
  157.3 9.0 %collective-permute-start.35 = (f32[2,2560]{1,0:T(2,128)S(1)}, f32[2,2560]{1,0:T(2,128)S(1)}, u32[]{:S(2)}, u32[]{:S(2)}) collective-permute-start(f32[2,2560]{1,0:T(2,128)S(1)} %constant_dynamic-slice_fusion.4), channel_id=1, source_target_pairs={{0,32},{1,33},{2,34},{3,35},{4,36},{5,37},{6,38},{7,39},{8,40},{9,... | collective-permute-start | bytes 61448 | tf_op jit(solution)/shard_map/ppermute | solution.py:27
  (15 other events, 71.9 us)

commit v3 on v2

--- a/solution.py
+++ b/solution.py
@@ -43,7 +43,7 @@
     return (x, 1 - c, z, y)
 
 
-Z_STEPS = (1, 2, 6)
+Z_STEPS = (2, 6, 1)
 
 
 def gray(j):
@@ -51,7 +51,11 @@
 
 
 def z_slot(j):
-    return j ^ ((j >> 2) << 1)
+    return (((j >> 1) ^ (j >> 2)) & 1) | ((j >> 1) & 2) | ((j & 1) << 2)
+
+
+def z_offset(slot):
+    return (slot >> 2) ^ ((slot & 1) * 2) ^ (((slot >> 1) & 1) * 6)
 
 
 def gather_z(rows, steps):
@@ -112,14 +116,12 @@
     return jnp.sum(jnp.where(here == lanes, row, 0.0), axis=1, keepdims=True).astype(jnp.int32)
 
 
-def order_kernel(flags, low, low_near, low_far, high, high_near, high_far, ra, rb, pa, pb):
-    line, width = low.shape
-    part = width // 2
+def order_kernel(flags, low, low_near, low_far, high, high_near, high_far, a, b):
+    line = low.shape[0]
     places = ring_places(flags[0])
-    for rows, near, far, base, policy in ((low, low_near, low_far, ra, pa), (high, high_near, high_far, rb, pb)):
+    for rows, near, far, out in ((low, low_near, low_far, a), (high, high_near, high_far, b)):
         for (piece, start), place in zip(((rows, 0), (near, 0), (far, 0), (far, line)), places):
-            policy[rows_at(place, line), :] = piece[start : start + line, :part]
-            base[rows_at(place, line), :] = piece[start : start + line, part:]
+            out[rows_at(place, line), :] = piece[start : start + line, :]
 
 
 def take_head(flags, head, keep, send, keep_done, send_done):
@@ -165,7 +167,7 @@
     first = pl.program_id(0) * count
 
     def pick(place, rows, near, far):
-        ring = rows.shape[0]
+        ring, part = far.shape[0] // 2, far.shape[1]
         lanes = lax.broadcasted_iota(jnp.int32, (count, 4 * ring), 1)
         one_hot = jnp.where(as_column(place[...], first, count) == lanes, 1.0, 0.0).astype(BF16)
         total = jnp.dot(one_hot[:, :ring], rows[...], preferred_element_type=F32)
@@ -174,13 +176,13 @@
         return total.astype(BF16)
 
     x = (pick(low_place, a, a_near, a_far), pick(high_place, b, b_near, b_far))
-    own, other = two_products(x, a.shape[1], head_keep, head_got)
+    own, other = two_products(x, a_far.shape[1], head_keep, head_got)
     store_halves(own, other, keep, send)
 
 
 def policy_kernel(line, flags, a, a_near, a_far, b, b_near, b_far, head_keep, head_got, keep, send, rows):
     step = pl.program_id(0)
-    ring, part = a.shape
+    ring, part = a.shape[0], a_far.shape[1]
     mine = keep.shape[0]
 
     @pl.when(step == 0)
@@ -193,7 +195,9 @@
         high = ((b, 0), (b_near, 0), (b_far, 0), (b_far, ring))
         for (piece, start), place in zip(high, places):
             for y in range(Y):
-                rows[rows_at((y ^ flip) * X + place, line), part:] = piece[start + y * line : start + (y + 1) * line, :]
+                rows[rows_at((y ^ flip) * X + place, line), part:] = piece[
+                    start + y * line : start + (y + 1) * line, :part
+                ]
 
     x = rows[rows_at(step, mine), :]
     own, other = two_products((x[:, :part], x[:, part:]), part, head_keep, head_got)
@@ -268,7 +272,7 @@
 
 
 def sent_kernel(
-    line, flags, common, result, result_got, parts, parts_got, head_keep, head_got, low, high, low_rows, high_rows, by_y, by_x
+    line, flags, common, result, result_got, parts, parts_got, head_keep, head_got, low, by_y, by_x
 ):
     mine = result.shape[1]
     core, flip = flags[0], 2 * flags[1]
@@ -289,9 +293,10 @@
             by_y[rows_at(y * X + x, line), :] = piece
             by_x[rows_at(x * Y + y, line), :] = piece
     low[...] = gradient(by_y[mine:, :], head_keep, head_got, 0).astype(BF16)
-    high[...] = gradient(by_x[mine:, :], head_keep, head_got, 1).astype(BF16)
-    low_rows[...] = by_y[:mine, :]
-    high_rows[...] = by_x[:mine, :]
+
+
+def high_kernel(flags, by_x, head_keep, head_got, high):
+    high[...] = gradient(by_x[high.shape[0] :, :], head_keep, head_got, 1).astype(BF16)
 
 
 def gradient(rows, head_keep, head_got, which):
@@ -303,9 +308,10 @@
     ) + lax.dot_general(rows[:, columns:], head_got[span, :], CONTRACT_LAST, preferred_element_type=F32)
 
 
-def kept_kernel(flags, low_rows, high_rows, head_keep, head_got, low, high):
-    low[...] = gradient(low_rows[...], head_keep, head_got, 0)
-    high[...] = gradient(high_rows[...], head_keep, head_got, 1)
+def kept_kernel(flags, by_y, by_x, head_keep, head_got, low, high):
+    mine = low.shape[0]
+    low[...] = gradient(by_y[:mine, :], head_keep, head_got, 0)
+    high[...] = gradient(by_x[:mine, :], head_keep, head_got, 1)
 
 
 def on_device(policy_hidden, reference_hidden, head_weight, pair_map, response_mask):
@@ -333,6 +339,21 @@
     rows, head_weight = lax.optimization_barrier((rows, head_weight))
     flags = jnp.stack([c0, c0 ^ (y0 >> 1)]).astype(jnp.int32)
     head_shape = jax.ShapeDtypeStruct((half, columns), BF16)
+    slot = jnp.arange(tokens, dtype=jnp.int32)[None]
+
+    def raw(j):
+        return jnp.where(second, jnp.where(j == 0, 0, jnp.where(j == 3, 1, j + 1)), gray(j))
+
+    sr, sc = slot % own_rows, (slot // own_rows) % CORES
+    sz = z_offset((slot // chip_rows) % Z) ^ z0
+    sx = gray((slot // line) % X) ^ x0
+    sy = gray((slot // ring) ^ jnp.where(swapped, 2, 0)) ^ y0
+    own_token = flat(sx, sc, sz, sy) * own_rows + sr
+    rows = gather_z(rows, Z_STEPS[:1])
+    rows, own_token = lax.optimization_barrier((rows, own_token))
+    partner = jnp.take(pair_map, own_token, axis=0)
+    rows = gather_z(rows, Z_STEPS[1:2])
+    rows, partner, head_weight = lax.optimization_barrier((rows, partner, head_weight))
     head_keep, head_send = run(
         take_head,
         "take_head",
@@ -342,22 +363,9 @@
         in_specs=[pl.BlockSpec(memory_space=pltpu.HBM)],
         scratch=[pltpu.SemaphoreType.DMA] * 2,
     )
-    slot = jnp.arange(tokens, dtype=jnp.int32)[None]
-
-    def raw(j):
-        return jnp.where(second, jnp.where(j == 0, 0, jnp.where(j == 3, 1, j + 1)), gray(j))
-
-    sr, sc = slot % own_rows, (slot // own_rows) % CORES
-    sz = z_slot((slot // chip_rows) % Z) ^ z0
-    sx = gray((slot // line) % X) ^ x0
-    sy = gray((slot // ring) ^ jnp.where(swapped, 2, 0)) ^ y0
-    partner = jnp.take(pair_map, flat(sx, sc, sz, sy) * own_rows + sr, axis=0)
-    rows = gather_z(rows, Z_STEPS[:1])
-    rows, partner = lax.optimization_barrier((rows, partner))
-    rows = gather_z(rows, Z_STEPS[1:2])
+    rows = gather_z(rows, Z_STEPS[2:])
     rows, head_keep, head_send = lax.optimization_barrier((rows, head_keep, head_send))
     head = (head_keep, exchange(head_send, across_cores))
-    rows = gather_z(rows, Z_STEPS[2:])
     pr, pdev = partner % own_rows, partner // own_rows
     py, pz, pc, px = pdev % Y, (pdev // Y) % Z, (pdev // (Y * Z)) % CORES, pdev // (Y * Z * CORES)
     tail = (z_slot(pz ^ z0) * CORES + pc) * own_rows + pr
@@ -365,26 +373,25 @@
     high_place = ((raw(px ^ x0) * Y + gray(py ^ y0)) * line + tail).astype(F32)
     common = (((sy * X + sx) * Z + sz) * chip_rows + sc * own_rows + sr).astype(F32)
 
-    low, high = rows[:, :half], rows[:, half:]
-    low_near, high_near = ring_near(low, along_x), ring_near(high, along_y)
-    low_far, high_far = ring_far(low, low_near, along_x), ring_far(high, high_near, along_y)
-    block = jax.ShapeDtypeStruct((ring, part), BF16)
-    ra, rb, pa, pb = run(
-        order_kernel,
-        "order",
-        flags,
-        (low, low_near, low_far, high, high_near, high_far),
-        [block] * 4,
-    )
-
-    ra_near, rb_near = ring_near(ra, along_y), ring_near(rb, along_x)
-    pa_near, pb_near = ring_near(pa, along_y), ring_near(pb, along_x)
-    ra_far, rb_far = ring_far(ra, ra_near, along_y), ring_far(rb, rb_near, along_x)
-    pa_far, pb_far = ring_far(pa, pa_near, along_y), ring_far(pb, pb_near, along_x)
+    spans = [(rows[:, part:half], rows[:, half + part :]), (rows[:, :part], rows[:, half : half + part])]
+    gathered = []
+    for low, high in spans:
+        low_near, high_near = ring_near(low, along_x), ring_near(high, along_y)
+        low_far, high_far = ring_far(low, low_near, along_x), ring_far(high, high_near, along_y)
+        a, b = run(
+            order_kernel,
+            "order",
+            flags,
+            (low, low_near, low_far, high, high_near, high_far),
+            [jax.ShapeDtypeStruct((ring, part), BF16)] * 2,
+        )
+        a_near, b_near = ring_near(a, along_y), ring_near(b, along_x)
+        a_far, b_far = ring_far(a, a_near, along_y), ring_far(b, b_near, along_x)
+        gathered.append((a, a_near, a_far, b, b_near, b_far))
+    base, policy = gathered
 
     logits = [jax.ShapeDtypeStruct((mine, 2 * columns), F32)] * 2
     flops = 4 * tokens * half * columns
-    base = (ra, ra_near, ra_far, rb, rb_near, rb_far)
     base_keep, base_send = run(
         base_kernel,
         "base_logits",
@@ -395,7 +402,6 @@
         flops=2 * flops,
     )
     base_got = exchange(base_send, across_cores)
-    policy = (pa, pa_near, pa_far, pb, pb_near, pb_far)
     policy_keep, policy_send = run(
         functools.partial(policy_kernel, line),
         "policy_logits",
@@ -429,27 +435,22 @@
     (result,) = run(result_kernel, "result", flags, (everyone, message), [message_shape])
     result_got = exchange(result, across_cores)
 
-    rows_shape = jax.ShapeDtypeStruct((mine, 2 * columns), BF16)
+    rows_shape = jax.ShapeDtypeStruct((tokens, 2 * columns), BF16)
     sent_shape = jax.ShapeDtypeStruct((mine, part), BF16)
     kept_shape = jax.ShapeDtypeStruct((mine, part), F32)
-    operands = (common, result, result_got, parts, parts_got)
-    low_sent, high_sent, low_rows, high_rows = run(
+    low_sent, by_y, by_x = run(
         functools.partial(sent_kernel, line),
-        "gradient_sent",
+        "gradient_sent_low",
         flags,
-        (*operands, *head),
-        [sent_shape, sent_shape, rows_shape, rows_shape],
-        scratch=[pltpu.VMEM((tokens, 2 * columns), BF16)] * 2,
-        flops=flops // 2,
-    )
-    low_got, high_got = exchange(low_sent, along_y(3, 1)), exchange(high_sent, along_x(3, 1))
+        (common, result, result_got, parts, parts_got, *head),
+        [sent_shape, rows_shape, rows_shape],
+        flops=flops // 4,
+    )
+    low_got = exchange(low_sent, along_y(3, 1))
+    (high_sent,) = run(high_kernel, "gradient_sent_high", flags, (by_x, *head), [sent_shape], flops=flops // 4)
+    high_got = exchange(high_sent, along_x(3, 1))
     low_kept, high_kept = run(
-        kept_kernel,
-        "gradient_kept",
-        flags,
-        (low_rows, high_rows, *head),
-        [kept_shape, kept_shape],
-        flops=flops // 2,
+        kept_kernel, "gradient_kept", flags, (by_y, by_x, *head), [kept_shape, kept_shape], flops=flops // 2
     )
     low_total = low_kept + low_got.astype(F32)
     high_total = high_kept + high_got.astype(F32)

time: 167 us -> 164 us (0.982)
  waiting for transfers between devices: 67.3 us -> 54.8 us
  starting transfers between devices: 60.5 us -> 65.8 us
  blocking collectives: 9.25 us -> 12.1 us
    ppermute x36 -> x40, waiting for transfers between devices: 67.3 us -> 54.8 us  [exchange(): return lax.ppermute(value, AXES, pairs)]
    ppermute x36 -> x40, starting transfers between devices: 60.5 us -> 65.8 us  [exchange(): return lax.ppermute(value, AXES, pairs)]
    all_to_all x1, blocking collectives: 9.25 us -> 12.1 us  [on_device(): lax.all_to_all(jnp.broadcast_to(line_message[None], (X * Y, 8, mine)), ('...]
    pallas_call x9 -> x11, Pallas kernels: 19.3 us -> 20.5 us  [run(): pl.pallas_call(kernel, out_shape=outputs, grid_spec=pltpu.PrefetchScalarG...]
  transfers between devices with their start and end apart: 36 -> 40, of which waited for: 27 -> 25; matrix products, arithmetic and copies ran while one was open for 3% -> 3% of each run, Pallas kernels for 9% -> 9%
where the time goes in v3:
time: 164 us
  starting transfers between devices  65.8 us (40%)
  waiting for transfers between devices  54.8 us (33%)
  Pallas kernels  20.5 us (12%)
  blocking collectives  12.1 us (7%)
  local copies, waits for them, and re-layouts  7.05 us (4%)
  other arithmetic  2.52 us (2%)
    ppermute x40, starting transfers between devices, exchange(): return lax.ppermute(value, AXES, pairs)  65.8 us
    ppermute x40, waiting for transfers between devices, exchange(): return lax.ppermute(value, AXES, pairs)  54.8 us
    pallas_call x11, Pallas kernels, run(): pl.pallas_call(kernel, out_shape=outputs, grid_spec=pltpu.PrefetchScalarG...  20.5 us
    all_to_all x1, blocking collectives, on_device(): lax.all_to_all(jnp.broadcast_to(line_message[None], (X * Y, 8, mine)), ('...  12.1 us
    gather x1, local copies, waits for them, and re-layouts, on_device(): partner = jnp.take(pair_map, own_token, axis=0)  3.48 us
  transfers between devices with their start and end apart: 40, of which 25 were waited for; matrix products, arithmetic and copies ran while one was open for 3% of the time, Pallas kernels for 9%

profile of v3, /device:TPU:1, one launch (start us, length us, event | category | flops | bytes accessed | tf_op | source)
XLA Modules:
  0.0 163.9 jit_solution(3667072280100639369)
XLA Ops:
  1.5 3.3 %collective-permute-start = (bf16[2,5120]{1,0:T(2,128)(2,1)S(1)}, bf16[2,5120]{1,0:T(2,128)(2,1)S(1)}, u32[]{:S(2)}, u32[]{:S(2)}) collective-permute-start(bf16[2,5120]{1,0:T(2,128)(2,1)S(1)} %pad_maximum_fusion.14), channel_id=1, source_target_pairs={{0,32},{1,33},{2,34},{3,35},{4,36},{5,37},{6,38},{7,39},{8,40},{9,... | collective-permute-start | bytes 61448 | tf_op jit(solution)/shard_map/ppermute | solution.py:27
  7.2 3.7 %collective-permute-done.1 = bf16[4,5120]{1,0:T(4,128)(2,1)S(1)} collective-permute-done((bf16[4,5120]{1,0:T(4,128)(2,1)S(1)}, bf16[4,5120]{1,0:T(4,128)(2,1)S(1)}, u32[]{:S(2)}, u32[]{:S(2)}) %collective-permute-start.1) | collective-permute-done | bytes 40992 | tf_op jit(solution)/shard_map/ppermute | solution.py:27
  11.0 3.1 %collective-permute-start.2 = (bf16[8,5120]{1,0:T(8,128)(2,1)S(1)}, bf16[8,5120]{1,0:T(8,128)(2,1)S(1)}, u32[]{:S(2)}, u32[]{:S(2)}) collective-permute-start(bf16[8,5120]{1,0:T(8,128)(2,1)S(1)} %pad_maximum_fusion.11), channel_id=1, source_target_pairs={{0,24},{1,25},{2,26},{3,27},{4,28},{5,29},{6,30},{7,31},{8,16},{9,... | collective-permute-start | bytes 245768 | tf_op jit(solution)/shard_map/ppermute | solution.py:27
  14.1 3.5 %gather_fusion = s32[512]{0:T(512)S(1)} fusion(s32[512]{0:T(512)S(1)} %copy-done, s32[1024]{0:T(1024)S(1)} %pad_clamp_fusion), kind=kCustom, calls=%fused_computation | custom fusion | bytes 6144 | tf_op jit(solution)/shard_map/jit(_take)/gather | solution.py:354
  18.6 2.5 %copy-done.1 = bf16[5120,512]{1,0:T(8,128)(2,1)S(1)} copy-done((bf16[5120,512]{1,0:T(8,128)(2,1)S(1)}, bf16[5120,512]{1,0:T(8,128)(2,1)}, u32[]{:S(2)}) %copy-start.1) | copy-done | bytes 5242904
  22.0 2.9 %collective-permute-start.12 = (bf16[2560,512]{1,0:T(8,128)(2,1)S(1)}, bf16[2560,512]{1,0:T(8,128)(2,1)S(1)}, u32[]{:S(2)}, u32[]{:S(2)}) collective-permute-start(bf16[2560,512]{1,0:T(8,128)(2,1)S(1)} %get-tuple-element.42), channel_id=1, source_target_pairs={{0,32},{1,33},{2,34},{3,35},{4,36},{5,37},{6,38},{7,39},{8,40},{9,... | collective-permute-start | bytes 7864328 | tf_op jit(solution)/shard_map/ppermute | solution.py:27
  25.0 2.6 %collective-permute-start.14 = (bf16[32,1280]{1,0:T(8,128)(2,1)S(1)}, bf16[32,1280]{1,0:T(8,128)(2,1)S(1)}, u32[]{:S(2)}, u32[]{:S(2)}) collective-permute-start(bf16[32,1280]{1,0:T(8,128)(2,1)S(1)} %get-tuple-element.65.low), channel_id=1, source_target_pairs={{0,64},{1,65},{2,66},{3,67},{4,68},{5,69},{6,70},{7,71},{8,72},{9,... | collective-permute-start | bytes 245768 | tf_op jit(solution)/shard_map/ppermute | solution.py:27
  27.5 2.7 %collective-permute-start.16 = (bf16[32,1280]{1,0:T(8,128)(2,1)S(1)}, bf16[32,1280]{1,0:T(8,128)(2,1)S(1)}, u32[]{:S(2)}, u32[]{:S(2)}) collective-permute-start(bf16[32,1280]{1,0:T(8,128)(2,1)S(1)} %get-tuple-element.64.high), channel_id=1, source_target_pairs={{0,1},{1,0},{2,3},{3,2},{4,5},{5,4},{6,7},{7,6},{8,9},{9,8},{10,11... | collective-permute-start | bytes 245768 | tf_op jit(solution)/shard_map/ppermute | solution.py:27
  32.5 2.5 %collective-permute-done.6.high_near = bf16[32,1280]{1,0:T(8,128)(2,1)S(1)} collective-permute-done((bf16[32,1280]{1,0:T(8,128)(2,1)S(1)}, bf16[32,1280]{1,0:T(8,128)(2,1)S(1)}, u32[]{:S(2)}, u32[]{:S(2)}) %collective-permute-start.6) | collective-permute-done | bytes 81952 | tf_op jit(solution)/shard_map/ppermute | solution.py:27
  39.3 2.6 %collective-permute-start.18 = (bf16[128,1280]{1,0:T(8,128)(2,1)S(1)}, bf16[128,1280]{1,0:T(8,128)(2,1)S(1)}, u32[]{:S(2)}, u32[]{:S(2)}) collective-permute-start(bf16[128,1280]{1,0:T(8,128)(2,1)S(1)} %get-tuple-element.46.a), channel_id=1, source_target_pairs={{0,1},{1,0},{2,3},{3,2},{4,5},{5,4},{6,7},{7,6},{8,9},{9,8},{10,11... | collective-permute-start | bytes 983048 | tf_op jit(solution)/shard_map/ppermute | solution.py:27
  43.2 3.3 %collective-permute-start.10 = (bf16[128,1280]{1,0:T(8,128)(2,1)S(1)}, bf16[128,1280]{1,0:T(8,128)(2,1)S(1)}, u32[]{:S(2)}, u32[]{:S(2)}) collective-permute-start(bf16[128,1280]{1,0:T(8,128)(2,1)S(1)} %get-tuple-element.40.b), channel_id=1, source_target_pairs={{0,64},{1,65},{2,66},{3,67},{4,68},{5,69},{6,70},{7,71},{8,72},{9,... | collective-permute-start | bytes 983048 | tf_op jit(solution)/shard_map/ppermute | solution.py:27
  46.6 2.7 %collective-permute-start.8 = (bf16[128,1280]{1,0:T(8,128)(2,1)S(1)}, bf16[128,1280]{1,0:T(8,128)(2,1)S(1)}, u32[]{:S(2)}, u32[]{:S(2)}) collective-permute-start(bf16[128,1280]{1,0:T(8,128)(2,1)S(1)} %get-tuple-element.39.a), channel_id=1, source_target_pairs={{0,1},{1,0},{2,3},{3,2},{4,5},{5,4},{6,7},{7,6},{8,9},{9,8},{10,11... | collective-permute-start | bytes 983048 | tf_op jit(solution)/shard_map/ppermute | solution.py:27
  54.2 7.1 %collective-permute-done.21.b_far = bf16[256,1280]{1,0:T(8,128)(2,1)S(1)} collective-permute-done((bf16[256,1280]{1,0:T(8,128)(2,1)S(1)}, bf16[256,1280]{1,0:T(8,128)(2,1)S(1)}, u32[]{:S(2)}, u32[]{:S(2)}) %collective-permute-start.21) | collective-permute-done | bytes 655392 | tf_op jit(solution)/shard_map/ppermute | solution.py:27
  61.5 6.0 %base_logits.1 = (f32[256,1024]{1,0:T(8,128)S(1)}, f32[256,1024]{1,0:T(8,128)S(1)}) custom-call(s32[2]{0:T(128)S(1)} %pad_add_fusion.flags, f32[1,512]{1,0:T(1,128)S(1)} %add_convert_fusion.1.low_place, f32[1,512]{1,0:T(1,128)S(1)} %get-tuple-element.58.high_place, bf16[128,1280]{1,0:T(8,128)(2,1)S(1)} %get-tuple-element.46.a, ...), custom_call_target="tpu_custom_call" | custom-call | flops 5368709120 | bytes 9965568 | tf_op jit(solution)/shard_map/base_logits/pallas_call | solution.py:89
  69.2 3.9 %policy_logits.1 = (f32[256,1024]{1,0:T(8,128)S(1)}, f32[256,1024]{1,0:T(8,128)S(1)}) custom-call(s32[2]{0:T(128)S(1)} %pad_add_fusion.flags, bf16[128,1280]{1,0:T(8,128)(2,1)S(1)} %get-tuple-element.39.a, bf16[128,1280]{1,0:T(8,128)(2,1)S(1)} %collective-permute-done.8.a_near, bf16[256,1280]{1,0:T(8,128)(2,1)S(1)} %collective-permute-done.9.a_far, ...), custom_call_target="tpu_custom_call" | custom-call | flops 2684354560 | bytes 9961472 | tf_op jit(solution)/shard_map/policy_logits/pallas_call | solution.py:89
  73.2 2.5 %collective-permute-start.13 = (f32[256,1024]{1,0:T(8,128)S(1)}, f32[256,1024]{1,0:T(8,128)S(1)}, u32[]{:S(2)}, u32[]{:S(2)}) collective-permute-start(f32[256,1024]{1,0:T(8,128)S(1)} %get-tuple-element.44), channel_id=1, source_target_pairs={{0,32},{1,33},{2,34},{3,35},{4,36},{5,37},{6,38},{7,39},{8,40},{9,... | collective-permute-start | bytes 3145736 | tf_op jit(solution)/shard_map/ppermute | solution.py:27
  83.6 2.7 %collective-permute-start.24 = (f32[16,256]{1,0:T(8,128)S(1)}, f32[16,256]{1,0:T(8,128)S(1)}, u32[]{:S(2)}, u32[]{:S(2)}) collective-permute-start(f32[16,256]{1,0:T(8,128)S(1)} %pad_maximum_fusion.16), channel_id=1, source_target_pairs={{0,24},{1,25},{2,26},{3,27},{4,28},{5,29},{6,30},{7,31},{8,16},{9,... | collective-permute-start | bytes 49160 | tf_op jit(solution)/shard_map/ppermute | solution.py:27
  91.7 12.1 %all_to_all.5.messages = f32[16,8,256]{2,1,0:T(8,128)S(1)} all-to-all(f32[16,8,256]{2,1,0:T(8,128)S(1)} %broadcast_in_dim.23), channel_id=1, replica_groups=mesh['x'=4,'core'=2,'z'=8,'y'=4] {'x','y'}, dimensions={0} | all-to-all | bytes 262144 | tf_op jit(solution)/shard_map/all_to_all | solution.py:434
  104.4 5.1 %collective-permute-start.26 = (f32[8,256]{1,0:T(8,128)S(1)}, f32[8,256]{1,0:T(8,128)S(1)}, u32[]{:S(2)}, u32[]{:S(2)}) collective-permute-start(f32[8,256]{1,0:T(8,128)S(1)} %result.1), channel_id=1, source_target_pairs={{0,32},{1,33},{2,34},{3,35},{4,36},{5,37},{6,38},{7,39},{8,40},{9,... | collective-permute-start | bytes 24584 | tf_op jit(solution)/shard_map/ppermute | solution.py:27
  116.4 7.1 %collective-permute-done.32 = bf16[256,1280]{1,0:T(8,128)(2,1)S(1)} collective-permute-done((bf16[256,1280]{1,0:T(8,128)(2,1)S(1)}, bf16[256,1280]{1,0:T(8,128)(2,1)S(1)}, u32[]{:S(2)}, u32[]{:S(2)}) %collective-permute-start.32) | collective-permute-done | bytes 655392 | tf_op jit(solution)/shard_map/ppermute | solution.py:27
  125.7 5.2 %collective-permute-done.33 = bf16[128,1280]{1,0:T(8,128)(2,1)S(1)} collective-permute-done((bf16[128,1280]{1,0:T(8,128)(2,1)S(1)}, bf16[128,1280]{1,0:T(8,128)(2,1)S(1)}, u32[]{:S(2)}, u32[]{:S(2)}) %collective-permute-start.33) | collective-permute-done | bytes 327712 | tf_op jit(solution)/shard_map/ppermute | solution.py:27
  132.6 2.9 %collective-permute-done.34 = bf16[64,1280]{1,0:T(8,128)(2,1)S(1)} collective-permute-done((bf16[64,1280]{1,0:T(8,128)(2,1)S(1)}, bf16[64,1280]{1,0:T(8,128)(2,1)S(1)}, u32[]{:S(2)}, u32[]{:S(2)}) %collective-permute-start.34) | collective-permute-done | bytes 163872 | tf_op jit(solution)/shard_map/ppermute | solution.py:27
  145.4 2.8 %collective-permute-start.37 = (bf16[8,2560]{1,0:T(8,128)(2,1)S(1)}, bf16[8,2560]{1,0:T(8,128)(2,1)S(1)}, u32[]{:S(2)}, u32[]{:S(2)}) collective-permute-start(bf16[8,2560]{1,0:T(8,128)(2,1)S(1)} %slice.196), channel_id=1, source_target_pairs={{0,24},{1,25},{2,26},{3,27},{4,28},{5,29},{6,30},{7,31},{8,16},{9,... | collective-permute-start | bytes 122888 | tf_op jit(solution)/shard_map/ppermute | solution.py:27
  154.2 8.2 %collective-permute-start.39 = (f32[2,2560]{1,0:T(2,128)S(1)}, f32[2,2560]{1,0:T(2,128)S(1)}, u32[]{:S(2)}, u32[]{:S(2)}) collective-permute-start(f32[2,2560]{1,0:T(2,128)S(1)} %constant_dynamic-slice_fusion.4), channel_id=1, source_target_pairs={{0,32},{1,33},{2,34},{3,35},{4,36},{5,37},{6,38},{7,39},{8,40},{9,... | collective-permute-start | bytes 61448 | tf_op jit(solution)/shard_map/ppermute | solution.py:27
  (134 shorter events, 61.5 us)
Async XLA Ops:
  5.8 5.1 %collective-permute-start.1 = (bf16[4,5120]{1,0:T(4,128)(2,1)S(1)}, bf16[4,5120]{1,0:T(4,128)(2,1)S(1)}, u32[]{:S(2)}, u32[]{:S(2)}) collective-permute-start(bf16[4,5120]{1,0:T(4,128)(2,1)S(1)} %pad_maximum_fusion.12), channel_id=1, source_target_pairs={{0,8},{1,9},{2,10},{3,11},{4,12},{5,13},{6,14},{7,15},{8,0},{9,1},... | collective-permute-start | bytes 122888 | tf_op jit(solution)/shard_map/ppermute | solution.py:27
  11.0 6.6 %collective-permute-start.2 = (bf16[8,5120]{1,0:T(8,128)(2,1)S(1)}, bf16[8,5120]{1,0:T(8,128)(2,1)S(1)}, u32[]{:S(2)}, u32[]{:S(2)}) collective-permute-start(bf16[8,5120]{1,0:T(8,128)(2,1)S(1)} %pad_maximum_fusion.11), channel_id=1, source_target_pairs={{0,24},{1,25},{2,26},{3,27},{4,28},{5,29},{6,30},{7,31},{8,16},{9,... | collective-permute-start | bytes 245768 | tf_op jit(solution)/shard_map/ppermute | solution.py:27
  22.0 39.5 %collective-permute-start.12 = (bf16[2560,512]{1,0:T(8,128)(2,1)S(1)}, bf16[2560,512]{1,0:T(8,128)(2,1)S(1)}, u32[]{:S(2)}, u32[]{:S(2)}) collective-permute-start(bf16[2560,512]{1,0:T(8,128)(2,1)S(1)} %get-tuple-element.42), channel_id=1, source_target_pairs={{0,32},{1,33},{2,34},{3,35},{4,36},{5,37},{6,38},{7,39},{8,40},{9,... | collective-permute-start | bytes 7864328 | tf_op jit(solution)/shard_map/ppermute | solution.py:27
  25.0 5.5 %collective-permute-start.14 = (bf16[32,1280]{1,0:T(8,128)(2,1)S(1)}, bf16[32,1280]{1,0:T(8,128)(2,1)S(1)}, u32[]{:S(2)}, u32[]{:S(2)}) collective-permute-start(bf16[32,1280]{1,0:T(8,128)(2,1)S(1)} %get-tuple-element.65.low), channel_id=1, source_target_pairs={{0,64},{1,65},{2,66},{3,67},{4,68},{5,69},{6,70},{7,71},{8,72},{9,... | collective-permute-start | bytes 245768 | tf_op jit(solution)/shard_map/ppermute | solution.py:27
  30.3 8.1 %collective-permute-start.4 = (bf16[32,1280]{1,0:T(8,128)(2,1)S(1)}, bf16[32,1280]{1,0:T(8,128)(2,1)S(1)}, u32[]{:S(2)}, u32[]{:S(2)}) collective-permute-start(bf16[32,1280]{1,0:T(8,128)(2,1)S(1)} %get-tuple-element.67.low), channel_id=1, source_target_pairs={{0,64},{1,65},{2,66},{3,67},{4,68},{5,69},{6,70},{7,71},{8,72},{9,... | collective-permute-start | bytes 245768 | tf_op jit(solution)/shard_map/ppermute | solution.py:27
  35.1 6.9 %collective-permute-start.7 = (bf16[64,1280]{1,0:T(8,128)(2,1)S(1)}, bf16[64,1280]{1,0:T(8,128)(2,1)S(1)}, u32[]{:S(2)}, u32[]{:S(2)}) collective-permute-start(bf16[64,1280]{1,0:T(8,128)(2,1)S(1)} %pad_maximum_fusion.8), channel_id=1, source_target_pairs={{0,3},{1,2},{2,1},{3,0},{4,7},{5,6},{6,5},{7,4},{8,11},{9,10},{10,... | collective-permute-start | bytes 491528 | tf_op jit(solution)/shard_map/ppermute | solution.py:27
  37.2 12.0 %collective-permute-start.20 = (bf16[128,1280]{1,0:T(8,128)(2,1)S(1)}, bf16[128,1280]{1,0:T(8,128)(2,1)S(1)}, u32[]{:S(2)}, u32[]{:S(2)}) collective-permute-start(bf16[128,1280]{1,0:T(8,128)(2,1)S(1)} %get-tuple-element.47.b), channel_id=1, source_target_pairs={{0,64},{1,65},{2,66},{3,67},{4,68},{5,69},{6,70},{7,71},{8,72},{9,... | collective-permute-start | bytes 983048 | tf_op jit(solution)/shard_map/ppermute | solution.py:27
  39.3 10.1 %collective-permute-start.18 = (bf16[128,1280]{1,0:T(8,128)(2,1)S(1)}, bf16[128,1280]{1,0:T(8,128)(2,1)S(1)}, u32[]{:S(2)}, u32[]{:S(2)}) collective-permute-start(bf16[128,1280]{1,0:T(8,128)(2,1)S(1)} %get-tuple-element.46.a), channel_id=1, source_target_pairs={{0,1},{1,0},{2,3},{3,2},{4,5},{5,4},{6,7},{7,6},{8,9},{9,8},{10,11... | collective-permute-start | bytes 983048 | tf_op jit(solution)/shard_map/ppermute | solution.py:27
  43.2 7.8 %collective-permute-start.10 = (bf16[128,1280]{1,0:T(8,128)(2,1)S(1)}, bf16[128,1280]{1,0:T(8,128)(2,1)S(1)}, u32[]{:S(2)}, u32[]{:S(2)}) collective-permute-start(bf16[128,1280]{1,0:T(8,128)(2,1)S(1)} %get-tuple-element.40.b), channel_id=1, source_target_pairs={{0,64},{1,65},{2,66},{3,67},{4,68},{5,69},{6,70},{7,71},{8,72},{9,... | collective-permute-start | bytes 983048 | tf_op jit(solution)/shard_map/ppermute | solution.py:27
  46.6 7.4 %collective-permute-start.8 = (bf16[128,1280]{1,0:T(8,128)(2,1)S(1)}, bf16[128,1280]{1,0:T(8,128)(2,1)S(1)}, u32[]{:S(2)}, u32[]{:S(2)}) collective-permute-start(bf16[128,1280]{1,0:T(8,128)(2,1)S(1)} %get-tuple-element.39.a), channel_id=1, source_target_pairs={{0,1},{1,0},{2,3},{3,2},{4,5},{5,4},{6,7},{7,6},{8,9},{9,8},{10,11... | collective-permute-start | bytes 983048 | tf_op jit(solution)/shard_map/ppermute | solution.py:27
  49.3 12.0 %collective-permute-start.21 = (bf16[256,1280]{1,0:T(8,128)(2,1)S(1)}, bf16[256,1280]{1,0:T(8,128)(2,1)S(1)}, u32[]{:S(2)}, u32[]{:S(2)}) collective-permute-start(bf16[256,1280]{1,0:T(8,128)(2,1)S(1)} %pad_maximum_fusion.3), channel_id=1, source_target_pairs={{0,192},{1,193},{2,194},{3,195},{4,196},{5,197},{6,198},{7,199},{8... | collective-permute-start | bytes 1966088 | tf_op jit(solution)/shard_map/ppermute | solution.py:27
  49.5 12.1 %collective-permute-start.19 = (bf16[256,1280]{1,0:T(8,128)(2,1)S(1)}, bf16[256,1280]{1,0:T(8,128)(2,1)S(1)}, u32[]{:S(2)}, u32[]{:S(2)}) collective-permute-start(bf16[256,1280]{1,0:T(8,128)(2,1)S(1)} %pad_maximum_fusion.2), channel_id=1, source_target_pairs={{0,3},{1,2},{2,1},{3,0},{4,7},{5,6},{6,5},{7,4},{8,11},{9,10},{10,... | collective-permute-start | bytes 1966088 | tf_op jit(solution)/shard_map/ppermute | solution.py:27
  51.1 18.1 %collective-permute-start.11 = (bf16[256,1280]{1,0:T(8,128)(2,1)S(1)}, bf16[256,1280]{1,0:T(8,128)(2,1)S(1)}, u32[]{:S(2)}, u32[]{:S(2)}) collective-permute-start(bf16[256,1280]{1,0:T(8,128)(2,1)S(1)} %pad_maximum_fusion.1), channel_id=1, source_target_pairs={{0,192},{1,193},{2,194},{3,195},{4,196},{5,197},{6,198},{7,199},{8... | collective-permute-start | bytes 1966088 | tf_op jit(solution)/shard_map/ppermute | solution.py:27
  54.0 15.2 %collective-permute-start.9 = (bf16[256,1280]{1,0:T(8,128)(2,1)S(1)}, bf16[256,1280]{1,0:T(8,128)(2,1)S(1)}, u32[]{:S(2)}, u32[]{:S(2)}) collective-permute-start(bf16[256,1280]{1,0:T(8,128)(2,1)S(1)} %pad_maximum_fusion), channel_id=1, source_target_pairs={{0,3},{1,2},{2,1},{3,0},{4,7},{5,6},{6,5},{7,4},{8,11},{9,10},{10,... | collective-permute-start | bytes 1966088 | tf_op jit(solution)/shard_map/ppermute | solution.py:27
  67.6 8.1 %collective-permute-start.22 = (f32[256,1024]{1,0:T(8,128)S(1)}, f32[256,1024]{1,0:T(8,128)S(1)}, u32[]{:S(2)}, u32[]{:S(2)}) collective-permute-start(f32[256,1024]{1,0:T(8,128)S(1)} %get-tuple-element.49), channel_id=1, source_target_pairs={{0,32},{1,33},{2,34},{3,35},{4,36},{5,37},{6,38},{7,39},{8,40},{9,... | collective-permute-start | bytes 3145736 | tf_op jit(solution)/shard_map/ppermute | solution.py:27
  79.7 30.6 %collective-permute-start.27 = (bf16[2,256,1024]{2,1,0:T(8,128)(2,1)S(1)}, bf16[2,256,1024]{2,1,0:T(8,128)(2,1)S(1)}, u32[]{:S(2)}, u32[]{:S(2)}) collective-permute-start(bf16[2,256,1024]{2,1,0:T(8,128)(2,1)S(1)} %get-tuple-element.52), channel_id=1, source_target_pairs={{0,32},{1,33},{2,34},{3,35},{4,36},{5,37},{6,38},{7,39},{8,40},{9,... | collective-permute-start | bytes 3145736 | tf_op jit(solution)/shard_map/ppermute | solution.py:27
  104.4 5.9 %collective-permute-start.26 = (f32[8,256]{1,0:T(8,128)S(1)}, f32[8,256]{1,0:T(8,128)S(1)}, u32[]{:S(2)}, u32[]{:S(2)}) collective-permute-start(f32[8,256]{1,0:T(8,128)S(1)} %result.1), channel_id=1, source_target_pairs={{0,32},{1,33},{2,34},{3,35},{4,36},{5,37},{6,38},{7,39},{8,40},{9,... | collective-permute-start | bytes 24584 | tf_op jit(solution)/shard_map/ppermute | solution.py:27
  113.7 9.8 %collective-permute-start.32 = (bf16[256,1280]{1,0:T(8,128)(2,1)S(1)}, bf16[256,1280]{1,0:T(8,128)(2,1)S(1)}, u32[]{:S(2)}, u32[]{:S(2)}) collective-permute-start(bf16[256,1280]{1,0:T(8,128)(2,1)S(1)} %gradient_sent_high.1), channel_id=1, source_target_pairs={{0,192},{1,193},{2,194},{3,195},{4,196},{5,197},{6,198},{7,199},{8... | collective-permute-start | bytes 1966088 | tf_op jit(solution)/shard_map/ppermute | solution.py:27
  114.0 10.7 %collective-permute-start.28 = (bf16[256,1280]{1,0:T(8,128)(2,1)S(1)}, bf16[256,1280]{1,0:T(8,128)(2,1)S(1)}, u32[]{:S(2)}, u32[]{:S(2)}) collective-permute-start(bf16[256,1280]{1,0:T(8,128)(2,1)S(1)} %get-tuple-element.56), channel_id=1, source_target_pairs={{0,3},{1,2},{2,1},{3,0},{4,7},{5,6},{6,5},{7,4},{8,11},{9,10},{10,... | collective-permute-start | bytes 1966088 | tf_op jit(solution)/shard_map/ppermute | solution.py:27
  123.7 7.2 %collective-permute-start.33 = (bf16[128,1280]{1,0:T(8,128)(2,1)S(1)}, bf16[128,1280]{1,0:T(8,128)(2,1)S(1)}, u32[]{:S(2)}, u32[]{:S(2)}) collective-permute-start(bf16[128,1280]{1,0:T(8,128)(2,1)S(1)} %slice.190), channel_id=1, source_target_pairs={{0,64},{1,65},{2,66},{3,67},{4,68},{5,69},{6,70},{7,71},{8,72},{9,... | collective-permute-start | bytes 983048 | tf_op jit(solution)/shard_map/ppermute | solution.py:27
  124.9 7.2 %collective-permute-start.29 = (bf16[128,1280]{1,0:T(8,128)(2,1)S(1)}, bf16[128,1280]{1,0:T(8,128)(2,1)S(1)}, u32[]{:S(2)}, u32[]{:S(2)}) collective-permute-start(bf16[128,1280]{1,0:T(8,128)(2,1)S(1)} %slice.191), channel_id=1, source_target_pairs={{0,1},{1,0},{2,3},{3,2},{4,5},{5,4},{6,7},{7,6},{8,9},{9,8},{10,11... | collective-permute-start | bytes 983048 | tf_op jit(solution)/shard_map/ppermute | solution.py:27
  136.5 5.1 %collective-permute-start.31 = (bf16[32,1280]{1,0:T(8,128)(2,1)S(1)}, bf16[32,1280]{1,0:T(8,128)(2,1)S(1)}, u32[]{:S(2)}, u32[]{:S(2)}) collective-permute-start(bf16[32,1280]{1,0:T(8,128)(2,1)S(1)} %slice.195), channel_id=1, source_target_pairs={{0,64},{1,65},{2,66},{3,67},{4,68},{5,69},{6,70},{7,71},{8,72},{9,... | collective-permute-start | bytes 245768 | tf_op jit(solution)/shard_map/ppermute | solution.py:27
  145.4 5.1 %collective-permute-start.37 = (bf16[8,2560]{1,0:T(8,128)(2,1)S(1)}, bf16[8,2560]{1,0:T(8,128)(2,1)S(1)}, u32[]{:S(2)}, u32[]{:S(2)}) collective-permute-start(bf16[8,2560]{1,0:T(8,128)(2,1)S(1)} %slice.196), channel_id=1, source_target_pairs={{0,24},{1,25},{2,26},{3,27},{4,28},{5,29},{6,30},{7,31},{8,16},{9,... | collective-permute-start | bytes 122888 | tf_op jit(solution)/shard_map/ppermute | solution.py:27
  154.2 9.1 %collective-permute-start.39 = (f32[2,2560]{1,0:T(2,128)S(1)}, f32[2,2560]{1,0:T(2,128)S(1)}, u32[]{:S(2)}, u32[]{:S(2)}) collective-permute-start(f32[2,2560]{1,0:T(2,128)S(1)} %constant_dynamic-slice_fusion.4), channel_id=1, source_target_pairs={{0,32},{1,33},{2,34},{3,35},{4,36},{5,37},{6,38},{7,39},{8,40},{9,... | collective-permute-start | bytes 61448 | tf_op jit(solution)/shard_map/ppermute | solution.py:27
  (19 other events, 96.5 us)

commit v4 on v3

--- a/solution.py
+++ b/solution.py
@@ -272,7 +272,7 @@
 
 
 def sent_kernel(
-    line, flags, common, result, result_got, parts, parts_got, head_keep, head_got, low, by_y, by_x
+    line, flags, common, result, result_got, parts, parts_got, head_keep, head_got, low, high, low_rows, high_rows, by_y, by_x
 ):
     mine = result.shape[1]
     core, flip = flags[0], 2 * flags[1]
@@ -293,10 +293,9 @@
             by_y[rows_at(y * X + x, line), :] = piece
             by_x[rows_at(x * Y + y, line), :] = piece
     low[...] = gradient(by_y[mine:, :], head_keep, head_got, 0).astype(BF16)
-
-
-def high_kernel(flags, by_x, head_keep, head_got, high):
-    high[...] = gradient(by_x[high.shape[0] :, :], head_keep, head_got, 1).astype(BF16)
+    high[...] = gradient(by_x[mine:, :], head_keep, head_got, 1).astype(BF16)
+    low_rows[...] = by_y[:mine, :]
+    high_rows[...] = by_x[:mine, :]
 
 
 def gradient(rows, head_keep, head_got, which):
@@ -308,10 +307,9 @@
     ) + lax.dot_general(rows[:, columns:], head_got[span, :], CONTRACT_LAST, preferred_element_type=F32)
 
 
-def kept_kernel(flags, by_y, by_x, head_keep, head_got, low, high):
-    mine = low.shape[0]
-    low[...] = gradient(by_y[:mine, :], head_keep, head_got, 0)
-    high[...] = gradient(by_x[:mine, :], head_keep, head_got, 1)
+def kept_kernel(flags, low_rows, high_rows, head_keep, head_got, low, high):
+    low[...] = gradient(low_rows[...], head_keep, head_got, 0)
+    high[...] = gradient(high_rows[...], head_keep, head_got, 1)
 
 
 def on_device(policy_hidden, reference_hidden, head_weight, pair_map, response_mask):
@@ -351,7 +349,8 @@
     own_token = flat(sx, sc, sz, sy) * own_rows + sr
     rows = gather_z(rows, Z_STEPS[:1])
     rows, own_token = lax.optimization_barrier((rows, own_token))
-    partner = jnp.take(pair_map, own_token, axis=0)
+    every = jnp.arange(tokens, dtype=jnp.int32)
+    partner = jnp.sum(jnp.where(own_token[0][:, None] == every[None], pair_map[None], 0), axis=1)[None]
     rows = gather_z(rows, Z_STEPS[1:2])
     rows, partner, head_weight = lax.optimization_barrier((rows, partner, head_weight))
     head_keep, head_send = run(
@@ -435,22 +434,27 @@
     (result,) = run(result_kernel, "result", flags, (everyone, message), [message_shape])
     result_got = exchange(result, across_cores)
 
-    rows_shape = jax.ShapeDtypeStruct((tokens, 2 * columns), BF16)
+    rows_shape = jax.ShapeDtypeStruct((mine, 2 * columns), BF16)
     sent_shape = jax.ShapeDtypeStruct((mine, part), BF16)
     kept_shape = jax.ShapeDtypeStruct((mine, part), F32)
-    low_sent, by_y, by_x = run(
+    operands = (common, result, result_got, parts, parts_got)
+    low_sent, high_sent, low_rows, high_rows = run(
         functools.partial(sent_kernel, line),
-        "gradient_sent_low",
-        flags,
-        (common, result, result_got, parts, parts_got, *head),
-        [sent_shape, rows_shape, rows_shape],
-        flops=flops // 4,
-    )
-    low_got = exchange(low_sent, along_y(3, 1))
-    (high_sent,) = run(high_kernel, "gradient_sent_high", flags, (by_x, *head), [sent_shape], flops=flops // 4)
-    high_got = exchange(high_sent, along_x(3, 1))
+        "gradient_sent",
+        flags,
+        (*operands, *head),
+        [sent_shape, sent_shape, rows_shape, rows_shape],
+        scratch=[pltpu.VMEM((tokens, 2 * columns), BF16)] * 2,
+        flops=flops // 2,
+    )
+    low_got, high_got = exchange(low_sent, along_y(3, 1)), exchange(high_sent, along_x(3, 1))
     low_kept, high_kept = run(
-        kept_kernel, "gradient_kept", flags, (by_y, by_x, *head), [kept_shape, kept_shape], flops=flops // 2
+        kept_kernel,
+        "gradient_kept",
+        flags,
+        (low_rows, high_rows, *head),
+        [kept_shape, kept_shape],
+        flops=flops // 2,
     )
     low_total = low_kept + low_got.astype(F32)
     high_total = high_kept + high_got.astype(F32)

time: 164 us -> 163 us (level)
  local copies, waits for them, and re-layouts: 7.05 us -> 3.55 us
    gather x1 -> x0, local copies, waits for them, and re-layouts: 3.48 us -> none  [on_device(): partner = jnp.take(pair_map, own_token, axis=0)]
    pallas_call x11 -> x10, Pallas kernels: 20.5 us -> 19.8 us  [run(): pl.pallas_call(kernel, out_shape=outputs, grid_spec=pltpu.PrefetchScalarG...]
  transfers between devices with their start and end apart: 40 -> 40, of which waited for: 25 -> 27; matrix products, arithmetic and copies ran while one was open for 3% -> 2% of each run, Pallas kernels for 9% -> 9%
where the time goes in v4:
time: 163 us; the launch traced here: 162 us
  starting transfers between devices  67.4 us (41%)
  waiting for transfers between devices  55.1 us (34%)
  Pallas kernels  19.8 us (12%)
  blocking collectives  12.1 us (7%)
  local copies, waits for them, and re-layouts  3.55 us (2%)
  other arithmetic  3.43 us (2%)
    ppermute x40, starting transfers between devices, exchange(): return lax.ppermute(value, AXES, pairs)  67.4 us
    ppermute x40, waiting for transfers between devices, exchange(): return lax.ppermute(value, AXES, pairs)  55.1 us
    pallas_call x10, Pallas kernels, run(): pl.pallas_call(kernel, out_shape=outputs, grid_spec=pltpu.PrefetchScalarG...  19.8 us
    all_to_all x1, blocking collectives, on_device(): lax.all_to_all(jnp.broadcast_to(line_message[None], (X * Y, 8, mine)), ('...  12.1 us
  transfers between devices with their start and end apart: 40, of which 27 were waited for; matrix products, arithmetic and copies ran while one was open for 2% of the time, Pallas kernels for 9%

profile of v4, /device:TPU:1, one launch (start us, length us, event | category | flops | bytes accessed | tf_op | source)
XLA Modules:
  0.0 162.4 jit_solution(4799105441016092003)
XLA Ops:
  1.5 3.3 %collective-permute-start = (bf16[2,5120]{1,0:T(2,128)(2,1)S(1)}, bf16[2,5120]{1,0:T(2,128)(2,1)S(1)}, u32[]{:S(2)}, u32[]{:S(2)}) collective-permute-start(bf16[2,5120]{1,0:T(2,128)(2,1)S(1)} %pad_maximum_fusion.14), channel_id=1, source_target_pairs={{0,32},{1,33},{2,34},{3,35},{4,36},{5,37},{6,38},{7,39},{8,40},{9,... | collective-permute-start | bytes 61448 | tf_op jit(solution)/shard_map/ppermute | solution.py:27
  7.2 3.7 %collective-permute-done.1 = bf16[4,5120]{1,0:T(4,128)(2,1)S(1)} collective-permute-done((bf16[4,5120]{1,0:T(4,128)(2,1)S(1)}, bf16[4,5120]{1,0:T(4,128)(2,1)S(1)}, u32[]{:S(2)}, u32[]{:S(2)}) %collective-permute-start.1) | collective-permute-done | bytes 40992 | tf_op jit(solution)/shard_map/ppermute | solution.py:27
  11.0 3.1 %collective-permute-start.2 = (bf16[8,5120]{1,0:T(8,128)(2,1)S(1)}, bf16[8,5120]{1,0:T(8,128)(2,1)S(1)}, u32[]{:S(2)}, u32[]{:S(2)}) collective-permute-start(bf16[8,5120]{1,0:T(8,128)(2,1)S(1)} %pad_maximum_fusion.11), channel_id=1, source_target_pairs={{0,24},{1,25},{2,26},{3,27},{4,28},{5,29},{6,30},{7,31},{8,16},{9,... | collective-permute-start | bytes 245768 | tf_op jit(solution)/shard_map/ppermute | solution.py:27
  16.8 2.5 %copy-done = bf16[5120,512]{1,0:T(8,128)(2,1)S(1)} copy-done((bf16[5120,512]{1,0:T(8,128)(2,1)S(1)}, bf16[5120,512]{1,0:T(8,128)(2,1)}, u32[]{:S(2)}) %copy-start) | copy-done | bytes 5242904
  20.9 3.6 %collective-permute-start.12 = (bf16[2560,512]{1,0:T(8,128)(2,1)S(1)}, bf16[2560,512]{1,0:T(8,128)(2,1)S(1)}, u32[]{:S(2)}, u32[]{:S(2)}) collective-permute-start(bf16[2560,512]{1,0:T(8,128)(2,1)S(1)} %get-tuple-element.43), channel_id=1, source_target_pairs={{0,32},{1,33},{2,34},{3,35},{4,36},{5,37},{6,38},{7,39},{8,40},{9,... | collective-permute-start | bytes 7864328 | tf_op jit(solution)/shard_map/ppermute | solution.py:27
  24.5 2.4 %collective-permute-start.14 = (bf16[32,1280]{1,0:T(8,128)(2,1)S(1)}, bf16[32,1280]{1,0:T(8,128)(2,1)S(1)}, u32[]{:S(2)}, u32[]{:S(2)}) collective-permute-start(bf16[32,1280]{1,0:T(8,128)(2,1)S(1)} %get-tuple-element.67.low), channel_id=1, source_target_pairs={{0,64},{1,65},{2,66},{3,67},{4,68},{5,69},{6,70},{7,71},{8,72},{9,... | collective-permute-start | bytes 245768 | tf_op jit(solution)/shard_map/ppermute | solution.py:27
  26.9 2.7 %collective-permute-start.16 = (bf16[32,1280]{1,0:T(8,128)(2,1)S(1)}, bf16[32,1280]{1,0:T(8,128)(2,1)S(1)}, u32[]{:S(2)}, u32[]{:S(2)}) collective-permute-start(bf16[32,1280]{1,0:T(8,128)(2,1)S(1)} %get-tuple-element.66.high), channel_id=1, source_target_pairs={{0,1},{1,0},{2,3},{3,2},{4,5},{5,4},{6,7},{7,6},{8,9},{9,8},{10,11... | collective-permute-start | bytes 245768 | tf_op jit(solution)/shard_map/ppermute | solution.py:27
  31.9 2.5 %collective-permute-done.6.high_near = bf16[32,1280]{1,0:T(8,128)(2,1)S(1)} collective-permute-done((bf16[32,1280]{1,0:T(8,128)(2,1)S(1)}, bf16[32,1280]{1,0:T(8,128)(2,1)S(1)}, u32[]{:S(2)}, u32[]{:S(2)}) %collective-permute-start.6) | collective-permute-done | bytes 81952 | tf_op jit(solution)/shard_map/ppermute | solution.py:27
  38.7 2.6 %collective-permute-start.18 = (bf16[128,1280]{1,0:T(8,128)(2,1)S(1)}, bf16[128,1280]{1,0:T(8,128)(2,1)S(1)}, u32[]{:S(2)}, u32[]{:S(2)}) collective-permute-start(bf16[128,1280]{1,0:T(8,128)(2,1)S(1)} %get-tuple-element.47.a), channel_id=1, source_target_pairs={{0,1},{1,0},{2,3},{3,2},{4,5},{5,4},{6,7},{7,6},{8,9},{9,8},{10,11... | collective-permute-start | bytes 983048 | tf_op jit(solution)/shard_map/ppermute | solution.py:27
  42.6 3.4 %collective-permute-start.10 = (bf16[128,1280]{1,0:T(8,128)(2,1)S(1)}, bf16[128,1280]{1,0:T(8,128)(2,1)S(1)}, u32[]{:S(2)}, u32[]{:S(2)}) collective-permute-start(bf16[128,1280]{1,0:T(8,128)(2,1)S(1)} %get-tuple-element.41.b), channel_id=1, source_target_pairs={{0,64},{1,65},{2,66},{3,67},{4,68},{5,69},{6,70},{7,71},{8,72},{9,... | collective-permute-start | bytes 983048 | tf_op jit(solution)/shard_map/ppermute | solution.py:27
  46.0 2.6 %collective-permute-start.8 = (bf16[128,1280]{1,0:T(8,128)(2,1)S(1)}, bf16[128,1280]{1,0:T(8,128)(2,1)S(1)}, u32[]{:S(2)}, u32[]{:S(2)}) collective-permute-start(bf16[128,1280]{1,0:T(8,128)(2,1)S(1)} %get-tuple-element.40.a), channel_id=1, source_target_pairs={{0,1},{1,0},{2,3},{3,2},{4,5},{5,4},{6,7},{7,6},{8,9},{9,8},{10,11... | collective-permute-start | bytes 983048 | tf_op jit(solution)/shard_map/ppermute | solution.py:27
  53.6 7.1 %collective-permute-done.21.b_far = bf16[256,1280]{1,0:T(8,128)(2,1)S(1)} collective-permute-done((bf16[256,1280]{1,0:T(8,128)(2,1)S(1)}, bf16[256,1280]{1,0:T(8,128)(2,1)S(1)}, u32[]{:S(2)}, u32[]{:S(2)}) %collective-permute-start.21) | collective-permute-done | bytes 655392 | tf_op jit(solution)/shard_map/ppermute | solution.py:27
  60.9 6.0 %base_logits.1 = (f32[256,1024]{1,0:T(8,128)S(1)}, f32[256,1024]{1,0:T(8,128)S(1)}) custom-call(s32[2]{0:T(128)S(1)} %pad_add_fusion.flags, f32[1,512]{1,0:T(1,128)S(1)} %add_convert_fusion.1.low_place, f32[1,512]{1,0:T(1,128)S(1)} %get-tuple-element.60.high_place, bf16[128,1280]{1,0:T(8,128)(2,1)S(1)} %get-tuple-element.47.a, ...), custom_call_target="tpu_custom_call" | custom-call | flops 5368709120 | bytes 9965568 | tf_op jit(solution)/shard_map/base_logits/pallas_call | solution.py:89
  68.6 3.9 %policy_logits.1 = (f32[256,1024]{1,0:T(8,128)S(1)}, f32[256,1024]{1,0:T(8,128)S(1)}) custom-call(s32[2]{0:T(128)S(1)} %pad_add_fusion.flags, bf16[128,1280]{1,0:T(8,128)(2,1)S(1)} %get-tuple-element.40.a, bf16[128,1280]{1,0:T(8,128)(2,1)S(1)} %collective-permute-done.8.a_near, bf16[256,1280]{1,0:T(8,128)(2,1)S(1)} %collective-permute-done.9.a_far, ...), custom_call_target="tpu_custom_call" | custom-call | flops 2684354560 | bytes 9961472 | tf_op jit(solution)/shard_map/policy_logits/pallas_call | solution.py:89
  72.5 2.5 %collective-permute-start.13 = (f32[256,1024]{1,0:T(8,128)S(1)}, f32[256,1024]{1,0:T(8,128)S(1)}, u32[]{:S(2)}, u32[]{:S(2)}) collective-permute-start(f32[256,1024]{1,0:T(8,128)S(1)} %get-tuple-element.45), channel_id=1, source_target_pairs={{0,32},{1,33},{2,34},{3,35},{4,36},{5,37},{6,38},{7,39},{8,40},{9,... | collective-permute-start | bytes 3145736 | tf_op jit(solution)/shard_map/ppermute | solution.py:27
  83.0 3.3 %collective-permute-start.24 = (f32[16,256]{1,0:T(8,128)S(1)}, f32[16,256]{1,0:T(8,128)S(1)}, u32[]{:S(2)}, u32[]{:S(2)}) collective-permute-start(f32[16,256]{1,0:T(8,128)S(1)} %pad_maximum_fusion.16), channel_id=1, source_target_pairs={{0,24},{1,25},{2,26},{3,27},{4,28},{5,29},{6,30},{7,31},{8,16},{9,... | collective-permute-start | bytes 49160 | tf_op jit(solution)/shard_map/ppermute | solution.py:27
  91.1 12.1 %all_to_all.5.messages = f32[16,8,256]{2,1,0:T(8,128)S(1)} all-to-all(f32[16,8,256]{2,1,0:T(8,128)S(1)} %broadcast_in_dim.33), channel_id=1, replica_groups=mesh['x'=4,'core'=2,'z'=8,'y'=4] {'x','y'}, dimensions={0} | all-to-all | bytes 262144 | tf_op jit(solution)/shard_map/all_to_all | solution.py:433
  103.8 5.0 %collective-permute-start.26 = (f32[8,256]{1,0:T(8,128)S(1)}, f32[8,256]{1,0:T(8,128)S(1)}, u32[]{:S(2)}, u32[]{:S(2)}) collective-permute-start(f32[8,256]{1,0:T(8,128)S(1)} %result.1), channel_id=1, source_target_pairs={{0,32},{1,33},{2,34},{3,35},{4,36},{5,37},{6,38},{7,39},{8,40},{9,... | collective-permute-start | bytes 24584 | tf_op jit(solution)/shard_map/ppermute | solution.py:27
  109.7 2.7 %gradient_sent.1 = (bf16[256,1280]{1,0:T(8,128)(2,1)S(1)}, bf16[256,1280]{1,0:T(8,128)(2,1)S(1)}, bf16[256,1024]{1,0:T(8,128)(2,1)S(1)}, bf16[256,1024]{1,0:T(8,128)(2,1)S(1)}) custom-call(s32[2]{0:T(128)S(1)} %pad_add_fusion.flags, f32[1,512]{1,0:T(1,128)S(1)} %add_convert_fusion.2.common, f32[8,256]{1,0:T(8,128)S(1)} %result.1, ...), custom_call_target="tpu_custom_call" | custom-call | flops 1342177280 | bytes 9717760 | tf_op jit(solution)/shard_map/gradient_sent/pallas_call | solution.py:89
  115.1 7.1 %collective-permute-done.32 = bf16[256,1280]{1,0:T(8,128)(2,1)S(1)} collective-permute-done((bf16[256,1280]{1,0:T(8,128)(2,1)S(1)}, bf16[256,1280]{1,0:T(8,128)(2,1)S(1)}, u32[]{:S(2)}, u32[]{:S(2)}) %collective-permute-start.32) | collective-permute-done | bytes 655392 | tf_op jit(solution)/shard_map/ppermute | solution.py:27
  124.4 5.2 %collective-permute-done.33 = bf16[128,1280]{1,0:T(8,128)(2,1)S(1)} collective-permute-done((bf16[128,1280]{1,0:T(8,128)(2,1)S(1)}, bf16[128,1280]{1,0:T(8,128)(2,1)S(1)}, u32[]{:S(2)}, u32[]{:S(2)}) %collective-permute-start.33) | collective-permute-done | bytes 327712 | tf_op jit(solution)/shard_map/ppermute | solution.py:27
  131.3 2.9 %collective-permute-done.34 = bf16[64,1280]{1,0:T(8,128)(2,1)S(1)} collective-permute-done((bf16[64,1280]{1,0:T(8,128)(2,1)S(1)}, bf16[64,1280]{1,0:T(8,128)(2,1)S(1)}, u32[]{:S(2)}, u32[]{:S(2)}) %collective-permute-start.34) | collective-permute-done | bytes 163872 | tf_op jit(solution)/shard_map/ppermute | solution.py:27
  144.1 3.4 %collective-permute-start.37 = (bf16[8,2560]{1,0:T(8,128)(2,1)S(1)}, bf16[8,2560]{1,0:T(8,128)(2,1)S(1)}, u32[]{:S(2)}, u32[]{:S(2)}) collective-permute-start(bf16[8,2560]{1,0:T(8,128)(2,1)S(1)} %slice.194), channel_id=1, source_target_pairs={{0,24},{1,25},{2,26},{3,27},{4,28},{5,29},{6,30},{7,31},{8,16},{9,... | collective-permute-start | bytes 122888 | tf_op jit(solution)/shard_map/ppermute | solution.py:27
  152.9 8.0 %collective-permute-start.39 = (f32[2,2560]{1,0:T(2,128)S(1)}, f32[2,2560]{1,0:T(2,128)S(1)}, u32[]{:S(2)}, u32[]{:S(2)}) collective-permute-start(f32[2,2560]{1,0:T(2,128)S(1)} %constant_dynamic-slice_fusion.3), channel_id=1, source_target_pairs={{0,32},{1,33},{2,34},{3,35},{4,36},{5,37},{6,38},{7,39},{8,40},{9,... | collective-permute-start | bytes 61448 | tf_op jit(solution)/shard_map/ppermute | solution.py:27
  (128 shorter events, 59.5 us)
Async XLA Ops:
  5.8 5.1 %collective-permute-start.1 = (bf16[4,5120]{1,0:T(4,128)(2,1)S(1)}, bf16[4,5120]{1,0:T(4,128)(2,1)S(1)}, u32[]{:S(2)}, u32[]{:S(2)}) collective-permute-start(bf16[4,5120]{1,0:T(4,128)(2,1)S(1)} %pad_maximum_fusion.12), channel_id=1, source_target_pairs={{0,8},{1,9},{2,10},{3,11},{4,12},{5,13},{6,14},{7,15},{8,0},{9,1},... | collective-permute-start | bytes 122888 | tf_op jit(solution)/shard_map/ppermute | solution.py:27
  11.0 5.5 %collective-permute-start.2 = (bf16[8,5120]{1,0:T(8,128)(2,1)S(1)}, bf16[8,5120]{1,0:T(8,128)(2,1)S(1)}, u32[]{:S(2)}, u32[]{:S(2)}) collective-permute-start(bf16[8,5120]{1,0:T(8,128)(2,1)S(1)} %pad_maximum_fusion.11), channel_id=1, source_target_pairs={{0,24},{1,25},{2,26},{3,27},{4,28},{5,29},{6,30},{7,31},{8,16},{9,... | collective-permute-start | bytes 245768 | tf_op jit(solution)/shard_map/ppermute | solution.py:27
  20.9 40.0 %collective-permute-start.12 = (bf16[2560,512]{1,0:T(8,128)(2,1)S(1)}, bf16[2560,512]{1,0:T(8,128)(2,1)S(1)}, u32[]{:S(2)}, u32[]{:S(2)}) collective-permute-start(bf16[2560,512]{1,0:T(8,128)(2,1)S(1)} %get-tuple-element.43), channel_id=1, source_target_pairs={{0,32},{1,33},{2,34},{3,35},{4,36},{5,37},{6,38},{7,39},{8,40},{9,... | collective-permute-start | bytes 7864328 | tf_op jit(solution)/shard_map/ppermute | solution.py:27
  24.5 5.4 %collective-permute-start.14 = (bf16[32,1280]{1,0:T(8,128)(2,1)S(1)}, bf16[32,1280]{1,0:T(8,128)(2,1)S(1)}, u32[]{:S(2)}, u32[]{:S(2)}) collective-permute-start(bf16[32,1280]{1,0:T(8,128)(2,1)S(1)} %get-tuple-element.67.low), channel_id=1, source_target_pairs={{0,64},{1,65},{2,66},{3,67},{4,68},{5,69},{6,70},{7,71},{8,72},{9,... | collective-permute-start | bytes 245768 | tf_op jit(solution)/shard_map/ppermute | solution.py:27
  29.7 8.1 %collective-permute-start.4 = (bf16[32,1280]{1,0:T(8,128)(2,1)S(1)}, bf16[32,1280]{1,0:T(8,128)(2,1)S(1)}, u32[]{:S(2)}, u32[]{:S(2)}) collective-permute-start(bf16[32,1280]{1,0:T(8,128)(2,1)S(1)} %get-tuple-element.69.low), channel_id=1, source_target_pairs={{0,64},{1,65},{2,66},{3,67},{4,68},{5,69},{6,70},{7,71},{8,72},{9,... | collective-permute-start | bytes 245768 | tf_op jit(solution)/shard_map/ppermute | solution.py:27
  34.5 6.9 %collective-permute-start.7 = (bf16[64,1280]{1,0:T(8,128)(2,1)S(1)}, bf16[64,1280]{1,0:T(8,128)(2,1)S(1)}, u32[]{:S(2)}, u32[]{:S(2)}) collective-permute-start(bf16[64,1280]{1,0:T(8,128)(2,1)S(1)} %pad_maximum_fusion.8), channel_id=1, source_target_pairs={{0,3},{1,2},{2,1},{3,0},{4,7},{5,6},{6,5},{7,4},{8,11},{9,10},{10,... | collective-permute-start | bytes 491528 | tf_op jit(solution)/shard_map/ppermute | solution.py:27
  36.6 12.0 %collective-permute-start.20 = (bf16[128,1280]{1,0:T(8,128)(2,1)S(1)}, bf16[128,1280]{1,0:T(8,128)(2,1)S(1)}, u32[]{:S(2)}, u32[]{:S(2)}) collective-permute-start(bf16[128,1280]{1,0:T(8,128)(2,1)S(1)} %get-tuple-element.48.b), channel_id=1, source_target_pairs={{0,64},{1,65},{2,66},{3,67},{4,68},{5,69},{6,70},{7,71},{8,72},{9,... | collective-permute-start | bytes 983048 | tf_op jit(solution)/shard_map/ppermute | solution.py:27
  38.7 10.1 %collective-permute-start.18 = (bf16[128,1280]{1,0:T(8,128)(2,1)S(1)}, bf16[128,1280]{1,0:T(8,128)(2,1)S(1)}, u32[]{:S(2)}, u32[]{:S(2)}) collective-permute-start(bf16[128,1280]{1,0:T(8,128)(2,1)S(1)} %get-tuple-element.47.a), channel_id=1, source_target_pairs={{0,1},{1,0},{2,3},{3,2},{4,5},{5,4},{6,7},{7,6},{8,9},{9,8},{10,11... | collective-permute-start | bytes 983048 | tf_op jit(solution)/shard_map/ppermute | solution.py:27
  42.6 7.9 %collective-permute-start.10 = (bf16[128,1280]{1,0:T(8,128)(2,1)S(1)}, bf16[128,1280]{1,0:T(8,128)(2,1)S(1)}, u32[]{:S(2)}, u32[]{:S(2)}) collective-permute-start(bf16[128,1280]{1,0:T(8,128)(2,1)S(1)} %get-tuple-element.41.b), channel_id=1, source_target_pairs={{0,64},{1,65},{2,66},{3,67},{4,68},{5,69},{6,70},{7,71},{8,72},{9,... | collective-permute-start | bytes 983048 | tf_op jit(solution)/shard_map/ppermute | solution.py:27
  46.0 7.4 %collective-permute-start.8 = (bf16[128,1280]{1,0:T(8,128)(2,1)S(1)}, bf16[128,1280]{1,0:T(8,128)(2,1)S(1)}, u32[]{:S(2)}, u32[]{:S(2)}) collective-permute-start(bf16[128,1280]{1,0:T(8,128)(2,1)S(1)} %get-tuple-element.40.a), channel_id=1, source_target_pairs={{0,1},{1,0},{2,3},{3,2},{4,5},{5,4},{6,7},{7,6},{8,9},{9,8},{10,11... | collective-permute-start | bytes 983048 | tf_op jit(solution)/shard_map/ppermute | solution.py:27
  48.7 12.0 %collective-permute-start.21 = (bf16[256,1280]{1,0:T(8,128)(2,1)S(1)}, bf16[256,1280]{1,0:T(8,128)(2,1)S(1)}, u32[]{:S(2)}, u32[]{:S(2)}) collective-permute-start(bf16[256,1280]{1,0:T(8,128)(2,1)S(1)} %pad_maximum_fusion.3), channel_id=1, source_target_pairs={{0,192},{1,193},{2,194},{3,195},{4,196},{5,197},{6,198},{7,199},{8... | collective-permute-start | bytes 1966088 | tf_op jit(solution)/shard_map/ppermute | solution.py:27
  48.8 12.1 %collective-permute-start.19 = (bf16[256,1280]{1,0:T(8,128)(2,1)S(1)}, bf16[256,1280]{1,0:T(8,128)(2,1)S(1)}, u32[]{:S(2)}, u32[]{:S(2)}) collective-permute-start(bf16[256,1280]{1,0:T(8,128)(2,1)S(1)} %pad_maximum_fusion.2), channel_id=1, source_target_pairs={{0,3},{1,2},{2,1},{3,0},{4,7},{5,6},{6,5},{7,4},{8,11},{9,10},{10,... | collective-permute-start | bytes 1966088 | tf_op jit(solution)/shard_map/ppermute | solution.py:27
  50.5 18.1 %collective-permute-start.11 = (bf16[256,1280]{1,0:T(8,128)(2,1)S(1)}, bf16[256,1280]{1,0:T(8,128)(2,1)S(1)}, u32[]{:S(2)}, u32[]{:S(2)}) collective-permute-start(bf16[256,1280]{1,0:T(8,128)(2,1)S(1)} %pad_maximum_fusion.1), channel_id=1, source_target_pairs={{0,192},{1,193},{2,194},{3,195},{4,196},{5,197},{6,198},{7,199},{8... | collective-permute-start | bytes 1966088 | tf_op jit(solution)/shard_map/ppermute | solution.py:27
  53.5 15.1 %collective-permute-start.9 = (bf16[256,1280]{1,0:T(8,128)(2,1)S(1)}, bf16[256,1280]{1,0:T(8,128)(2,1)S(1)}, u32[]{:S(2)}, u32[]{:S(2)}) collective-permute-start(bf16[256,1280]{1,0:T(8,128)(2,1)S(1)} %pad_maximum_fusion), channel_id=1, source_target_pairs={{0,3},{1,2},{2,1},{3,0},{4,7},{5,6},{6,5},{7,4},{8,11},{9,10},{10,... | collective-permute-start | bytes 1966088 | tf_op jit(solution)/shard_map/ppermute | solution.py:27
  66.9 8.1 %collective-permute-start.22 = (f32[256,1024]{1,0:T(8,128)S(1)}, f32[256,1024]{1,0:T(8,128)S(1)}, u32[]{:S(2)}, u32[]{:S(2)}) collective-permute-start(f32[256,1024]{1,0:T(8,128)S(1)} %get-tuple-element.50), channel_id=1, source_target_pairs={{0,32},{1,33},{2,34},{3,35},{4,36},{5,37},{6,38},{7,39},{8,40},{9,... | collective-permute-start | bytes 3145736 | tf_op jit(solution)/shard_map/ppermute | solution.py:27
  79.1 30.6 %collective-permute-start.27 = (bf16[2,256,1024]{2,1,0:T(8,128)(2,1)S(1)}, bf16[2,256,1024]{2,1,0:T(8,128)(2,1)S(1)}, u32[]{:S(2)}, u32[]{:S(2)}) collective-permute-start(bf16[2,256,1024]{2,1,0:T(8,128)(2,1)S(1)} %get-tuple-element.53), channel_id=1, source_target_pairs={{0,32},{1,33},{2,34},{3,35},{4,36},{5,37},{6,38},{7,39},{8,40},{9,... | collective-permute-start | bytes 3145736 | tf_op jit(solution)/shard_map/ppermute | solution.py:27
  103.8 5.9 %collective-permute-start.26 = (f32[8,256]{1,0:T(8,128)S(1)}, f32[8,256]{1,0:T(8,128)S(1)}, u32[]{:S(2)}, u32[]{:S(2)}) collective-permute-start(f32[8,256]{1,0:T(8,128)S(1)} %result.1), channel_id=1, source_target_pairs={{0,32},{1,33},{2,34},{3,35},{4,36},{5,37},{6,38},{7,39},{8,40},{9,... | collective-permute-start | bytes 24584 | tf_op jit(solution)/shard_map/ppermute | solution.py:27
  112.4 9.8 %collective-permute-start.32 = (bf16[256,1280]{1,0:T(8,128)(2,1)S(1)}, bf16[256,1280]{1,0:T(8,128)(2,1)S(1)}, u32[]{:S(2)}, u32[]{:S(2)}) collective-permute-start(bf16[256,1280]{1,0:T(8,128)(2,1)S(1)} %get-tuple-element.59), channel_id=1, source_target_pairs={{0,192},{1,193},{2,194},{3,195},{4,196},{5,197},{6,198},{7,199},{8... | collective-permute-start | bytes 1966088 | tf_op jit(solution)/shard_map/ppermute | solution.py:27
  112.7 10.7 %collective-permute-start.28 = (bf16[256,1280]{1,0:T(8,128)(2,1)S(1)}, bf16[256,1280]{1,0:T(8,128)(2,1)S(1)}, u32[]{:S(2)}, u32[]{:S(2)}) collective-permute-start(bf16[256,1280]{1,0:T(8,128)(2,1)S(1)} %get-tuple-element.57), channel_id=1, source_target_pairs={{0,3},{1,2},{2,1},{3,0},{4,7},{5,6},{6,5},{7,4},{8,11},{9,10},{10,... | collective-permute-start | bytes 1966088 | tf_op jit(solution)/shard_map/ppermute | solution.py:27
  122.4 7.2 %collective-permute-start.33 = (bf16[128,1280]{1,0:T(8,128)(2,1)S(1)}, bf16[128,1280]{1,0:T(8,128)(2,1)S(1)}, u32[]{:S(2)}, u32[]{:S(2)}) collective-permute-start(bf16[128,1280]{1,0:T(8,128)(2,1)S(1)} %slice.188), channel_id=1, source_target_pairs={{0,64},{1,65},{2,66},{3,67},{4,68},{5,69},{6,70},{7,71},{8,72},{9,... | collective-permute-start | bytes 983048 | tf_op jit(solution)/shard_map/ppermute | solution.py:27
  123.5 7.2 %collective-permute-start.29 = (bf16[128,1280]{1,0:T(8,128)(2,1)S(1)}, bf16[128,1280]{1,0:T(8,128)(2,1)S(1)}, u32[]{:S(2)}, u32[]{:S(2)}) collective-permute-start(bf16[128,1280]{1,0:T(8,128)(2,1)S(1)} %slice.189), channel_id=1, source_target_pairs={{0,1},{1,0},{2,3},{3,2},{4,5},{5,4},{6,7},{7,6},{8,9},{9,8},{10,11... | collective-permute-start | bytes 983048 | tf_op jit(solution)/shard_map/ppermute | solution.py:27
  135.2 5.1 %collective-permute-start.31 = (bf16[32,1280]{1,0:T(8,128)(2,1)S(1)}, bf16[32,1280]{1,0:T(8,128)(2,1)S(1)}, u32[]{:S(2)}, u32[]{:S(2)}) collective-permute-start(bf16[32,1280]{1,0:T(8,128)(2,1)S(1)} %slice.193), channel_id=1, source_target_pairs={{0,64},{1,65},{2,66},{3,67},{4,68},{5,69},{6,70},{7,71},{8,72},{9,... | collective-permute-start | bytes 245768 | tf_op jit(solution)/shard_map/ppermute | solution.py:27
  144.1 5.1 %collective-permute-start.37 = (bf16[8,2560]{1,0:T(8,128)(2,1)S(1)}, bf16[8,2560]{1,0:T(8,128)(2,1)S(1)}, u32[]{:S(2)}, u32[]{:S(2)}) collective-permute-start(bf16[8,2560]{1,0:T(8,128)(2,1)S(1)} %slice.194), channel_id=1, source_target_pairs={{0,24},{1,25},{2,26},{3,27},{4,28},{5,29},{6,30},{7,31},{8,16},{9,... | collective-permute-start | bytes 122888 | tf_op jit(solution)/shard_map/ppermute | solution.py:27
  152.9 8.8 %collective-permute-start.39 = (f32[2,2560]{1,0:T(2,128)S(1)}, f32[2,2560]{1,0:T(2,128)S(1)}, u32[]{:S(2)}, u32[]{:S(2)}) collective-permute-start(f32[2,2560]{1,0:T(2,128)S(1)} %constant_dynamic-slice_fusion.3), channel_id=1, source_target_pairs={{0,32},{1,33},{2,34},{3,35},{4,36},{5,37},{6,38},{7,39},{8,40},{9,... | collective-permute-start | bytes 61448 | tf_op jit(solution)/shard_map/ppermute | solution.py:27
  (18 other events, 83.9 us)

commit v5 on v4

--- a/solution.py
+++ b/solution.py
@@ -334,7 +334,6 @@
     keep = side_by_side(c0 * half)
     got = exchange(side_by_side((1 - c0) * half), across_cores)
     rows = jnp.concatenate([jnp.where(second, got, keep), jnp.where(second, keep, got)], 0)
-    rows, head_weight = lax.optimization_barrier((rows, head_weight))
     flags = jnp.stack([c0, c0 ^ (y0 >> 1)]).astype(jnp.int32)
     head_shape = jax.ShapeDtypeStruct((half, columns), BF16)
     slot = jnp.arange(tokens, dtype=jnp.int32)[None]
@@ -352,7 +351,7 @@
     every = jnp.arange(tokens, dtype=jnp.int32)
     partner = jnp.sum(jnp.where(own_token[0][:, None] == every[None], pair_map[None], 0), axis=1)[None]
     rows = gather_z(rows, Z_STEPS[1:2])
-    rows, partner, head_weight = lax.optimization_barrier((rows, partner, head_weight))
+    rows, partner = lax.optimization_barrier((rows, partner))
     head_keep, head_send = run(
         take_head,
         "take_head",

time: 163 us -> 163 us (level)
  no operation moved by 1% of the time
where the time goes in v5:
time: 163 us; the launch traced here: 162 us
  starting transfers between devices  67.4 us (41%)
  waiting for transfers between devices  55.1 us (34%)
  Pallas kernels  19.8 us (12%)
  blocking collectives  12.1 us (7%)
  local copies, waits for them, and re-layouts  3.55 us (2%)
  other arithmetic  3.46 us (2%)
    ppermute x40, starting transfers between devices, exchange(): return lax.ppermute(value, AXES, pairs)  67.4 us
    ppermute x40, waiting for transfers between devices, exchange(): return lax.ppermute(value, AXES, pairs)  55.1 us
    pallas_call x10, Pallas kernels, run(): pl.pallas_call(kernel, out_shape=outputs, grid_spec=pltpu.PrefetchScalarG...  19.8 us
    all_to_all x1, blocking collectives, on_device(): lax.all_to_all(jnp.broadcast_to(line_message[None], (X * Y, 8, mine)), ('...  12.1 us
  transfers between devices with their start and end apart: 40, of which 27 were waited for; matrix products, arithmetic and copies ran while one was open for 2% of the time, Pallas kernels for 9%

profile of v5, /device:TPU:1, one launch (start us, length us, event | category | flops | bytes accessed | tf_op | source)
XLA Modules:
  0.0 162.4 jit_solution(1064966340498613032)
XLA Ops:
  1.5 3.3 %collective-permute-start = (bf16[2,5120]{1,0:T(2,128)(2,1)S(1)}, bf16[2,5120]{1,0:T(2,128)(2,1)S(1)}, u32[]{:S(2)}, u32[]{:S(2)}) collective-permute-start(bf16[2,5120]{1,0:T(2,128)(2,1)S(1)} %pad_maximum_fusion.14), channel_id=1, source_target_pairs={{0,32},{1,33},{2,34},{3,35},{4,36},{5,37},{6,38},{7,39},{8,40},{9,... | collective-permute-start | bytes 61448 | tf_op jit(solution)/shard_map/ppermute | solution.py:27
  7.2 3.7 %collective-permute-done.1 = bf16[4,5120]{1,0:T(4,128)(2,1)S(1)} collective-permute-done((bf16[4,5120]{1,0:T(4,128)(2,1)S(1)}, bf16[4,5120]{1,0:T(4,128)(2,1)S(1)}, u32[]{:S(2)}, u32[]{:S(2)}) %collective-permute-start.1) | collective-permute-done | bytes 40992 | tf_op jit(solution)/shard_map/ppermute | solution.py:27
  11.0 3.1 %collective-permute-start.2 = (bf16[8,5120]{1,0:T(8,128)(2,1)S(1)}, bf16[8,5120]{1,0:T(8,128)(2,1)S(1)}, u32[]{:S(2)}, u32[]{:S(2)}) collective-permute-start(bf16[8,5120]{1,0:T(8,128)(2,1)S(1)} %pad_maximum_fusion.11), channel_id=1, source_target_pairs={{0,24},{1,25},{2,26},{3,27},{4,28},{5,29},{6,30},{7,31},{8,16},{9,... | collective-permute-start | bytes 245768 | tf_op jit(solution)/shard_map/ppermute | solution.py:27
  16.9 2.5 %copy-done = bf16[5120,512]{1,0:T(8,128)(2,1)S(1)} copy-done((bf16[5120,512]{1,0:T(8,128)(2,1)S(1)}, bf16[5120,512]{1,0:T(8,128)(2,1)}, u32[]{:S(2)}) %copy-start) | copy-done | bytes 5242904
  20.9 3.6 %collective-permute-start.12 = (bf16[2560,512]{1,0:T(8,128)(2,1)S(1)}, bf16[2560,512]{1,0:T(8,128)(2,1)S(1)}, u32[]{:S(2)}, u32[]{:S(2)}) collective-permute-start(bf16[2560,512]{1,0:T(8,128)(2,1)S(1)} %get-tuple-element.37), channel_id=1, source_target_pairs={{0,32},{1,33},{2,34},{3,35},{4,36},{5,37},{6,38},{7,39},{8,40},{9,... | collective-permute-start | bytes 7864328 | tf_op jit(solution)/shard_map/ppermute | solution.py:27
  24.5 2.4 %collective-permute-start.14 = (bf16[32,1280]{1,0:T(8,128)(2,1)S(1)}, bf16[32,1280]{1,0:T(8,128)(2,1)S(1)}, u32[]{:S(2)}, u32[]{:S(2)}) collective-permute-start(bf16[32,1280]{1,0:T(8,128)(2,1)S(1)} %get-tuple-element.61.low), channel_id=1, source_target_pairs={{0,64},{1,65},{2,66},{3,67},{4,68},{5,69},{6,70},{7,71},{8,72},{9,... | collective-permute-start | bytes 245768 | tf_op jit(solution)/shard_map/ppermute | solution.py:27
  27.0 2.7 %collective-permute-start.16 = (bf16[32,1280]{1,0:T(8,128)(2,1)S(1)}, bf16[32,1280]{1,0:T(8,128)(2,1)S(1)}, u32[]{:S(2)}, u32[]{:S(2)}) collective-permute-start(bf16[32,1280]{1,0:T(8,128)(2,1)S(1)} %get-tuple-element.60.high), channel_id=1, source_target_pairs={{0,1},{1,0},{2,3},{3,2},{4,5},{5,4},{6,7},{7,6},{8,9},{9,8},{10,11... | collective-permute-start | bytes 245768 | tf_op jit(solution)/shard_map/ppermute | solution.py:27
  31.9 2.5 %collective-permute-done.6.high_near = bf16[32,1280]{1,0:T(8,128)(2,1)S(1)} collective-permute-done((bf16[32,1280]{1,0:T(8,128)(2,1)S(1)}, bf16[32,1280]{1,0:T(8,128)(2,1)S(1)}, u32[]{:S(2)}, u32[]{:S(2)}) %collective-permute-start.6) | collective-permute-done | bytes 81952 | tf_op jit(solution)/shard_map/ppermute | solution.py:27
  38.7 2.6 %collective-permute-start.18 = (bf16[128,1280]{1,0:T(8,128)(2,1)S(1)}, bf16[128,1280]{1,0:T(8,128)(2,1)S(1)}, u32[]{:S(2)}, u32[]{:S(2)}) collective-permute-start(bf16[128,1280]{1,0:T(8,128)(2,1)S(1)} %get-tuple-element.41.a), channel_id=1, source_target_pairs={{0,1},{1,0},{2,3},{3,2},{4,5},{5,4},{6,7},{7,6},{8,9},{9,8},{10,11... | collective-permute-start | bytes 983048 | tf_op jit(solution)/shard_map/ppermute | solution.py:27
  42.6 3.4 %collective-permute-start.10 = (bf16[128,1280]{1,0:T(8,128)(2,1)S(1)}, bf16[128,1280]{1,0:T(8,128)(2,1)S(1)}, u32[]{:S(2)}, u32[]{:S(2)}) collective-permute-start(bf16[128,1280]{1,0:T(8,128)(2,1)S(1)} %get-tuple-element.35.b), channel_id=1, source_target_pairs={{0,64},{1,65},{2,66},{3,67},{4,68},{5,69},{6,70},{7,71},{8,72},{9,... | collective-permute-start | bytes 983048 | tf_op jit(solution)/shard_map/ppermute | solution.py:27
  46.0 2.6 %collective-permute-start.8 = (bf16[128,1280]{1,0:T(8,128)(2,1)S(1)}, bf16[128,1280]{1,0:T(8,128)(2,1)S(1)}, u32[]{:S(2)}, u32[]{:S(2)}) collective-permute-start(bf16[128,1280]{1,0:T(8,128)(2,1)S(1)} %get-tuple-element.34.a), channel_id=1, source_target_pairs={{0,1},{1,0},{2,3},{3,2},{4,5},{5,4},{6,7},{7,6},{8,9},{9,8},{10,11... | collective-permute-start | bytes 983048 | tf_op jit(solution)/shard_map/ppermute | solution.py:27
  53.6 7.1 %collective-permute-done.21.b_far = bf16[256,1280]{1,0:T(8,128)(2,1)S(1)} collective-permute-done((bf16[256,1280]{1,0:T(8,128)(2,1)S(1)}, bf16[256,1280]{1,0:T(8,128)(2,1)S(1)}, u32[]{:S(2)}, u32[]{:S(2)}) %collective-permute-start.21) | collective-permute-done | bytes 655392 | tf_op jit(solution)/shard_map/ppermute | solution.py:27
  60.9 6.0 %base_logits.1 = (f32[256,1024]{1,0:T(8,128)S(1)}, f32[256,1024]{1,0:T(8,128)S(1)}) custom-call(s32[2]{0:T(128)S(1)} %pad_add_fusion.flags, f32[1,512]{1,0:T(1,128)S(1)} %add_convert_fusion.1.low_place, f32[1,512]{1,0:T(1,128)S(1)} %get-tuple-element.54.high_place, bf16[128,1280]{1,0:T(8,128)(2,1)S(1)} %get-tuple-element.41.a, ...), custom_call_target="tpu_custom_call" | custom-call | flops 5368709120 | bytes 9965568 | tf_op jit(solution)/shard_map/base_logits/pallas_call | solution.py:89
  68.6 3.9 %policy_logits.1 = (f32[256,1024]{1,0:T(8,128)S(1)}, f32[256,1024]{1,0:T(8,128)S(1)}) custom-call(s32[2]{0:T(128)S(1)} %pad_add_fusion.flags, bf16[128,1280]{1,0:T(8,128)(2,1)S(1)} %get-tuple-element.34.a, bf16[128,1280]{1,0:T(8,128)(2,1)S(1)} %collective-permute-done.8.a_near, bf16[256,1280]{1,0:T(8,128)(2,1)S(1)} %collective-permute-done.9.a_far, ...), custom_call_target="tpu_custom_call" | custom-call | flops 2684354560 | bytes 9961472 | tf_op jit(solution)/shard_map/policy_logits/pallas_call | solution.py:89
  72.6 2.5 %collective-permute-start.13 = (f32[256,1024]{1,0:T(8,128)S(1)}, f32[256,1024]{1,0:T(8,128)S(1)}, u32[]{:S(2)}, u32[]{:S(2)}) collective-permute-start(f32[256,1024]{1,0:T(8,128)S(1)} %get-tuple-element.39), channel_id=1, source_target_pairs={{0,32},{1,33},{2,34},{3,35},{4,36},{5,37},{6,38},{7,39},{8,40},{9,... | collective-permute-start | bytes 3145736 | tf_op jit(solution)/shard_map/ppermute | solution.py:27
  83.0 3.3 %collective-permute-start.24 = (f32[16,256]{1,0:T(8,128)S(1)}, f32[16,256]{1,0:T(8,128)S(1)}, u32[]{:S(2)}, u32[]{:S(2)}) collective-permute-start(f32[16,256]{1,0:T(8,128)S(1)} %pad_maximum_fusion.16), channel_id=1, source_target_pairs={{0,24},{1,25},{2,26},{3,27},{4,28},{5,29},{6,30},{7,31},{8,16},{9,... | collective-permute-start | bytes 49160 | tf_op jit(solution)/shard_map/ppermute | solution.py:27
  91.2 12.1 %all_to_all.5.messages = f32[16,8,256]{2,1,0:T(8,128)S(1)} all-to-all(f32[16,8,256]{2,1,0:T(8,128)S(1)} %broadcast_in_dim.33), channel_id=1, replica_groups=mesh['x'=4,'core'=2,'z'=8,'y'=4] {'x','y'}, dimensions={0} | all-to-all | bytes 262144 | tf_op jit(solution)/shard_map/all_to_all | solution.py:432
  103.9 5.0 %collective-permute-start.26 = (f32[8,256]{1,0:T(8,128)S(1)}, f32[8,256]{1,0:T(8,128)S(1)}, u32[]{:S(2)}, u32[]{:S(2)}) collective-permute-start(f32[8,256]{1,0:T(8,128)S(1)} %result.1), channel_id=1, source_target_pairs={{0,32},{1,33},{2,34},{3,35},{4,36},{5,37},{6,38},{7,39},{8,40},{9,... | collective-permute-start | bytes 24584 | tf_op jit(solution)/shard_map/ppermute | solution.py:27
  109.7 2.7 %gradient_sent.1 = (bf16[256,1280]{1,0:T(8,128)(2,1)S(1)}, bf16[256,1280]{1,0:T(8,128)(2,1)S(1)}, bf16[256,1024]{1,0:T(8,128)(2,1)S(1)}, bf16[256,1024]{1,0:T(8,128)(2,1)S(1)}) custom-call(s32[2]{0:T(128)S(1)} %pad_add_fusion.flags, f32[1,512]{1,0:T(1,128)S(1)} %add_convert_fusion.2.common, f32[8,256]{1,0:T(8,128)S(1)} %result.1, ...), custom_call_target="tpu_custom_call" | custom-call | flops 1342177280 | bytes 9717760 | tf_op jit(solution)/shard_map/gradient_sent/pallas_call | solution.py:89
  115.1 7.1 %collective-permute-done.32 = bf16[256,1280]{1,0:T(8,128)(2,1)S(1)} collective-permute-done((bf16[256,1280]{1,0:T(8,128)(2,1)S(1)}, bf16[256,1280]{1,0:T(8,128)(2,1)S(1)}, u32[]{:S(2)}, u32[]{:S(2)}) %collective-permute-start.32) | collective-permute-done | bytes 655392 | tf_op jit(solution)/shard_map/ppermute | solution.py:27
  124.5 5.2 %collective-permute-done.33 = bf16[128,1280]{1,0:T(8,128)(2,1)S(1)} collective-permute-done((bf16[128,1280]{1,0:T(8,128)(2,1)S(1)}, bf16[128,1280]{1,0:T(8,128)(2,1)S(1)}, u32[]{:S(2)}, u32[]{:S(2)}) %collective-permute-start.33) | collective-permute-done | bytes 327712 | tf_op jit(solution)/shard_map/ppermute | solution.py:27
  131.3 2.9 %collective-permute-done.34 = bf16[64,1280]{1,0:T(8,128)(2,1)S(1)} collective-permute-done((bf16[64,1280]{1,0:T(8,128)(2,1)S(1)}, bf16[64,1280]{1,0:T(8,128)(2,1)S(1)}, u32[]{:S(2)}, u32[]{:S(2)}) %collective-permute-start.34) | collective-permute-done | bytes 163872 | tf_op jit(solution)/shard_map/ppermute | solution.py:27
  144.1 3.4 %collective-permute-start.37 = (bf16[8,2560]{1,0:T(8,128)(2,1)S(1)}, bf16[8,2560]{1,0:T(8,128)(2,1)S(1)}, u32[]{:S(2)}, u32[]{:S(2)}) collective-permute-start(bf16[8,2560]{1,0:T(8,128)(2,1)S(1)} %slice.194), channel_id=1, source_target_pairs={{0,24},{1,25},{2,26},{3,27},{4,28},{5,29},{6,30},{7,31},{8,16},{9,... | collective-permute-start | bytes 122888 | tf_op jit(solution)/shard_map/ppermute | solution.py:27
  152.9 8.0 %collective-permute-start.39 = (f32[2,2560]{1,0:T(2,128)S(1)}, f32[2,2560]{1,0:T(2,128)S(1)}, u32[]{:S(2)}, u32[]{:S(2)}) collective-permute-start(f32[2,2560]{1,0:T(2,128)S(1)} %constant_dynamic-slice_fusion.3), channel_id=1, source_target_pairs={{0,32},{1,33},{2,34},{3,35},{4,36},{5,37},{6,38},{7,39},{8,40},{9,... | collective-permute-start | bytes 61448 | tf_op jit(solution)/shard_map/ppermute | solution.py:27
  (128 shorter events, 59.5 us)
Async XLA Ops:
  5.8 5.1 %collective-permute-start.1 = (bf16[4,5120]{1,0:T(4,128)(2,1)S(1)}, bf16[4,5120]{1,0:T(4,128)(2,1)S(1)}, u32[]{:S(2)}, u32[]{:S(2)}) collective-permute-start(bf16[4,5120]{1,0:T(4,128)(2,1)S(1)} %pad_maximum_fusion.12), channel_id=1, source_target_pairs={{0,8},{1,9},{2,10},{3,11},{4,12},{5,13},{6,14},{7,15},{8,0},{9,1},... | collective-permute-start | bytes 122888 | tf_op jit(solution)/shard_map/ppermute | solution.py:27
  11.0 5.5 %collective-permute-start.2 = (bf16[8,5120]{1,0:T(8,128)(2,1)S(1)}, bf16[8,5120]{1,0:T(8,128)(2,1)S(1)}, u32[]{:S(2)}, u32[]{:S(2)}) collective-permute-start(bf16[8,5120]{1,0:T(8,128)(2,1)S(1)} %pad_maximum_fusion.11), channel_id=1, source_target_pairs={{0,24},{1,25},{2,26},{3,27},{4,28},{5,29},{6,30},{7,31},{8,16},{9,... | collective-permute-start | bytes 245768 | tf_op jit(solution)/shard_map/ppermute | solution.py:27
  20.9 40.0 %collective-permute-start.12 = (bf16[2560,512]{1,0:T(8,128)(2,1)S(1)}, bf16[2560,512]{1,0:T(8,128)(2,1)S(1)}, u32[]{:S(2)}, u32[]{:S(2)}) collective-permute-start(bf16[2560,512]{1,0:T(8,128)(2,1)S(1)} %get-tuple-element.37), channel_id=1, source_target_pairs={{0,32},{1,33},{2,34},{3,35},{4,36},{5,37},{6,38},{7,39},{8,40},{9,... | collective-permute-start | bytes 7864328 | tf_op jit(solution)/shard_map/ppermute | solution.py:27
  24.5 5.4 %collective-permute-start.14 = (bf16[32,1280]{1,0:T(8,128)(2,1)S(1)}, bf16[32,1280]{1,0:T(8,128)(2,1)S(1)}, u32[]{:S(2)}, u32[]{:S(2)}) collective-permute-start(bf16[32,1280]{1,0:T(8,128)(2,1)S(1)} %get-tuple-element.61.low), channel_id=1, source_target_pairs={{0,64},{1,65},{2,66},{3,67},{4,68},{5,69},{6,70},{7,71},{8,72},{9,... | collective-permute-start | bytes 245768 | tf_op jit(solution)/shard_map/ppermute | solution.py:27
  29.7 8.1 %collective-permute-start.4 = (bf16[32,1280]{1,0:T(8,128)(2,1)S(1)}, bf16[32,1280]{1,0:T(8,128)(2,1)S(1)}, u32[]{:S(2)}, u32[]{:S(2)}) collective-permute-start(bf16[32,1280]{1,0:T(8,128)(2,1)S(1)} %get-tuple-element.63.low), channel_id=1, source_target_pairs={{0,64},{1,65},{2,66},{3,67},{4,68},{5,69},{6,70},{7,71},{8,72},{9,... | collective-permute-start | bytes 245768 | tf_op jit(solution)/shard_map/ppermute | solution.py:27
  34.5 6.9 %collective-permute-start.7 = (bf16[64,1280]{1,0:T(8,128)(2,1)S(1)}, bf16[64,1280]{1,0:T(8,128)(2,1)S(1)}, u32[]{:S(2)}, u32[]{:S(2)}) collective-permute-start(bf16[64,1280]{1,0:T(8,128)(2,1)S(1)} %pad_maximum_fusion.8), channel_id=1, source_target_pairs={{0,3},{1,2},{2,1},{3,0},{4,7},{5,6},{6,5},{7,4},{8,11},{9,10},{10,... | collective-permute-start | bytes 491528 | tf_op jit(solution)/shard_map/ppermute | solution.py:27
  36.7 12.0 %collective-permute-start.20 = (bf16[128,1280]{1,0:T(8,128)(2,1)S(1)}, bf16[128,1280]{1,0:T(8,128)(2,1)S(1)}, u32[]{:S(2)}, u32[]{:S(2)}) collective-permute-start(bf16[128,1280]{1,0:T(8,128)(2,1)S(1)} %get-tuple-element.42.b), channel_id=1, source_target_pairs={{0,64},{1,65},{2,66},{3,67},{4,68},{5,69},{6,70},{7,71},{8,72},{9,... | collective-permute-start | bytes 983048 | tf_op jit(solution)/shard_map/ppermute | solution.py:27
  38.7 10.1 %collective-permute-start.18 = (bf16[128,1280]{1,0:T(8,128)(2,1)S(1)}, bf16[128,1280]{1,0:T(8,128)(2,1)S(1)}, u32[]{:S(2)}, u32[]{:S(2)}) collective-permute-start(bf16[128,1280]{1,0:T(8,128)(2,1)S(1)} %get-tuple-element.41.a), channel_id=1, source_target_pairs={{0,1},{1,0},{2,3},{3,2},{4,5},{5,4},{6,7},{7,6},{8,9},{9,8},{10,11... | collective-permute-start | bytes 983048 | tf_op jit(solution)/shard_map/ppermute | solution.py:27
  42.6 7.9 %collective-permute-start.10 = (bf16[128,1280]{1,0:T(8,128)(2,1)S(1)}, bf16[128,1280]{1,0:T(8,128)(2,1)S(1)}, u32[]{:S(2)}, u32[]{:S(2)}) collective-permute-start(bf16[128,1280]{1,0:T(8,128)(2,1)S(1)} %get-tuple-element.35.b), channel_id=1, source_target_pairs={{0,64},{1,65},{2,66},{3,67},{4,68},{5,69},{6,70},{7,71},{8,72},{9,... | collective-permute-start | bytes 983048 | tf_op jit(solution)/shard_map/ppermute | solution.py:27
  46.0 7.4 %collective-permute-start.8 = (bf16[128,1280]{1,0:T(8,128)(2,1)S(1)}, bf16[128,1280]{1,0:T(8,128)(2,1)S(1)}, u32[]{:S(2)}, u32[]{:S(2)}) collective-permute-start(bf16[128,1280]{1,0:T(8,128)(2,1)S(1)} %get-tuple-element.34.a), channel_id=1, source_target_pairs={{0,1},{1,0},{2,3},{3,2},{4,5},{5,4},{6,7},{7,6},{8,9},{9,8},{10,11... | collective-permute-start | bytes 983048 | tf_op jit(solution)/shard_map/ppermute | solution.py:27
  48.7 12.0 %collective-permute-start.21 = (bf16[256,1280]{1,0:T(8,128)(2,1)S(1)}, bf16[256,1280]{1,0:T(8,128)(2,1)S(1)}, u32[]{:S(2)}, u32[]{:S(2)}) collective-permute-start(bf16[256,1280]{1,0:T(8,128)(2,1)S(1)} %pad_maximum_fusion.3), channel_id=1, source_target_pairs={{0,192},{1,193},{2,194},{3,195},{4,196},{5,197},{6,198},{7,199},{8... | collective-permute-start | bytes 1966088 | tf_op jit(solution)/shard_map/ppermute | solution.py:27
  48.9 12.1 %collective-permute-start.19 = (bf16[256,1280]{1,0:T(8,128)(2,1)S(1)}, bf16[256,1280]{1,0:T(8,128)(2,1)S(1)}, u32[]{:S(2)}, u32[]{:S(2)}) collective-permute-start(bf16[256,1280]{1,0:T(8,128)(2,1)S(1)} %pad_maximum_fusion.2), channel_id=1, source_target_pairs={{0,3},{1,2},{2,1},{3,0},{4,7},{5,6},{6,5},{7,4},{8,11},{9,10},{10,... | collective-permute-start | bytes 1966088 | tf_op jit(solution)/shard_map/ppermute | solution.py:27
  50.6 18.1 %collective-permute-start.11 = (bf16[256,1280]{1,0:T(8,128)(2,1)S(1)}, bf16[256,1280]{1,0:T(8,128)(2,1)S(1)}, u32[]{:S(2)}, u32[]{:S(2)}) collective-permute-start(bf16[256,1280]{1,0:T(8,128)(2,1)S(1)} %pad_maximum_fusion.1), channel_id=1, source_target_pairs={{0,192},{1,193},{2,194},{3,195},{4,196},{5,197},{6,198},{7,199},{8... | collective-permute-start | bytes 1966088 | tf_op jit(solution)/shard_map/ppermute | solution.py:27
  53.5 15.1 %collective-permute-start.9 = (bf16[256,1280]{1,0:T(8,128)(2,1)S(1)}, bf16[256,1280]{1,0:T(8,128)(2,1)S(1)}, u32[]{:S(2)}, u32[]{:S(2)}) collective-permute-start(bf16[256,1280]{1,0:T(8,128)(2,1)S(1)} %pad_maximum_fusion), channel_id=1, source_target_pairs={{0,3},{1,2},{2,1},{3,0},{4,7},{5,6},{6,5},{7,4},{8,11},{9,10},{10,... | collective-permute-start | bytes 1966088 | tf_op jit(solution)/shard_map/ppermute | solution.py:27
  67.0 8.1 %collective-permute-start.22 = (f32[256,1024]{1,0:T(8,128)S(1)}, f32[256,1024]{1,0:T(8,128)S(1)}, u32[]{:S(2)}, u32[]{:S(2)}) collective-permute-start(f32[256,1024]{1,0:T(8,128)S(1)} %get-tuple-element.44), channel_id=1, source_target_pairs={{0,32},{1,33},{2,34},{3,35},{4,36},{5,37},{6,38},{7,39},{8,40},{9,... | collective-permute-start | bytes 3145736 | tf_op jit(solution)/shard_map/ppermute | solution.py:27
  79.1 30.6 %collective-permute-start.27 = (bf16[2,256,1024]{2,1,0:T(8,128)(2,1)S(1)}, bf16[2,256,1024]{2,1,0:T(8,128)(2,1)S(1)}, u32[]{:S(2)}, u32[]{:S(2)}) collective-permute-start(bf16[2,256,1024]{2,1,0:T(8,128)(2,1)S(1)} %get-tuple-element.47), channel_id=1, source_target_pairs={{0,32},{1,33},{2,34},{3,35},{4,36},{5,37},{6,38},{7,39},{8,40},{9,... | collective-permute-start | bytes 3145736 | tf_op jit(solution)/shard_map/ppermute | solution.py:27
  103.9 5.9 %collective-permute-start.26 = (f32[8,256]{1,0:T(8,128)S(1)}, f32[8,256]{1,0:T(8,128)S(1)}, u32[]{:S(2)}, u32[]{:S(2)}) collective-permute-start(f32[8,256]{1,0:T(8,128)S(1)} %result.1), channel_id=1, source_target_pairs={{0,32},{1,33},{2,34},{3,35},{4,36},{5,37},{6,38},{7,39},{8,40},{9,... | collective-permute-start | bytes 24584 | tf_op jit(solution)/shard_map/ppermute | solution.py:27
  112.4 9.8 %collective-permute-start.32 = (bf16[256,1280]{1,0:T(8,128)(2,1)S(1)}, bf16[256,1280]{1,0:T(8,128)(2,1)S(1)}, u32[]{:S(2)}, u32[]{:S(2)}) collective-permute-start(bf16[256,1280]{1,0:T(8,128)(2,1)S(1)} %get-tuple-element.53), channel_id=1, source_target_pairs={{0,192},{1,193},{2,194},{3,195},{4,196},{5,197},{6,198},{7,199},{8... | collective-permute-start | bytes 1966088 | tf_op jit(solution)/shard_map/ppermute | solution.py:27
  112.7 10.7 %collective-permute-start.28 = (bf16[256,1280]{1,0:T(8,128)(2,1)S(1)}, bf16[256,1280]{1,0:T(8,128)(2,1)S(1)}, u32[]{:S(2)}, u32[]{:S(2)}) collective-permute-start(bf16[256,1280]{1,0:T(8,128)(2,1)S(1)} %get-tuple-element.51), channel_id=1, source_target_pairs={{0,3},{1,2},{2,1},{3,0},{4,7},{5,6},{6,5},{7,4},{8,11},{9,10},{10,... | collective-permute-start | bytes 1966088 | tf_op jit(solution)/shard_map/ppermute | solution.py:27
  122.4 7.2 %collective-permute-start.33 = (bf16[128,1280]{1,0:T(8,128)(2,1)S(1)}, bf16[128,1280]{1,0:T(8,128)(2,1)S(1)}, u32[]{:S(2)}, u32[]{:S(2)}) collective-permute-start(bf16[128,1280]{1,0:T(8,128)(2,1)S(1)} %slice.188), channel_id=1, source_target_pairs={{0,64},{1,65},{2,66},{3,67},{4,68},{5,69},{6,70},{7,71},{8,72},{9,... | collective-permute-start | bytes 983048 | tf_op jit(solution)/shard_map/ppermute | solution.py:27
  123.6 7.2 %collective-permute-start.29 = (bf16[128,1280]{1,0:T(8,128)(2,1)S(1)}, bf16[128,1280]{1,0:T(8,128)(2,1)S(1)}, u32[]{:S(2)}, u32[]{:S(2)}) collective-permute-start(bf16[128,1280]{1,0:T(8,128)(2,1)S(1)} %slice.189), channel_id=1, source_target_pairs={{0,1},{1,0},{2,3},{3,2},{4,5},{5,4},{6,7},{7,6},{8,9},{9,8},{10,11... | collective-permute-start | bytes 983048 | tf_op jit(solution)/shard_map/ppermute | solution.py:27
  135.2 5.1 %collective-permute-start.31 = (bf16[32,1280]{1,0:T(8,128)(2,1)S(1)}, bf16[32,1280]{1,0:T(8,128)(2,1)S(1)}, u32[]{:S(2)}, u32[]{:S(2)}) collective-permute-start(bf16[32,1280]{1,0:T(8,128)(2,1)S(1)} %slice.193), channel_id=1, source_target_pairs={{0,64},{1,65},{2,66},{3,67},{4,68},{5,69},{6,70},{7,71},{8,72},{9,... | collective-permute-start | bytes 245768 | tf_op jit(solution)/shard_map/ppermute | solution.py:27
  144.1 5.1 %collective-permute-start.37 = (bf16[8,2560]{1,0:T(8,128)(2,1)S(1)}, bf16[8,2560]{1,0:T(8,128)(2,1)S(1)}, u32[]{:S(2)}, u32[]{:S(2)}) collective-permute-start(bf16[8,2560]{1,0:T(8,128)(2,1)S(1)} %slice.194), channel_id=1, source_target_pairs={{0,24},{1,25},{2,26},{3,27},{4,28},{5,29},{6,30},{7,31},{8,16},{9,... | collective-permute-start | bytes 122888 | tf_op jit(solution)/shard_map/ppermute | solution.py:27
  152.9 8.8 %collective-permute-start.39 = (f32[2,2560]{1,0:T(2,128)S(1)}, f32[2,2560]{1,0:T(2,128)S(1)}, u32[]{:S(2)}, u32[]{:S(2)}) collective-permute-start(f32[2,2560]{1,0:T(2,128)S(1)} %constant_dynamic-slice_fusion.3), channel_id=1, source_target_pairs={{0,32},{1,33},{2,34},{3,35},{4,36},{5,37},{6,38},{7,39},{8,40},{9,... | collective-permute-start | bytes 61448 | tf_op jit(solution)/shard_map/ppermute | solution.py:27
  (18 other events, 83.9 us)
